TPU v7x, 32 devices: a whole 2x2x4 slice. The times are simulated.
32 devices in a mesh: ctx: 8 (over z, core), head: 4 (over y, x).
Axes of the slice: x: 2, y: 2, z: 4, core: 2. Of those that a mesh axis runs over, the one named last changes fastest.
Arguments:
- light_query: bfloat16 [4096, 32, 128], P(('ctx', 'head')), may hold values from -6 to 6
- light_keys: bfloat16 [4096, 32, 128], P(('ctx', 'head')), may hold values from -0.5390625 to 0.5390625
- light_values: bfloat16 [4096, 32, 128], P(('ctx', 'head')), may hold values from -6 to 6
- decay_rate: float32 [32], replicated, may hold values from 0.00048828125 to 0.05
- norm_gain: float32 [32, 128], replicated, may hold values from 0.5 to 1.5
- soft_query: bfloat16 [4096, 32, 128], P(('ctx', 'head')), may hold values from -120 to 120
- soft_keys: bfloat16 [4096, 4, 128], P(('ctx', 'head')), may hold values from -8 to 8
- soft_values: bfloat16 [4096, 4, 128], P(('ctx', 'head')), may hold values from -6 to 6
- segment_ids: int32 [4096], P(('ctx', 'head')), may hold values from 0 to 7, never falling along the last dimension, each value on 1 to 1024 neighbouring positions
Outputs:
- light_out: bfloat16 [4096, 32, 128], P(('ctx', 'head'))
- soft_out: bfloat16 [4096, 32, 128], P(('ctx', 'head'))
Inputs may be any that keep to these rules, and one draw needn't show every extreme that they name: `segment_ids`: document ids never fall along the tokens; each document covers 1 to 1024 consecutive tokens, and one covers exactly 1024.
All inputs are finite; a program needn't handle non-finite values.
Results may differ from a plain program's by a relative error of at most 0.004.
Values may be sent and summed in bfloat16 or wider, within the bound.
No kernel may reach another device: no remote copies, remote signals or barrier semaphores. Data moves between devices by JAX's collectives and lax.ppermute only.
A program may use at most 64 MiB of HBM per device.

v0:
```python
import jax
import jax.numpy as jnp
from jax import lax
from jax.sharding import PartitionSpec as P

LOOK = 2


HIGH = lax.Precision.HIGHEST
NEG_FILL = -1e30
NORM_EPS = 1e-06


def shifted(value, axis, by):
    count = lax.axis_size(axis)
    pairs = [(i, i + by) for i in range(count) if 0 <= i + by < count]
    return lax.ppermute(value, axis, pairs)


def local_lightning(query_group, key_group, value_group, decay, sid_group):
    group_len, per_dev, width = query_group.shape
    block = min(512, group_len)
    blocks = group_len // block
    offsets = jnp.arange(block, dtype=jnp.int32)
    distance = offsets[:, None] - offsets[None, :]
    causal = distance >= 0
    spread = jnp.maximum(distance, 0).astype(jnp.float32)
    within = jnp.exp(-decay[:, None, None] * spread[None])
    lead_decay = jnp.exp(-decay[None, :] * (offsets + 1).astype(jnp.float32)[:, None])
    tail_decay = jnp.exp(-decay[None, :] * (block - 1 - offsets).astype(jnp.float32)[:, None])
    full_decay = jnp.exp(-decay * block)

    def advance(carried, inputs):
        state_now, prev_sid = carried
        query_block, key_block, value_block, sid_block = inputs
        allowed = causal & (sid_block[:, None] == sid_block[None, :])
        scores = jnp.einsum(
            "thd,jhd->htj", query_block, key_block, preferred_element_type=jnp.float32
        )
        weights = scores * jnp.where(allowed[None], within, 0.0)
        value_wide = value_block.astype(jnp.float32)
        local_part = jnp.einsum("htj,jhd->thd", weights, value_wide, precision=HIGH)
        carry_in = (sid_block == prev_sid).astype(jnp.float32)
        inherited = jnp.einsum(
            "thd,hde->the", query_block.astype(jnp.float32), state_now, precision=HIGH
        )
        inherited = inherited * (lead_decay * carry_in[:, None])[:, :, None]
        last_sid = sid_block[-1]
        keep_rate = jnp.where(last_sid == prev_sid, full_decay, 0.0)
        open_doc = (sid_block == last_sid).astype(jnp.float32)
        weighted_keys = key_block.astype(jnp.float32) * (tail_decay * open_doc[:, None])[:, :, None]
        state_next = keep_rate[:, None, None] * state_now + jnp.einsum(
            "jhd,jhe->hde", weighted_keys, value_wide, precision=HIGH
        )
        return ((state_next, last_sid), local_part + inherited)

    initial = (jnp.zeros((per_dev, width, width), jnp.float32), jnp.float32(-1.0))
    shaped = (
        query_group.reshape(blocks, block, per_dev, width),
        key_group.reshape(blocks, block, per_dev, width),
        value_group.reshape(blocks, block, per_dev, width),
        sid_group.reshape(blocks, block),
    )
    (state_end, _), outputs = lax.scan(advance, initial, shaped)
    return (outputs.reshape(group_len, per_dev, width), state_end)


def body(
    light_query,
    light_keys,
    light_values,
    decay_rate,
    norm_gain,
    soft_query,
    soft_keys,
    soft_values,
    segment_ids,
):
    n_head = lax.axis_size("head")
    n_ctx = lax.axis_size("ctx")
    head_pos = lax.axis_index("head")
    tok_dev, heads, width = light_query.shape
    per_dev = heads // n_head
    kv_heads = soft_keys.shape[1]
    span_heads = n_head // kv_heads
    sid_plus = (segment_ids + 1).astype(jnp.bfloat16)
    sid_wide = jnp.broadcast_to(sid_plus[:, None, None], (tok_dev, n_head, 1))
    query_group, key_group, value_group, soft_group, sid_group_wide = (
        lax.all_to_all(light_query, "head", split_axis=1, concat_axis=0, tiled=True),
        lax.all_to_all(light_keys, "head", split_axis=1, concat_axis=0, tiled=True),
        lax.all_to_all(light_values, "head", split_axis=1, concat_axis=0, tiled=True),
        lax.all_to_all(soft_query, "head", split_axis=1, concat_axis=0, tiled=True),
        lax.all_to_all(sid_wide, "head", split_axis=1, concat_axis=0, tiled=True),
    )
    all_keys, all_values = (
        lax.all_gather(soft_keys, "head", axis=0, tiled=True),
        lax.all_gather(soft_values, "head", axis=0, tiled=True),
    )
    kv_index = head_pos // span_heads
    own_keys = lax.dynamic_index_in_dim(all_keys, kv_index, 1, keepdims=False)
    own_values = lax.dynamic_index_in_dim(all_values, kv_index, 1, keepdims=False)
    group_len = query_group.shape[0]
    sid_group_plus = sid_group_wide[:, 0, 0]
    sid_group = sid_group_plus.astype(jnp.float32) - 1.0
    decay = lax.dynamic_slice_in_dim(decay_rate, head_pos * per_dev, per_dev, 0)
    gain = lax.dynamic_slice_in_dim(norm_gain, head_pos * per_dev, per_dev, 0)
    local_raw, state_local = local_lightning(query_group, key_group, value_group, decay, sid_group)
    entry_sid = sid_group[0:1]
    exit_sid = sid_group[group_len - 1 : group_len]
    rate_local = jnp.where(entry_sid == exit_sid, jnp.exp(-decay * group_len), 0.0)
    start_pair = (jnp.zeros((per_dev, width, width), jnp.float32), jnp.zeros((1,), jnp.float32))

    def relay_update(carried):
        state_before, exit_before = carried
        linked = (exit_before[0] == entry_sid[0]).astype(jnp.float32)
        return state_local + (rate_local * linked)[:, None, None] * state_before

    def near_turn(turn_index, carried):
        return shifted((relay_update(carried), exit_sid), "ctx", 1)

    state_incoming, exit_incoming = lax.fori_loop(0, min(LOOK, n_ctx - 1), near_turn, start_pair)
    positions = jnp.arange(group_len, dtype=jnp.int32)
    lead_decay = jnp.exp(-decay[None, :] * (positions + 1).astype(jnp.float32)[:, None])
    continues = (sid_group == exit_incoming[0]).astype(jnp.float32)
    inherited = jnp.einsum(
        "thd,hde->the", query_group.astype(jnp.float32), state_incoming, precision=HIGH
    )
    light_raw = local_raw + inherited * (lead_decay * continues[:, None])[:, :, None]
    mean_square = jnp.mean(light_raw * light_raw, axis=-1, keepdims=True)
    light_group = (light_raw * lax.rsqrt(mean_square + NORM_EPS) * gain[None]).astype(jnp.bfloat16)
    earlier = (own_keys, own_values, sid_group_plus)
    received_keys = [own_keys]
    received_values = [own_values]
    received_sids = [sid_group_plus]
    for _ in range(LOOK):
        earlier = shifted((earlier[0], earlier[1], earlier[2]), "ctx", 1)
        received_keys.insert(0, earlier[0])
        received_values.insert(0, earlier[1])
        received_sids.insert(0, earlier[2])
    keys_span = jnp.concatenate(received_keys, 0)
    values_span = jnp.concatenate(received_values, 0)
    sid_span = jnp.concatenate(received_sids, 0).astype(jnp.float32)
    query_sid = sid_group_plus.astype(jnp.float32)
    reach = LOOK * group_len
    tile = min(512, group_len)
    scale = width ** (-0.5)

    def attend(tile_index):
        start = tile_index * tile
        query_tile = lax.dynamic_slice_in_dim(soft_group, start, tile, 0)
        tile_sid = lax.dynamic_slice_in_dim(query_sid, start, tile, 0)
        key_window = lax.dynamic_slice_in_dim(keys_span, start, reach + tile, 0)
        value_window = lax.dynamic_slice_in_dim(values_span, start, reach + tile, 0)
        sid_window = lax.dynamic_slice_in_dim(sid_span, start, reach + tile, 0)
        query_pos = start + jnp.arange(tile, dtype=jnp.int32)
        key_pos = start - reach + jnp.arange(reach + tile, dtype=jnp.int32)
        allowed = (key_pos[None, :] <= query_pos[:, None]) & (
            sid_window[None, :] == tile_sid[:, None]
        )
        scores = (
            jnp.einsum("thd,jd->htj", query_tile, key_window, preferred_element_type=jnp.float32)
            * scale
        )
        scores = jnp.where(allowed[None], scores, NEG_FILL)
        peak = jnp.max(scores, axis=-1, keepdims=True)
        probs = jnp.exp(scores - peak)
        total = jnp.sum(probs, axis=-1)
        mixed = jnp.einsum(
            "htj,jd->thd",
            probs.astype(jnp.bfloat16),
            value_window,
            preferred_element_type=jnp.float32,
        )
        return (mixed / jnp.transpose(total)[:, :, None]).astype(jnp.bfloat16)

    soft_tiles = lax.map(attend, jnp.arange(group_len // tile, dtype=jnp.int32))
    soft_group_out = soft_tiles.reshape(group_len, per_dev, width)
    light_out, soft_out = (
        lax.all_to_all(light_group, "head", split_axis=0, concat_axis=1, tiled=True),
        lax.all_to_all(soft_group_out, "head", split_axis=0, concat_axis=1, tiled=True),
    )
    return (light_out, soft_out)


def solution(mesh):
    placed = (
        P(("ctx", "head"), None, None),
        P(("ctx", "head"), None, None),
        P(("ctx", "head"), None, None),
        P(),
        P(),
        P(("ctx", "head"), None, None),
        P(("ctx", "head"), None, None),
        P(("ctx", "head"), None, None),
        P(("ctx", "head")),
    )
    return jax.shard_map(
        body,
        mesh=mesh,
        in_specs=placed,
        out_specs=(P(("ctx", "head"), None, None), P(("ctx", "head"), None, None)),
        check_vma=False,
    )
```

profile of v0, /device:TPU:8, one launch (start us, length us, event | category | flops | bytes accessed | tf_op | source)
XLA Modules:
  0.0 191.1 jit_solution(18215246338585358752)
XLA Ops:
  2.0 3.7 %all-to-all-start.2 = ((bf16[128,4,1]{0,2,1:T(2,128)(2,1)}), bf16[128,4,1]{0,2,1:T(2,128)(2,1)}, u32[]{:S(2)}, u32[]{:S(2)}) async-start(bf16[128,4,1]{0,2,1:T(2,128)(2,1)} %broadcast_in_dim.107), calls=%async_computation.2 | async-start | bytes 4096 | tf_op jit(solution)/shard_map/all_to_all | solution.py:93
  6.7 10.5 %all_gather.7 = bf16[512,4,128]{2,0,1:T(8,128)(2,1)S(1)} all-gather(bf16[128,4,128]{2,0,1:T(8,128)(2,1)S(1)} %copy.47), channel_id=1, replica_groups=mesh['ctx'=8,'head'=4] {'head'}, dimensions={0}, use_global_device_ids=true | all-gather | bytes 655360 | tf_op jit(solution)/shard_map/all_gather | solution.py:96
  19.8 11.5 %all_gather.6 = bf16[512,4,128]{2,1,0:T(4,128)(2,1)S(1)} all-gather(bf16[128,4,128]{2,1,0:T(4,128)(2,1)} %param.18), channel_id=1, replica_groups=mesh['ctx'=8,'head'=4] {'head'}, dimensions={0}, use_global_device_ids=true | all-gather | bytes 655360 | tf_op jit(solution)/shard_map/all_gather | solution.py:97
  42.6 3.5 %all-to-all-start.5 = ((bf16[128,32,128]{2,0,1:T(8,128)(2,1)}), bf16[128,32,128]{2,0,1:T(8,128)(2,1)S(1)}, u32[]{:S(2)}, u32[]{:S(2)}) async-start(bf16[128,32,128]{2,0,1:T(8,128)(2,1)} %copy.48), calls=%async_computation.5 | async-start | bytes 2097152 | tf_op jit(solution)/shard_map/all_to_all | solution.py:92
  46.8 3.6 %collective-permute-start.4 = (bf16[512]{0:T(512)(128)(2,1)S(1)}, bf16[512]{0:T(512)(128)(2,1)S(1)}, u32[]{:S(2)}, u32[]{:S(2)}) collective-permute-start(bf16[512]{0:T(512)(128)(2,1)S(1)} %get-tuple-element.163), channel_id=1, source_target_pairs={{0,4},{4,8},{8,12},{12,16},{16,20},{20,24},{24,28},{1,5},{5,9},{9,... | collective-permute-start | bytes 3080 | tf_op jit(solution)/shard_map/ppermute | solution.py:17
  57.8 2.4 %collective-permute-start.5 = (bf16[512]{0:T(512)(128)(2,1)S(1)}, bf16[512]{0:T(512)(128)(2,1)S(1)}, u32[]{:S(2)}, u32[]{:S(2)}) collective-permute-start(bf16[512]{0:T(512)(128)(2,1)S(1)} %collective-permute-done.4), channel_id=1, source_target_pairs={{0,4},{4,8},{8,12},{12,16},{16,20},{20,24},{24,28},{1,5},{5,9},{9,... | collective-permute-start | bytes 3080 | tf_op jit(solution)/shard_map/ppermute | solution.py:17
  66.0 2.3 %collective-permute-start.3 = (bf16[512,128]{0,1:T(8,128)(2,1)}, bf16[512,128]{0,1:T(8,128)(2,1)S(1)}, u32[]{:S(2)}, u32[]{:S(2)}) collective-permute-start(bf16[512,128]{0,1:T(8,128)(2,1)} %collective-permute-done.2), channel_id=1, source_target_pairs={{0,4},{4,8},{8,12},{12,16},{16,20},{20,24},{24,28},{1,5},{5,9},{9,... | collective-permute-start | bytes 393224 | tf_op jit(solution)/shard_map/ppermute | solution.py:17
  68.3 4.2 %all-to-all-start.3 = ((bf16[128,32,128]{2,0,1:T(8,128)(2,1)}), bf16[128,32,128]{2,0,1:T(8,128)(2,1)S(1)}, u32[]{:S(2)}, u32[]{:S(2)}) async-start(bf16[128,32,128]{2,0,1:T(8,128)(2,1)} %copy.38), calls=%async_computation.3 | async-start | bytes 2097152 | tf_op jit(solution)/shard_map/all_to_all | solution.py:91
  72.6 11.4 %fusion.48 = (f32[8,512]{1,0:T(8,128)S(1)}, f32[8,512,1536]{1,2,0:T(8,128)}) fusion(bf16[512,8,128]{2,0,1:T(8,128)(2,1)S(1)} %bitcast.84, bf16[512,128]{1,0:T(8,128)(2,1)} %dynamic-slice_bitcast_fusion, bf16[512,128]{1,0:T(8,128)(2,1)} %collective-permute-done.6, bf16[512,128]{1,0:T(8,128)(2,1)S(1)} %collective-permute-done.7, pred[512,1536]{0,1:T(8,128)(4,1)S(1)} %fusion.14), kind=kOutput, calls=%fused_computation.79 | convolution fusion | flops 1630662656 | bytes 27410432 | tf_op jit(solution)/shard_map/while/body/eval_jaxpr/thd,jd->htj/dot_general | solution.py:161
  86.3 3.5 %all-to-all-start.1 = ((bf16[128,32,128]{2,0,1:T(8,128)(2,1)}), bf16[128,32,128]{2,0,1:T(8,128)(2,1)S(1)}, u32[]{:S(2)}, u32[]{:S(2)}) async-start(bf16[128,32,128]{2,0,1:T(8,128)(2,1)} %copy.36), calls=%async_computation.1 | async-start | bytes 2097152 | tf_op jit(solution)/shard_map/all_to_all | solution.py:90
  89.8 10.2 %fusion = f32[8,512]{1,0:T(8,128)S(1)} fusion(f32[8,512,1536]{1,2,0:T(8,128)} %get-tuple-element.175, f32[8,512]{1,0:T(8,128)S(1)} %get-tuple-element.174), kind=kLoop, calls=%fused_computation.4 | loop fusion | flops 12578816 | bytes 25198592 | tf_op jit(solution)/shard_map/while/body/eval_jaxpr/reduce_sum | solution.py:167
  100.1 2.8 %all-to-all-done.1 = bf16[128,32,128]{2,0,1:T(8,128)(2,1)S(1)} async-done(((bf16[128,32,128]{2,0,1:T(8,128)(2,1)}), bf16[128,32,128]{2,0,1:T(8,128)(2,1)S(1)}, u32[]{:S(2)}, u32[]{:S(2)}) %all-to-all-start.1) | async-done | bytes 1048608 | tf_op jit(solution)/shard_map/all_to_all | solution.py:90
  102.9 4.4 %all-to-all-start = ((bf16[128,32,128]{2,0,1:T(8,128)(2,1)}), bf16[128,32,128]{2,0,1:T(8,128)(2,1)}, u32[]{:S(2)}, u32[]{:S(2)}) async-start(bf16[128,32,128]{2,0,1:T(8,128)(2,1)} %copy.34), calls=%async_computation | async-start | bytes 2097152 | tf_op jit(solution)/shard_map/all_to_all | solution.py:89
  107.4 12.6 %fusion.15 = bf16[512,8,128]{0,2,1:T(8,128)(2,1)S(1)} fusion(f32[8,512,1536]{1,2,0:T(8,128)} %get-tuple-element.175, f32[8,512]{1,0:T(8,128)S(1)} %get-tuple-element.174, f32[512,8]{0,1:T(8,128)S(1)} %bitcast.94, bf16[512,128]{0,1:T(8,128)(2,1)S(1)} %bitcast.93, bf16[512,128]{0,1:T(8,128)(2,1)} %collective-permute-done.2, ...), kind=kOutput, calls=%fused_computation.20 | convolution fusion | flops 1625423872 | bytes 26640384 | tf_op jit(solution)/shard_map/while/body/eval_jaxpr/htj,jd->thd/dot_general | solution.py:168
  123.5 4.3 %all-to-all-start.6 = ((bf16[512,8,128]{2,1,0:T(8,128)(2,1)}), bf16[512,8,128]{2,1,0:T(8,128)(2,1)}, u32[]{:S(2)}, u32[]{:S(2)}) async-start(bf16[512,8,128]{2,1,0:T(8,128)(2,1)} %copy.51), calls=%async_computation.6 | async-start | bytes 2097152 | tf_op jit(solution)/shard_map/all_to_all | solution.py:180
  131.4 4.5 %fusion.49 = f32[8,512,512]{2,1,0:T(8,128)} fusion(bf16[512,8,128]{2,0,1:T(8,128)(2,1)S(1)} %bitcast.80, bf16[512,8,128]{2,0,1:T(8,128)(2,1)S(1)} %bitcast.82), kind=kOutput, calls=%fused_computation.80 | convolution fusion | flops 536870912 | bytes 10485760 | tf_op jit(solution)/shard_map/while/body/eval_jaxpr/thd,jhd->htj/dot_general | solution.py:37
  136.0 2.7 %fusion.23 = f32[8,128,128]{2,1,0:T(8,128)S(1)} fusion(bf16[512,8,128]{0,2,1:T(8,128)(2,1)S(1)} %copy-done.3, bf16[512,8,128]{2,0,1:T(8,128)(2,1)S(1)} %bitcast.83, f32[512,8]{0,1:T(8,128)S(1)} %copy-done.10, f32[8]{0:T(128)S(1)} %copy-done.20), kind=kOutput, calls=%fused_computation.30 | convolution fusion | flops 806486016 | bytes 2637856 | tf_op jit(solution)/shard_map/while/body/eval_jaxpr/jhd,jhe->hde/dot_general | solution.py:52
  138.8 22.6 %while.4 = (s32[]{:T(128)}, f32[8,128,128]{2,1,0:T(8,128)S(1)}, f32[1]{0:T(128)}, f32[1]{0:T(128)}, f32[8]{0:T(128)S(1)}, /*index=5*/f32[8,128,128]{2,1,0:T(8,128)S(1)}, f32[1]{0:T(128)}, s32[]{:T(128)}) while((s32[]{:T(128)}, f32[8,128,128]{2,1,0:T(8,128)S(1)}, f32[1]{0:T(128)}, f32[1]{0:T(128)}, f32[8]{0:T(128)S(1)}, ...), condition=%wide.region_1.2_spmd, body=%wide.region_0.1_spmd.sunk | while | flops 262156 | bytes 3670263 | solution.py:121
  142.1 8.0 %collective-permute-done = f32[8,128,128]{2,1,0:T(8,128)S(1)} collective-permute-done((f32[8,128,128]{2,1,0:T(8,128)S(1)}, f32[8,128,128]{2,1,0:T(8,128)S(1)}, u32[]{:S(2)}, u32[]{:S(2)}) %collective-permute-start) | collective-permute-done | bytes 524320 | tf_op jit(solution)/shard_map/while/body/eval_jaxpr/ppermute | solution.py:17
  153.4 8.0 %collective-permute-done = f32[8,128,128]{2,1,0:T(8,128)S(1)} collective-permute-done((f32[8,128,128]{2,1,0:T(8,128)S(1)}, f32[8,128,128]{2,1,0:T(8,128)S(1)}, u32[]{:S(2)}, u32[]{:S(2)}) %collective-permute-start) | collective-permute-done | bytes 524320 | tf_op jit(solution)/shard_map/while/body/eval_jaxpr/ppermute | solution.py:17
  161.5 9.6 %fusion.5 = f32[8,512,128]{1,2,0:T(8,128)S(1)} fusion(bf16[512,8,128]{0,2,1:T(8,128)(2,1)} %squeeze.45, f32[8,512,512]{2,1,0:T(8,128)} %fusion.49, f32[512,512]{1,0:T(8,128)} %maximum_convert_fusion, f32[8]{0:T(128)S(1)} %copy-done.19, pred[512,512]{1,0:T(8,128)(4,1)S(1)} %fusion.28), kind=kOutput, calls=%fused_computation.8 | convolution fusion | flops 3227516928 | bytes 12845088 | tf_op jit(solution)/shard_map/while/body/eval_jaxpr/htj,jhd->thd/dot_general | solution.py:42
  174.4 4.1 %all-to-all-start.4 = ((bf16[512,8,128]{2,1,0:T(8,128)(2,1)}), bf16[512,8,128]{2,1,0:T(8,128)(2,1)S(1)}, u32[]{:S(2)}, u32[]{:S(2)}) async-start(bf16[512,8,128]{2,1,0:T(8,128)(2,1)} %copy.44), calls=%async_computation.4 | async-start | bytes 2097152 | tf_op jit(solution)/shard_map/all_to_all | solution.py:179
  178.6 2.4 %copy.63 = bf16[128,4,8,128]{3,2,1,0:T(8,128)(2,1)} copy(bf16[128,4,8,128]{3,2,0,1:T(8,128)(2,1)} %bitcast.34) | data formatting | bytes 2097152 | tf_op jit(solution)/shard_map/all_to_all | solution.py:180
  180.9 9.0 %all-to-all-done.4 = bf16[512,8,128]{2,1,0:T(8,128)(2,1)S(1)} async-done(((bf16[512,8,128]{2,1,0:T(8,128)(2,1)}), bf16[512,8,128]{2,1,0:T(8,128)(2,1)S(1)}, u32[]{:S(2)}, u32[]{:S(2)}) %all-to-all-start.4) | async-done | bytes 1048608 | tf_op jit(solution)/shard_map/all_to_all | solution.py:179
  (108 shorter events, 46.1 us)
Async XLA Ops:
  0.6 35.3 %copy-start = (f32[32,128]{1,0:T(8,128)S(1)}, f32[32,128]{1,0:T(8,128)}, u32[]{:S(2)}) copy-start(f32[32,128]{1,0:T(8,128)} %param.15) | copy-start | bytes 49156
  0.6 36.4 %copy-start.6 = (bf16[128,32,128]{2,1,0:T(8,128)(2,1)S(1)}, bf16[128,32,128]{2,1,0:T(8,128)(2,1)}, u32[]{:S(2)}) copy-start(bf16[128,32,128]{2,1,0:T(8,128)(2,1)} %param.16) | copy-start | bytes 3145732
  0.7 37.8 %copy-start.7 = (bf16[128,32,128]{2,1,0:T(8,128)(2,1)S(1)}, bf16[128,32,128]{2,1,0:T(8,128)(2,1)}, u32[]{:S(2)}) copy-start(bf16[128,32,128]{2,1,0:T(8,128)(2,1)} %param.13) | copy-start | bytes 3145732
  2.0 40.6 %all-to-all-start.2 = ((bf16[128,4,1]{0,2,1:T(2,128)(2,1)}), bf16[128,4,1]{0,2,1:T(2,128)(2,1)}, u32[]{:S(2)}, u32[]{:S(2)}) async-start(bf16[128,4,1]{0,2,1:T(2,128)(2,1)} %broadcast_in_dim.107), calls=%async_computation.2 | async-start | bytes 4096 | tf_op jit(solution)/shard_map/all_to_all | solution.py:93
  17.9 44.9 %collective-permute-start.6 = (bf16[512,128]{1,0:T(8,128)(2,1)}, bf16[512,128]{1,0:T(8,128)(2,1)}, u32[]{:S(2)}, u32[]{:S(2)}) collective-permute-start(bf16[512,128]{1,0:T(8,128)(2,1)} %dynamic-slice_bitcast_fusion), channel_id=1, source_target_pairs={{0,4},{4,8},{8,12},{12,16},{16,20},{20,24},{24,28},{1,5},{5,9},{9,... | collective-permute-start | bytes 393224 | tf_op jit(solution)/shard_map/ppermute | solution.py:17
  31.7 34.2 %collective-permute-start.2 = (bf16[512,128]{0,1:T(8,128)(2,1)S(1)}, bf16[512,128]{0,1:T(8,128)(2,1)}, u32[]{:S(2)}, u32[]{:S(2)}) collective-permute-start(bf16[512,128]{0,1:T(8,128)(2,1)S(1)} %bitcast.92), channel_id=1, source_target_pairs={{0,4},{4,8},{8,12},{12,16},{16,20},{20,24},{24,28},{1,5},{5,9},{9,... | collective-permute-start | bytes 393224 | tf_op jit(solution)/shard_map/ppermute | solution.py:17
  39.9 24.8 %copy-start.11 = (s32[1536]{0:T(1024)S(1)}, s32[1536]{0:T(1024)}, u32[]{:S(2)}) copy-start(s32[1536]{0:T(1024)} %iota_add_fusion) | copy-start | bytes 18436
  42.6 25.7 %all-to-all-start.5 = ((bf16[128,32,128]{2,0,1:T(8,128)(2,1)}), bf16[128,32,128]{2,0,1:T(8,128)(2,1)S(1)}, u32[]{:S(2)}, u32[]{:S(2)}) async-start(bf16[128,32,128]{2,0,1:T(8,128)(2,1)} %copy.48), calls=%async_computation.5 | async-start | bytes 2097152 | tf_op jit(solution)/shard_map/all_to_all | solution.py:92
  46.8 11.0 %collective-permute-start.4 = (bf16[512]{0:T(512)(128)(2,1)S(1)}, bf16[512]{0:T(512)(128)(2,1)S(1)}, u32[]{:S(2)}, u32[]{:S(2)}) collective-permute-start(bf16[512]{0:T(512)(128)(2,1)S(1)} %get-tuple-element.163), channel_id=1, source_target_pairs={{0,4},{4,8},{8,12},{12,16},{16,20},{20,24},{24,28},{1,5},{5,9},{9,... | collective-permute-start | bytes 3080 | tf_op jit(solution)/shard_map/ppermute | solution.py:17
  51.3 87.4 %collective-permute-start.1 = (f32[1]{0:T(128)}, f32[1]{0:T(128)}, u32[]{:S(2)}, u32[]{:S(2)}) collective-permute-start(f32[1]{0:T(128)} %get-tuple-element.169), channel_id=1, source_target_pairs={{0,4},{4,8},{8,12},{12,16},{16,20},{20,24},{24,28},{1,5},{5,9},{9,... | collective-permute-start | bytes 20 | tf_op jit(solution)/shard_map/while/body/eval_jaxpr/ppermute | solution.py:17
  57.8 4.9 %collective-permute-start.5 = (bf16[512]{0:T(512)(128)(2,1)S(1)}, bf16[512]{0:T(512)(128)(2,1)S(1)}, u32[]{:S(2)}, u32[]{:S(2)}) collective-permute-start(bf16[512]{0:T(512)(128)(2,1)S(1)} %collective-permute-done.4), channel_id=1, source_target_pairs={{0,4},{4,8},{8,12},{12,16},{16,20},{20,24},{24,28},{1,5},{5,9},{9,... | collective-permute-start | bytes 3080 | tf_op jit(solution)/shard_map/ppermute | solution.py:17
  62.7 9.9 %collective-permute-start.7 = (bf16[512,128]{1,0:T(8,128)(2,1)}, bf16[512,128]{1,0:T(8,128)(2,1)S(1)}, u32[]{:S(2)}, u32[]{:S(2)}) collective-permute-start(bf16[512,128]{1,0:T(8,128)(2,1)} %collective-permute-done.6), channel_id=1, source_target_pairs={{0,4},{4,8},{8,12},{12,16},{16,20},{20,24},{24,28},{1,5},{5,9},{9,... | collective-permute-start | bytes 393224 | tf_op jit(solution)/shard_map/ppermute | solution.py:17
  66.0 41.4 %collective-permute-start.3 = (bf16[512,128]{0,1:T(8,128)(2,1)}, bf16[512,128]{0,1:T(8,128)(2,1)S(1)}, u32[]{:S(2)}, u32[]{:S(2)}) collective-permute-start(bf16[512,128]{0,1:T(8,128)(2,1)} %collective-permute-done.2), channel_id=1, source_target_pairs={{0,4},{4,8},{8,12},{12,16},{16,20},{20,24},{24,28},{1,5},{5,9},{9,... | collective-permute-start | bytes 393224 | tf_op jit(solution)/shard_map/ppermute | solution.py:17
  68.3 18.0 %all-to-all-start.3 = ((bf16[128,32,128]{2,0,1:T(8,128)(2,1)}), bf16[128,32,128]{2,0,1:T(8,128)(2,1)S(1)}, u32[]{:S(2)}, u32[]{:S(2)}) async-start(bf16[128,32,128]{2,0,1:T(8,128)(2,1)} %copy.38), calls=%async_computation.3 | async-start | bytes 2097152 | tf_op jit(solution)/shard_map/all_to_all | solution.py:91
  86.3 16.6 %all-to-all-start.1 = ((bf16[128,32,128]{2,0,1:T(8,128)(2,1)}), bf16[128,32,128]{2,0,1:T(8,128)(2,1)S(1)}, u32[]{:S(2)}, u32[]{:S(2)}) async-start(bf16[128,32,128]{2,0,1:T(8,128)(2,1)} %copy.36), calls=%async_computation.1 | async-start | bytes 2097152 | tf_op jit(solution)/shard_map/all_to_all | solution.py:90
  102.9 20.6 %all-to-all-start = ((bf16[128,32,128]{2,0,1:T(8,128)(2,1)}), bf16[128,32,128]{2,0,1:T(8,128)(2,1)}, u32[]{:S(2)}, u32[]{:S(2)}) async-start(bf16[128,32,128]{2,0,1:T(8,128)(2,1)} %copy.34), calls=%async_computation | async-start | bytes 2097152 | tf_op jit(solution)/shard_map/all_to_all | solution.py:89
  123.5 50.9 %all-to-all-start.6 = ((bf16[512,8,128]{2,1,0:T(8,128)(2,1)}), bf16[512,8,128]{2,1,0:T(8,128)(2,1)}, u32[]{:S(2)}, u32[]{:S(2)}) async-start(bf16[512,8,128]{2,1,0:T(8,128)(2,1)} %copy.51), calls=%async_computation.6 | async-start | bytes 2097152 | tf_op jit(solution)/shard_map/all_to_all | solution.py:180
  138.8 22.6 %copy-start.13 = (bf16[512]{0:T(512)(128)(2,1)S(1)}, bf16[512]{0:T(512)(128)(2,1)}, u32[]{:S(2)}) copy-start(bf16[512]{0:T(512)(128)(2,1)} %copy-done.12) | copy-start | bytes 3076
  138.8 22.6 %copy-start.15 = (f32[512]{0:T(512)S(1)}, f32[512]{0:T(512)}, u32[]{:S(2)}) copy-start(f32[512]{0:T(512)} %add_convert_fusion) | copy-start | bytes 6148
  138.8 22.6 %copy-start.16 = (f32[512]{0:T(512)S(1)}, f32[512]{0:T(512)}, u32[]{:S(2)}) copy-start(f32[512]{0:T(512)} %get-tuple-element.170) | copy-start | bytes 6148
  138.8 22.6 %copy-start.19 = (f32[8]{0:T(128)S(1)}, f32[8]{0:T(128)}, u32[]{:S(2)}) copy-start(f32[8]{0:T(128)} %copy-done.18) | copy-start | bytes 100
  139.6 10.5 %collective-permute-start = (f32[8,128,128]{2,1,0:T(8,128)S(1)}, f32[8,128,128]{2,1,0:T(8,128)S(1)}, u32[]{:S(2)}, u32[]{:S(2)}) collective-permute-start(f32[8,128,128]{2,1,0:T(8,128)S(1)} %multiply_add_fusion.2), channel_id=1, source_target_pairs={{0,4},{4,8},{8,12},{12,16},{16,20},{20,24},{24,28},{1,5},{5,9},{9,... | collective-permute-start | bytes 1572872 | tf_op jit(solution)/shard_map/while/body/eval_jaxpr/ppermute | solution.py:17
  150.9 10.5 %collective-permute-start = (f32[8,128,128]{2,1,0:T(8,128)S(1)}, f32[8,128,128]{2,1,0:T(8,128)S(1)}, u32[]{:S(2)}, u32[]{:S(2)}) collective-permute-start(f32[8,128,128]{2,1,0:T(8,128)S(1)} %multiply_add_fusion.2), channel_id=1, source_target_pairs={{0,4},{4,8},{8,12},{12,16},{16,20},{20,24},{24,28},{1,5},{5,9},{9,... | collective-permute-start | bytes 1572872 | tf_op jit(solution)/shard_map/while/body/eval_jaxpr/ppermute | solution.py:17
  174.4 15.5 %all-to-all-start.4 = ((bf16[512,8,128]{2,1,0:T(8,128)(2,1)}), bf16[512,8,128]{2,1,0:T(8,128)(2,1)S(1)}, u32[]{:S(2)}, u32[]{:S(2)}) async-start(bf16[512,8,128]{2,1,0:T(8,128)(2,1)} %copy.44), calls=%async_computation.4 | async-start | bytes 2097152 | tf_op jit(solution)/shard_map/all_to_all | solution.py:179
  (15 other events, 127.7 us)
where the time goes:
time: 192 us; the launch traced here: 191 us
  starting transfers between devices  47.5 us (25%)
  matrix products  44.7 us (23%)
  waiting for transfers between devices  32.1 us (17%)
  blocking collectives  22 us (11%)
  other arithmetic  19.7 us (10%)
  local copies, waits for them, and re-layouts  19.3 us (10%)
  between operations  3.14 us (2%)
  loops' own time  2.47 us (1%)
    ppermute x9, starting transfers between devices, shifted(): return lax.ppermute(value, axis, pairs)  19.8 us
    ppermute x9, waiting for transfers between devices, shifted(): return lax.ppermute(value, axis, pairs)  18 us
    dot_general x1, matrix products, attend(): jnp.einsum('htj,jd->thd', probs.astype(jnp.bfloat16), value_window, prefe...  12.6 us
    all_gather x1, blocking collectives, body(): lax.all_gather(soft_values, 'head', axis=0, tiled=True)  11.5 us
    dot_general x1, matrix products, attend(): jnp.einsum('thd,jd->htj', query_tile, key_window, preferred_element_type=...  11.4 us
    all_gather x1, blocking collectives, body(): lax.all_gather(soft_keys, 'head', axis=0, tiled=True)  10.5 us
    reduce_sum x1, other arithmetic, attend(): total = jnp.sum(probs, axis=-1)  10.2 us
    dot_general x1, matrix products, advance(): local_part = jnp.einsum('htj,jhd->thd', weights, value_wide, precision=HIGH)  9.57 us
  transfers between devices with their start and end apart: 16, of which 6 were waited for; matrix products, arithmetic and copies ran while one was open for 42% of the time, Pallas kernels for 0%

commit v1 on v0

v1 whole, which is shorter than its diff:
```python
import functools
import math

import jax
import jax.numpy as jnp
from jax import lax
from jax.experimental import pallas as pl
from jax.experimental.pallas import tpu as pltpu
from jax.sharding import PartitionSpec as P

LOOK = 2
NEG_FILL = -1e30
NORM_EPS = 1e-06
TAIL = 16
F32 = jnp.float32
BF16 = jnp.bfloat16
AXES = ("ctx", "head")


def params(limit_mib):
    return pltpu.CompilerParams(vmem_limit_bytes=limit_mib * 1024 * 1024)


def vmem_specs(count):
    return [pl.BlockSpec(memory_space=pltpu.VMEM)] * count


def smem_specs(count):
    return [pl.BlockSpec(memory_space=pltpu.SMEM)] * count


def column(row):
    size = row.shape[1]
    return jnp.transpose(jnp.broadcast_to(row, (size, size)))


def dot(left, right, contract):
    return lax.dot_general(left, right, (contract, ((), ())), preferred_element_type=F32)


def split(value):
    high = value.astype(BF16)
    return high, (value - high.astype(F32)).astype(BF16)


def source_kernel(members, me_ref, rate_ref, sid_ref, key_ref, value_ref, skey_ref, svalue_ref, *rest):
    outs, pay_ref = rest[:members], rest[members]
    key_wide, value_wide, small = rest[members + 1 :]
    tokens, heads, width = key_ref.shape
    kv_heads = skey_ref.shape[1]
    per = heads // members
    me = me_ref[0]
    sid_row = (sid_ref[...] + 1).astype(F32)
    tail = jnp.broadcast_to(sid_row, (TAIL, tokens)).astype(BF16)
    open_row = (sid_row == jnp.max(sid_row, axis=1, keepdims=True)).astype(F32)
    open_column = column(open_row)
    behind = (tokens - 1 - lax.broadcasted_iota(jnp.int32, (tokens, width), 0)).astype(F32)
    for at, ref in enumerate((skey_ref, svalue_ref)):
        small[...] = ref[...].astype(F32).reshape(tokens * kv_heads, width)
        for g in range(kv_heads):
            rows = pl.ds((at * kv_heads + g) * tokens, tokens)
            pay_ref[rows, :] = small[pl.ds(g, tokens, stride=kv_heads), :].astype(BF16)
    pay_ref[pl.ds(2 * kv_heads * tokens, TAIL), :] = tail
    key_wide[...] = key_ref[...].astype(F32).reshape(tokens * heads, width)
    value_wide[...] = value_ref[...].astype(F32).reshape(tokens * heads, width)
    for k in range(members):
        for j in range(per):
            head = (me ^ k) * per + j
            keys = key_wide[pl.ds(head, tokens, stride=heads), :]
            values = value_wide[pl.ds(head, tokens, stride=heads), :].astype(BF16)
            weighted = keys * (open_column * jnp.exp(-rate_ref[head] * behind))
            high, low = split(weighted)
            state = dot(
                jnp.concatenate([high, low], 0), jnp.concatenate([values, values], 0), ((0,), (0,))
            )
            outs[k][pl.ds(j * width, width), :] = state.astype(BF16)
        outs[k][pl.ds(per * width, TAIL), :] = tail


def gather_slots(members, me, pays, slots):
    for k in range(members):
        slots[me ^ k] = pays[k][...]


def advance(slots, block, per, width, tokens, rates, state, last):
    tail = slots[block, pl.ds(per * width, TAIL), :].astype(F32)
    now = jnp.max(tail, axis=(0, 1), keepdims=True)
    same = (now == last).astype(F32)
    state = [
        slots[block, pl.ds(j * width, width), :].astype(F32)
        + (same * jnp.exp(jnp.full((1, width), -rates[j] * tokens, F32))) * state[j]
        for j in range(per)
    ]
    return state, now


def ending_kernel(members, tokens, me_ref, rate_ref, *rest):
    pays, out_ref, slots = rest[:members], rest[members], rest[members + 1]
    width = out_ref.shape[1]
    per = (out_ref.shape[0] - TAIL) // width
    me = me_ref[0]
    gather_slots(members, me, pays, slots)
    rates = [rate_ref[me * per + j] for j in range(per)]
    state = [jnp.zeros((width, width), F32)] * per
    last = jnp.zeros((1, 1), F32)
    for block in range(members):
        state, last = advance(slots, block, per, width, tokens, rates, state, last)
    for j in range(per):
        out_ref[pl.ds(j * width, width), :] = state[j].astype(BF16)
    out_ref[pl.ds(per * width, TAIL), :] = jnp.broadcast_to(last, (TAIL, width)).astype(BF16)


def prefix_kernel(members, tokens, me_ref, rate_ref, entry_ref, *rest):
    pays, outs = rest[:members], rest[members : 2 * members]
    slots, results = rest[2 * members :]
    width = entry_ref.shape[1]
    per = (entry_ref.shape[0] - TAIL) // width
    me = me_ref[0]
    gather_slots(members, me, pays, slots)
    rates = [rate_ref[me * per + j] for j in range(per)]
    state = [entry_ref[pl.ds(j * width, width), :].astype(F32) for j in range(per)]
    last = jnp.max(entry_ref[pl.ds(per * width, TAIL), :].astype(F32), axis=(0, 1), keepdims=True)
    for block in range(members):
        for j in range(per):
            results[block, pl.ds(j * width, width), :] = state[j].astype(BF16)
        results[block, pl.ds(per * width, TAIL), :] = jnp.broadcast_to(last, (TAIL, width)).astype(BF16)
        if block < members - 1:
            state, last = advance(slots, block, per, width, tokens, rates, state, last)
    for k in range(members):
        outs[k][...] = results[me ^ k]


def light_kernel(members, me_ref, rate_ref, sid_ref, gain_ref, query_ref, key_ref, value_ref, *rest):
    pays, out_ref = rest[:members], rest[members]
    query_wide, key_wide, value_wide, out_wide = rest[members + 1 :]
    tokens, heads, width = query_ref.shape
    per = heads // members
    me = me_ref[0]
    sid_row = (sid_ref[...] + 1).astype(F32)
    sid_column = column(sid_row)
    entry = jnp.max(pays[0][pl.ds(per * width, TAIL), :].astype(F32), axis=(0, 1), keepdims=True)
    continues = (sid_column == entry).astype(F32)
    row_at = lax.broadcasted_iota(jnp.int32, (tokens, tokens), 0)
    distance = row_at - lax.broadcasted_iota(jnp.int32, (tokens, tokens), 1)
    allowed = ((distance >= 0) & (sid_column == sid_row)).astype(F32)
    spread = jnp.maximum(distance, 0).astype(F32)
    ahead = (row_at + 1).astype(F32)
    query_wide[...] = query_ref[...].astype(F32).reshape(tokens * heads, width)
    key_wide[...] = key_ref[...].astype(F32).reshape(tokens * heads, width)
    value_wide[...] = value_ref[...].astype(F32).reshape(tokens * heads, width)
    for k in range(members):
        for j in range(per):
            head = (me ^ k) * per + j
            rows = pl.ds(head, tokens, stride=heads)
            query = query_wide[rows, :].astype(BF16)
            keys = key_wide[rows, :].astype(BF16)
            values = value_wide[rows, :].astype(BF16)
            rate = rate_ref[head]
            weights = dot(query, keys, ((1,), (1,))) * (allowed * jnp.exp(-rate * spread))
            high, low = split(weights)
            raw = dot(
                jnp.concatenate([high, low], 1), jnp.concatenate([values, values], 0), ((1,), (0,))
            )
            inherited = dot(query, pays[k][pl.ds(j * width, width), :], ((1,), (0,)))
            raw = raw + inherited * (continues * jnp.exp(-rate * ahead))
            mean_square = jnp.mean(raw * raw, axis=1, keepdims=True)
            gain = gain_ref[pl.ds(head, 1), :]
            out_wide[rows, :] = raw * lax.rsqrt(mean_square + NORM_EPS) * gain
    out_ref[...] = out_wide[...].reshape(tokens, heads, width).astype(BF16)


def soft_kernel(blocks, kv_heads, chunk, sid_ref, query_ref, *rest):
    pays, out_ref = rest[:blocks], rest[blocks]
    keys_all, values_all, bias = rest[blocks + 1 :]
    tokens, heads, width = query_ref.shape
    share = heads // kv_heads
    sid_row = (sid_ref[...] + 1).astype(F32)
    sid_column = column(sid_row)
    causal = lax.broadcasted_iota(jnp.int32, (tokens, tokens), 0) >= lax.broadcasted_iota(
        jnp.int32, (tokens, tokens), 1
    )
    for at in range(blocks):
        span = pl.ds(at * tokens, tokens)
        for g in range(kv_heads):
            keys_all[g, span, :] = pays[at][pl.ds(g * tokens, tokens), :]
            values_all[g, span, :] = pays[at][pl.ds((kv_heads + g) * tokens, tokens), :]
        key_sid = pays[at][pl.ds(2 * kv_heads * tokens, TAIL), :].astype(F32)[0:1, :]
        allowed = sid_column == key_sid
        if at == blocks - 1:
            allowed = allowed & causal
        fill = jnp.where(allowed, 0.0, NEG_FILL).reshape(tokens, 1, tokens)
        bias[:, span] = jnp.broadcast_to(fill, (tokens, share, tokens)).reshape(tokens * share, tokens)
    factor = width ** (-0.5) * math.log2(math.e)
    pair = 2

    def step(at, carry):
        start = pl.multiple_of(at * chunk, chunk)
        rows = pl.ds(pl.multiple_of(at * chunk * share, chunk * share), chunk * share)
        for gg in range(kv_heads // pair):
            query_wide = query_ref[pl.ds(start, chunk), pl.ds(gg * pair * share, pair * share), :].astype(F32)
            mixed = []
            for s in range(pair):
                g = gg * pair + s
                query = query_wide[:, s * share : (s + 1) * share, :].reshape(chunk * share, width).astype(BF16)
                scores = dot(query, keys_all[g], ((1,), (1,))) + bias[rows, :]
                peak = jnp.max(scores, axis=1, keepdims=True)
                probs = jnp.exp2((scores - peak) * factor)
                total = jnp.sum(probs, axis=1, keepdims=True)
                out = dot(probs.astype(BF16), values_all[g], ((1,), (0,))) / total
                mixed.append(out.reshape(chunk, share, width))
            out_ref[pl.ds(start, chunk), pl.ds(gg * pair * share, pair * share), :] = jnp.concatenate(
                mixed, 1
            ).astype(BF16)
        return carry

    lax.fori_loop(0, tokens // chunk, step, 0)


def body(
    light_query,
    light_keys,
    light_values,
    decay_rate,
    norm_gain,
    soft_query,
    soft_keys,
    soft_values,
    segment_ids,
):
    n_head = lax.axis_size("head")
    n_all = lax.axis_size("ctx") * n_head
    members = LOOK * n_head
    me = lax.rem(lax.axis_index("ctx"), LOOK) * n_head + lax.axis_index("head")
    me_arg = jnp.reshape(me, (1,)).astype(jnp.int32)
    tokens, heads, width = light_query.shape
    kv_heads = soft_keys.shape[1]
    per = heads // members
    sid_row = segment_ids.reshape(1, tokens)

    def partner(value, k):
        pairs = [(i, i - i % members + ((i % members) ^ k)) for i in range(n_all)]
        return lax.ppermute(value, AXES, pairs)

    def onward(value):
        return lax.ppermute(value, AXES, [(i, i + members) for i in range(n_all - members)])

    state_shape = jax.ShapeDtypeStruct((per * width + TAIL, width), BF16)
    pay_shape = jax.ShapeDtypeStruct((2 * kv_heads * tokens + TAIL, width), BF16)
    wide = pltpu.VMEM((tokens * heads, width), F32)
    slots = pltpu.VMEM((members,) + state_shape.shape, BF16)

    made = pl.pallas_call(
        functools.partial(source_kernel, members),
        out_shape=[state_shape] * members + [pay_shape],
        in_specs=smem_specs(2) + vmem_specs(5),
        out_specs=vmem_specs(members + 1),
        scratch_shapes=[wide, wide, pltpu.VMEM((tokens * kv_heads, width), F32)],
        compiler_params=params(32),
        name="source",
    )(me_arg, decay_rate, sid_row, light_keys, light_values, soft_keys, soft_values)
    states, own_pay = made[:members], made[members]

    prev_pay = onward(own_pay)
    states = [states[0]] + [partner(states[k], k) for k in range(1, members)]
    ending = pl.pallas_call(
        functools.partial(ending_kernel, members, tokens),
        out_shape=state_shape,
        in_specs=smem_specs(2) + vmem_specs(members),
        out_specs=vmem_specs(1)[0],
        scratch_shapes=[slots],
        compiler_params=params(32),
        name="ending",
    )(me_arg, decay_rate, *states)
    entry = onward(ending)
    window = [prev_pay]
    for k in range(1, members):
        later = (me ^ k) > me
        window.append(partner(jnp.where(later, own_pay, prev_pay), k))
    window.append(own_pay)
    entries = pl.pallas_call(
        functools.partial(prefix_kernel, members, tokens),
        out_shape=[state_shape] * members,
        in_specs=smem_specs(2) + vmem_specs(members + 1),
        out_specs=vmem_specs(members),
        scratch_shapes=[slots, slots],
        compiler_params=params(32),
        name="prefix",
    )(me_arg, decay_rate, entry, *states)
    entries = [entries[0]] + [partner(entries[k], k) for k in range(1, members)]

    blocks = members + 1
    chunk = math.gcd(tokens, 32)
    soft_out = pl.pallas_call(
        functools.partial(soft_kernel, blocks, kv_heads, chunk),
        out_shape=jax.ShapeDtypeStruct((tokens, heads, width), BF16),
        in_specs=vmem_specs(2 + blocks),
        out_specs=vmem_specs(1)[0],
        scratch_shapes=[
            pltpu.VMEM((kv_heads, blocks * tokens, width), BF16),
            pltpu.VMEM((kv_heads, blocks * tokens, width), BF16),
            pltpu.VMEM((tokens * heads // kv_heads, blocks * tokens), F32),
        ],
        compiler_params=params(60),
        cost_estimate=pl.CostEstimate(
            flops=4 * tokens * heads * blocks * tokens * width,
            bytes_accessed=4 * tokens * heads * width + blocks * 4 * kv_heads * tokens * width,
            transcendentals=tokens * heads * blocks * tokens,
        ),
        name="soft",
    )(sid_row, soft_query, *window)

    light_out = pl.pallas_call(
        functools.partial(light_kernel, members),
        out_shape=jax.ShapeDtypeStruct((tokens, heads, width), BF16),
        in_specs=smem_specs(2) + vmem_specs(5 + members),
        out_specs=vmem_specs(1)[0],
        scratch_shapes=[wide] * 4,
        compiler_params=params(48),
        name="light",
    )(me_arg, decay_rate, sid_row, norm_gain, light_query, light_keys, light_values, *entries)
    return (light_out, soft_out)


def solution(mesh):
    placed = P(("ctx", "head"), None, None)
    return jax.shard_map(
        body,
        mesh=mesh,
        in_specs=(placed, placed, placed, P(), P(), placed, placed, placed, P(("ctx", "head"))),
        out_specs=(placed, placed),
        check_vma=False,
    )
```

time: 192 us -> 93.1 us (0.48)
  the two profiles are of different devices: /device:TPU:8 before, /device:TPU:0 now
where the time goes in v1:
time: 93.1 us; the launch traced here: 92.8 us
  Pallas kernels  30.9 us (33%)
  starting transfers between devices  27.4 us (29%)
  waiting for transfers between devices  26.5 us (28%)
  local copies, waits for them, and re-layouts  6.92 us (7%)
    ppermute x21, waiting for transfers between devices, partner(): return lax.ppermute(value, AXES, pairs)  23.6 us
    ppermute x21, starting transfers between devices, partner(): return lax.ppermute(value, AXES, pairs)  20 us
    pallas_call x1, Pallas kernels, body(): pl.pallas_call(functools.partial(soft_kernel, blocks, kv_heads, chunk), o...  14.4 us
    pallas_call x1, Pallas kernels, body(): pl.pallas_call(functools.partial(light_kernel, members), out_shape=jax.Sh...  10.6 us
    ppermute x2, starting transfers between devices, onward(): lax.ppermute(value, AXES, [(i, i + members) for i in range(n_all - member...  7.42 us
    unnamed x38, local copies, waits for them, and re-layouts  6.92 us
    pallas_call x1, Pallas kernels, body(): pl.pallas_call(functools.partial(source_kernel, members), out_shape=[stat...  3.92 us
    ppermute x2, waiting for transfers between devices, onward(): lax.ppermute(value, AXES, [(i, i + members) for i in range(n_all - member...  2.9 us
  transfers between devices with their start and end apart: 23, of which 10 were waited for; matrix products, arithmetic and copies ran while one was open for 0% of the time, Pallas kernels for 14%

profile of v1, /device:TPU:0, one launch (start us, length us, event | category | flops | bytes accessed | tf_op | source)
XLA Modules:
  0.0 92.8 jit_solution(5611411625359262052)
XLA Ops:
  1.3 1.2 %copy-done = bf16[128,32,128]{2,1,0:T(8,128)(2,1)S(1)} copy-done((bf16[128,32,128]{2,1,0:T(8,128)(2,1)S(1)}, bf16[128,32,128]{2,1,0:T(8,128)(2,1)}, u32[]{:S(2)}) %copy-start) | copy-done | bytes 1048600
  2.5 1.2 %copy-done.2 = bf16[128,32,128]{2,1,0:T(8,128)(2,1)S(1)} copy-done((bf16[128,32,128]{2,1,0:T(8,128)(2,1)S(1)}, bf16[128,32,128]{2,1,0:T(8,128)(2,1)}, u32[]{:S(2)}) %copy-start.2) | copy-done | bytes 1048600
  5.6 3.9 %source.1 = (bf16[528,128]{1,0:T(8,128)(2,1)S(1)}, bf16[528,128]{1,0:T(8,128)(2,1)S(1)}, bf16[528,128]{1,0:T(8,128)(2,1)S(1)}, bf16[528,128]{1,0:T(8,128)(2,1)S(...) custom-call(s32[1]{0:T(128)} %bitcast.me_ref, ...), custom_call_target="tpu_custom_call" | custom-call | tf_op jit(solution)/shard_map/source/pallas_call | solution.py:252
  9.5 3.0 %collective-permute-start = (bf16[528,128]{1,0:T(8,128)(2,1)S(1)}, bf16[528,128]{1,0:T(8,128)(2,1)S(1)}, u32[]{:S(2)}, u32[]{:S(2)}) collective-permute-start(bf16[528,128]{1,0:T(8,128)(2,1)S(1)} %get-tuple-element.20), channel_id=1, source_target_pairs={{0,1},{1,0},{2,3},{3,2},{4,5},{5,4},{6,7},{7,6},{8,9},{9,8},{10,11... | collective-permute-start | bytes 405512 | tf_op jit(solution)/shard_map/ppermute | solution.py:242
  12.5 1.5 %collective-permute-start.1 = (bf16[528,128]{1,0:T(8,128)(2,1)S(1)}, bf16[528,128]{1,0:T(8,128)(2,1)S(1)}, u32[]{:S(2)}, u32[]{:S(2)}) collective-permute-start(bf16[528,128]{1,0:T(8,128)(2,1)S(1)} %get-tuple-element.21), channel_id=1, source_target_pairs={{0,2},{1,3},{2,0},{3,1},{4,6},{5,7},{6,4},{7,5},{8,10},{9,11},{10,... | collective-permute-start | bytes 405512 | tf_op jit(solution)/shard_map/ppermute | solution.py:242
  14.1 2.1 %collective-permute-start.4 = (bf16[528,128]{1,0:T(8,128)(2,1)S(1)}, bf16[528,128]{1,0:T(8,128)(2,1)S(1)}, u32[]{:S(2)}, u32[]{:S(2)}) collective-permute-start(bf16[528,128]{1,0:T(8,128)(2,1)S(1)} %get-tuple-element.24), channel_id=1, source_target_pairs={{0,5},{1,4},{2,7},{3,6},{4,1},{5,0},{6,3},{7,2},{8,13},{9,12},{10,... | collective-permute-start | bytes 405512 | tf_op jit(solution)/shard_map/ppermute | solution.py:242
  17.2 2.3 %collective-permute-done.1.rest_2_ = bf16[528,128]{1,0:T(8,128)(2,1)S(1)} collective-permute-done((bf16[528,128]{1,0:T(8,128)(2,1)S(1)}, bf16[528,128]{1,0:T(8,128)(2,1)S(1)}, u32[]{:S(2)}, u32[]{:S(2)}) %collective-permute-start.1) | collective-permute-done | bytes 135200 | tf_op jit(solution)/shard_map/ppermute | solution.py:242
  20.2 1.3 %collective-permute-done.2.rest_3_ = bf16[528,128]{1,0:T(8,128)(2,1)S(1)} collective-permute-done((bf16[528,128]{1,0:T(8,128)(2,1)S(1)}, bf16[528,128]{1,0:T(8,128)(2,1)S(1)}, u32[]{:S(2)}, u32[]{:S(2)}) %collective-permute-start.2) | collective-permute-done | bytes 135200 | tf_op jit(solution)/shard_map/ppermute | solution.py:242
  21.5 3.5 %collective-permute-start.15 = (bf16[1040,128]{1,0:T(8,128)(2,1)S(1)}, bf16[1040,128]{1,0:T(8,128)(2,1)S(1)}, u32[]{:S(2)}, u32[]{:S(2)}) collective-permute-start(bf16[1040,128]{1,0:T(8,128)(2,1)S(1)} %get-tuple-element.35.rest_8_), channel_id=1, source_target_pairs={{0,8},{1,9},{2,10},{3,11},{4,12},{5,13},{6,14},{7,15},{8,16},{9,17... | collective-permute-start | bytes 798728 | tf_op jit(solution)/shard_map/ppermute | solution.py:245
  25.0 1.1 %collective-permute-done.6.rest_7_ = bf16[528,128]{1,0:T(8,128)(2,1)S(1)} collective-permute-done((bf16[528,128]{1,0:T(8,128)(2,1)S(1)}, bf16[528,128]{1,0:T(8,128)(2,1)S(1)}, u32[]{:S(2)}, u32[]{:S(2)}) %collective-permute-start.6) | collective-permute-done | bytes 135200 | tf_op jit(solution)/shard_map/ppermute | solution.py:242
  27.1 3.9 %collective-permute-start.7 = (bf16[528,128]{1,0:T(8,128)(2,1)S(1)}, bf16[528,128]{1,0:T(8,128)(2,1)S(1)}, u32[]{:S(2)}, u32[]{:S(2)}) collective-permute-start(bf16[528,128]{1,0:T(8,128)(2,1)S(1)} %ending.1), channel_id=1, source_target_pairs={{0,8},{1,9},{2,10},{3,11},{4,12},{5,13},{6,14},{7,15},{8,16},{9,17... | collective-permute-start | bytes 405512 | tf_op jit(solution)/shard_map/ppermute | solution.py:245
  31.0 2.9 %collective-permute-done.7.entry_ref = bf16[528,128]{1,0:T(8,128)(2,1)S(1)} collective-permute-done((bf16[528,128]{1,0:T(8,128)(2,1)S(1)}, bf16[528,128]{1,0:T(8,128)(2,1)S(1)}, u32[]{:S(2)}, u32[]{:S(2)}) %collective-permute-start.7) | collective-permute-done | bytes 135200 | tf_op jit(solution)/shard_map/ppermute | solution.py:245
  33.9 1.0 %prefix.1 = (bf16[528,128]{1,0:T(8,128)(2,1)S(1)}, bf16[528,128]{1,0:T(8,128)(2,1)S(1)}, bf16[528,128]{1,0:T(8,128)(2,1)S(1)}, bf16[528,128]{1,0:T(8,128)(2,1)S(...) custom-call(s32[1]{0:T(128)} %bitcast.me_ref, ...), custom_call_target="tpu_custom_call" | custom-call | tf_op jit(solution)/shard_map/prefix/pallas_call | solution.py:280
  35.0 2.1 %collective-permute-start.8 = (bf16[528,128]{1,0:T(8,128)(2,1)S(1)}, bf16[528,128]{1,0:T(8,128)(2,1)S(1)}, u32[]{:S(2)}, u32[]{:S(2)}) collective-permute-start(bf16[528,128]{1,0:T(8,128)(2,1)S(1)} %get-tuple-element.28), channel_id=1, source_target_pairs={{0,1},{1,0},{2,3},{3,2},{4,5},{5,4},{6,7},{7,6},{8,9},{9,8},{10,11... | collective-permute-start | bytes 405512 | tf_op jit(solution)/shard_map/ppermute | solution.py:242
  37.1 1.5 %collective-permute-start.10 = (bf16[528,128]{1,0:T(8,128)(2,1)S(1)}, bf16[528,128]{1,0:T(8,128)(2,1)S(1)}, u32[]{:S(2)}, u32[]{:S(2)}) collective-permute-start(bf16[528,128]{1,0:T(8,128)(2,1)S(1)} %get-tuple-element.30), channel_id=1, source_target_pairs={{0,3},{1,2},{2,1},{3,0},{4,7},{5,6},{6,5},{7,4},{8,11},{9,10},{10,... | collective-permute-start | bytes 405512 | tf_op jit(solution)/shard_map/ppermute | solution.py:242
  39.3 1.5 %collective-permute-start.22 = (bf16[1040,128]{1,0:T(8,128)(2,1)S(1)}, bf16[1040,128]{1,0:T(8,128)(2,1)S(1)}, u32[]{:S(2)}, u32[]{:S(2)}) collective-permute-start(bf16[1040,128]{1,0:T(8,128)(2,1)S(1)} %get-tuple-element.36), channel_id=1, source_target_pairs={{0,7},{1,6},{2,5},{3,4},{4,3},{5,2},{6,1},{7,0},{8,15},{9,14},{10,... | collective-permute-start | bytes 798728 | tf_op jit(solution)/shard_map/ppermute | solution.py:242
  41.0 1.5 %collective-permute-start.21 = (bf16[1040,128]{1,0:T(8,128)(2,1)S(1)}, bf16[1040,128]{1,0:T(8,128)(2,1)S(1)}, u32[]{:S(2)}, u32[]{:S(2)}) collective-permute-start(bf16[1040,128]{1,0:T(8,128)(2,1)S(1)} %get-tuple-element.37), channel_id=1, source_target_pairs={{0,6},{1,7},{2,4},{3,5},{4,2},{5,3},{6,0},{7,1},{8,14},{9,15},{10,... | collective-permute-start | bytes 798728 | tf_op jit(solution)/shard_map/ppermute | solution.py:242
  42.5 8.6 %collective-permute-done.9.rest_2_ = bf16[528,128]{1,0:T(8,128)(2,1)S(1)} collective-permute-done((bf16[528,128]{1,0:T(8,128)(2,1)S(1)}, bf16[528,128]{1,0:T(8,128)(2,1)S(1)}, u32[]{:S(2)}, u32[]{:S(2)}) %collective-permute-start.9) | collective-permute-done | bytes 135200 | tf_op jit(solution)/shard_map/ppermute | solution.py:242
  51.9 3.6 %collective-permute-done.12.rest_5_ = bf16[528,128]{1,0:T(8,128)(2,1)S(1)} collective-permute-done((bf16[528,128]{1,0:T(8,128)(2,1)S(1)}, bf16[528,128]{1,0:T(8,128)(2,1)S(1)}, u32[]{:S(2)}, u32[]{:S(2)}) %collective-permute-start.12) | collective-permute-done | bytes 135200 | tf_op jit(solution)/shard_map/ppermute | solution.py:242
  55.8 5.3 %collective-permute-done.13.rest_6_ = bf16[528,128]{1,0:T(8,128)(2,1)S(1)} collective-permute-done((bf16[528,128]{1,0:T(8,128)(2,1)S(1)}, bf16[528,128]{1,0:T(8,128)(2,1)S(1)}, u32[]{:S(2)}, u32[]{:S(2)}) %collective-permute-start.13) | collective-permute-done | bytes 135200 | tf_op jit(solution)/shard_map/ppermute | solution.py:242
  62.0 1.2 %collective-permute-start.18 = (bf16[1040,128]{1,0:T(8,128)(2,1)S(1)}, bf16[1040,128]{1,0:T(8,128)(2,1)S(1)}, u32[]{:S(2)}, u32[]{:S(2)}) collective-permute-start(bf16[1040,128]{1,0:T(8,128)(2,1)S(1)} %get-tuple-element.40), channel_id=1, source_target_pairs={{0,3},{1,2},{2,1},{3,0},{4,7},{5,6},{6,5},{7,4},{8,11},{9,10},{10,... | collective-permute-start | bytes 798728 | tf_op jit(solution)/shard_map/ppermute | solution.py:242
  63.9 1.6 %collective-permute-start.16 = (bf16[1040,128]{1,0:T(8,128)(2,1)S(1)}, bf16[1040,128]{1,0:T(8,128)(2,1)S(1)}, u32[]{:S(2)}, u32[]{:S(2)}) collective-permute-start(bf16[1040,128]{1,0:T(8,128)(2,1)S(1)} %get-tuple-element.42), channel_id=1, source_target_pairs={{0,1},{1,0},{2,3},{3,2},{4,5},{5,4},{6,7},{7,6},{8,9},{9,8},{10,11... | collective-permute-start | bytes 798728 | tf_op jit(solution)/shard_map/ppermute | solution.py:242
  65.5 10.6 %light.1 = bf16[128,32,128]{2,1,0:T(8,128)(2,1)} custom-call(s32[1]{0:T(128)} %bitcast.me_ref, f32[32]{0:T(128)S(1)} %copy-done.9, s32[1,128]{1,0:T(1,128)S(1)} %bitcast.4, f32[32,128]{1,0:T(8,128)S(1)} %copy-done.8, bf16[128,32,128]{2,1,0:T(8,128)(2,1)S(1)} %copy-done.4, bf16[128,32,128]{2,1,0:T(8,128)(2,1)S(1)} %copy-done.1, ...), custom_call_target="tpu_custom_call" | custom-call | tf_op jit(solution)/shard_map/light/pallas_call | solution.py:312
  78.3 14.4 %soft.1 = bf16[128,32,128]{2,1,0:T(8,128)(2,1)} custom-call(s32[1,128]{1,0:T(1,128)} %bitcast.2, bf16[128,32,128]{2,1,0:T(8,128)(2,1)} %query_ref.3, bf16[1040,128]{1,0:T(8,128)(2,1)} %copy-done.11, bf16[1040,128]{1,0:T(8,128)(2,1)} %copy-done.18, bf16[1040,128]{1,0:T(8,128)(2,1)} %copy-done.17, bf16[1040,128]{1,0:T(8,128)(2,1)} %copy-done.16, ...), custom_call_target="tpu_custom_call" | custom-call | flops 2415919104 | bytes 4456448 | tf_op jit(solution)/shard_map/soft/pallas_call | solution.py:293
  (66 shorter events, 10.9 us)
Async XLA Ops:
  9.5 7.0 %collective-permute-start = (bf16[528,128]{1,0:T(8,128)(2,1)S(1)}, bf16[528,128]{1,0:T(8,128)(2,1)S(1)}, u32[]{:S(2)}, u32[]{:S(2)}) collective-permute-start(bf16[528,128]{1,0:T(8,128)(2,1)S(1)} %get-tuple-element.20), channel_id=1, source_target_pairs={{0,1},{1,0},{2,3},{3,2},{4,5},{5,4},{6,7},{7,6},{8,9},{9,8},{10,11... | collective-permute-start | bytes 405512 | tf_op jit(solution)/shard_map/ppermute | solution.py:242
  12.5 7.0 %collective-permute-start.1 = (bf16[528,128]{1,0:T(8,128)(2,1)S(1)}, bf16[528,128]{1,0:T(8,128)(2,1)S(1)}, u32[]{:S(2)}, u32[]{:S(2)}) collective-permute-start(bf16[528,128]{1,0:T(8,128)(2,1)S(1)} %get-tuple-element.21), channel_id=1, source_target_pairs={{0,2},{1,3},{2,0},{3,1},{4,6},{5,7},{6,4},{7,5},{8,10},{9,11},{10,... | collective-permute-start | bytes 405512 | tf_op jit(solution)/shard_map/ppermute | solution.py:242
  14.0 7.5 %collective-permute-start.2 = (bf16[528,128]{1,0:T(8,128)(2,1)S(1)}, bf16[528,128]{1,0:T(8,128)(2,1)S(1)}, u32[]{:S(2)}, u32[]{:S(2)}) collective-permute-start(bf16[528,128]{1,0:T(8,128)(2,1)S(1)} %get-tuple-element.22), channel_id=1, source_target_pairs={{0,3},{1,2},{2,1},{3,0},{4,7},{5,6},{6,5},{7,4},{8,11},{9,10},{10,... | collective-permute-start | bytes 405512 | tf_op jit(solution)/shard_map/ppermute | solution.py:242
  14.1 10.9 %collective-permute-start.3 = (bf16[528,128]{1,0:T(8,128)(2,1)S(1)}, bf16[528,128]{1,0:T(8,128)(2,1)S(1)}, u32[]{:S(2)}, u32[]{:S(2)}) collective-permute-start(bf16[528,128]{1,0:T(8,128)(2,1)S(1)} %get-tuple-element.23), channel_id=1, source_target_pairs={{0,4},{1,5},{2,6},{3,7},{4,0},{5,1},{6,2},{7,3},{8,12},{9,13},{10,... | collective-permute-start | bytes 405512 | tf_op jit(solution)/shard_map/ppermute | solution.py:242
  14.1 10.9 %collective-permute-start.4 = (bf16[528,128]{1,0:T(8,128)(2,1)S(1)}, bf16[528,128]{1,0:T(8,128)(2,1)S(1)}, u32[]{:S(2)}, u32[]{:S(2)}) collective-permute-start(bf16[528,128]{1,0:T(8,128)(2,1)S(1)} %get-tuple-element.24), channel_id=1, source_target_pairs={{0,5},{1,4},{2,7},{3,6},{4,1},{5,0},{6,3},{7,2},{8,13},{9,12},{10,... | collective-permute-start | bytes 405512 | tf_op jit(solution)/shard_map/ppermute | solution.py:242
  16.5 8.5 %collective-permute-start.5 = (bf16[528,128]{1,0:T(8,128)(2,1)S(1)}, bf16[528,128]{1,0:T(8,128)(2,1)S(1)}, u32[]{:S(2)}, u32[]{:S(2)}) collective-permute-start(bf16[528,128]{1,0:T(8,128)(2,1)S(1)} %get-tuple-element.25), channel_id=1, source_target_pairs={{0,6},{1,7},{2,4},{3,5},{4,2},{5,3},{6,0},{7,1},{8,14},{9,15},{10,... | collective-permute-start | bytes 405512 | tf_op jit(solution)/shard_map/ppermute | solution.py:242
  19.5 6.6 %collective-permute-start.6 = (bf16[528,128]{1,0:T(8,128)(2,1)S(1)}, bf16[528,128]{1,0:T(8,128)(2,1)S(1)}, u32[]{:S(2)}, u32[]{:S(2)}) collective-permute-start(bf16[528,128]{1,0:T(8,128)(2,1)S(1)} %get-tuple-element.26), channel_id=1, source_target_pairs={{0,7},{1,6},{2,5},{3,4},{4,3},{5,2},{6,1},{7,0},{8,15},{9,14},{10,... | collective-permute-start | bytes 405512 | tf_op jit(solution)/shard_map/ppermute | solution.py:242
  21.5 17.1 %collective-permute-start.15 = (bf16[1040,128]{1,0:T(8,128)(2,1)S(1)}, bf16[1040,128]{1,0:T(8,128)(2,1)S(1)}, u32[]{:S(2)}, u32[]{:S(2)}) collective-permute-start(bf16[1040,128]{1,0:T(8,128)(2,1)S(1)} %get-tuple-element.35.rest_8_), channel_id=1, source_target_pairs={{0,8},{1,9},{2,10},{3,11},{4,12},{5,13},{6,14},{7,15},{8,16},{9,17... | collective-permute-start | bytes 798728 | tf_op jit(solution)/shard_map/ppermute | solution.py:245
  27.1 6.9 %collective-permute-start.7 = (bf16[528,128]{1,0:T(8,128)(2,1)S(1)}, bf16[528,128]{1,0:T(8,128)(2,1)S(1)}, u32[]{:S(2)}, u32[]{:S(2)}) collective-permute-start(bf16[528,128]{1,0:T(8,128)(2,1)S(1)} %ending.1), channel_id=1, source_target_pairs={{0,8},{1,9},{2,10},{3,11},{4,12},{5,13},{6,14},{7,15},{8,16},{9,17... | collective-permute-start | bytes 405512 | tf_op jit(solution)/shard_map/ppermute | solution.py:245
  33.9 31.5 %copy-start.4 = (bf16[128,32,128]{2,1,0:T(8,128)(2,1)S(1)}, bf16[128,32,128]{2,1,0:T(8,128)(2,1)}, u32[]{:S(2)}) copy-start(bf16[128,32,128]{2,1,0:T(8,128)(2,1)} %query_ref.2) | copy-start | bytes 3145732
  35.0 6.0 %collective-permute-start.8 = (bf16[528,128]{1,0:T(8,128)(2,1)S(1)}, bf16[528,128]{1,0:T(8,128)(2,1)S(1)}, u32[]{:S(2)}, u32[]{:S(2)}) collective-permute-start(bf16[528,128]{1,0:T(8,128)(2,1)S(1)} %get-tuple-element.28), channel_id=1, source_target_pairs={{0,1},{1,0},{2,3},{3,2},{4,5},{5,4},{6,7},{7,6},{8,9},{9,8},{10,11... | collective-permute-start | bytes 405512 | tf_op jit(solution)/shard_map/ppermute | solution.py:242
  37.1 14.0 %collective-permute-start.9 = (bf16[528,128]{1,0:T(8,128)(2,1)S(1)}, bf16[528,128]{1,0:T(8,128)(2,1)S(1)}, u32[]{:S(2)}, u32[]{:S(2)}) collective-permute-start(bf16[528,128]{1,0:T(8,128)(2,1)S(1)} %get-tuple-element.29), channel_id=1, source_target_pairs={{0,2},{1,3},{2,0},{3,1},{4,6},{5,7},{6,4},{7,5},{8,10},{9,11},{10,... | collective-permute-start | bytes 405512 | tf_op jit(solution)/shard_map/ppermute | solution.py:242
  37.1 14.0 %collective-permute-start.10 = (bf16[528,128]{1,0:T(8,128)(2,1)S(1)}, bf16[528,128]{1,0:T(8,128)(2,1)S(1)}, u32[]{:S(2)}, u32[]{:S(2)}) collective-permute-start(bf16[528,128]{1,0:T(8,128)(2,1)S(1)} %get-tuple-element.30), channel_id=1, source_target_pairs={{0,3},{1,2},{2,1},{3,0},{4,7},{5,6},{6,5},{7,4},{8,11},{9,10},{10,... | collective-permute-start | bytes 405512 | tf_op jit(solution)/shard_map/ppermute | solution.py:242
  38.6 12.5 %collective-permute-start.11 = (bf16[528,128]{1,0:T(8,128)(2,1)S(1)}, bf16[528,128]{1,0:T(8,128)(2,1)S(1)}, u32[]{:S(2)}, u32[]{:S(2)}) collective-permute-start(bf16[528,128]{1,0:T(8,128)(2,1)S(1)} %get-tuple-element.31), channel_id=1, source_target_pairs={{0,4},{1,5},{2,6},{3,7},{4,0},{5,1},{6,2},{7,3},{8,12},{9,13},{10,... | collective-permute-start | bytes 405512 | tf_op jit(solution)/shard_map/ppermute | solution.py:242
  39.3 23.8 %collective-permute-start.22 = (bf16[1040,128]{1,0:T(8,128)(2,1)S(1)}, bf16[1040,128]{1,0:T(8,128)(2,1)S(1)}, u32[]{:S(2)}, u32[]{:S(2)}) collective-permute-start(bf16[1040,128]{1,0:T(8,128)(2,1)S(1)} %get-tuple-element.36), channel_id=1, source_target_pairs={{0,7},{1,6},{2,5},{3,4},{4,3},{5,2},{6,1},{7,0},{8,15},{9,14},{10,... | collective-permute-start | bytes 798728 | tf_op jit(solution)/shard_map/ppermute | solution.py:242
  41.0 22.9 %collective-permute-start.21 = (bf16[1040,128]{1,0:T(8,128)(2,1)S(1)}, bf16[1040,128]{1,0:T(8,128)(2,1)S(1)}, u32[]{:S(2)}, u32[]{:S(2)}) collective-permute-start(bf16[1040,128]{1,0:T(8,128)(2,1)S(1)} %get-tuple-element.37), channel_id=1, source_target_pairs={{0,6},{1,7},{2,4},{3,5},{4,2},{5,3},{6,0},{7,1},{8,14},{9,15},{10,... | collective-permute-start | bytes 798728 | tf_op jit(solution)/shard_map/ppermute | solution.py:242
  51.1 4.4 %collective-permute-start.12 = (bf16[528,128]{1,0:T(8,128)(2,1)S(1)}, bf16[528,128]{1,0:T(8,128)(2,1)S(1)}, u32[]{:S(2)}, u32[]{:S(2)}) collective-permute-start(bf16[528,128]{1,0:T(8,128)(2,1)S(1)} %get-tuple-element.32), channel_id=1, source_target_pairs={{0,5},{1,4},{2,7},{3,6},{4,1},{5,0},{6,3},{7,2},{8,13},{9,12},{10,... | collective-permute-start | bytes 405512 | tf_op jit(solution)/shard_map/ppermute | solution.py:242
  51.1 10.1 %collective-permute-start.13 = (bf16[528,128]{1,0:T(8,128)(2,1)S(1)}, bf16[528,128]{1,0:T(8,128)(2,1)S(1)}, u32[]{:S(2)}, u32[]{:S(2)}) collective-permute-start(bf16[528,128]{1,0:T(8,128)(2,1)S(1)} %get-tuple-element.33), channel_id=1, source_target_pairs={{0,6},{1,7},{2,4},{3,5},{4,2},{5,3},{6,0},{7,1},{8,14},{9,15},{10,... | collective-permute-start | bytes 405512 | tf_op jit(solution)/shard_map/ppermute | solution.py:242
  51.1 10.9 %collective-permute-start.14 = (bf16[528,128]{1,0:T(8,128)(2,1)S(1)}, bf16[528,128]{1,0:T(8,128)(2,1)S(1)}, u32[]{:S(2)}, u32[]{:S(2)}) collective-permute-start(bf16[528,128]{1,0:T(8,128)(2,1)S(1)} %get-tuple-element.34), channel_id=1, source_target_pairs={{0,7},{1,6},{2,5},{3,4},{4,3},{5,2},{6,1},{7,0},{8,15},{9,14},{10,... | collective-permute-start | bytes 405512 | tf_op jit(solution)/shard_map/ppermute | solution.py:242
  55.5 20.6 %collective-permute-start.20 = (bf16[1040,128]{1,0:T(8,128)(2,1)S(1)}, bf16[1040,128]{1,0:T(8,128)(2,1)S(1)}, u32[]{:S(2)}, u32[]{:S(2)}) collective-permute-start(bf16[1040,128]{1,0:T(8,128)(2,1)S(1)} %get-tuple-element.38), channel_id=1, source_target_pairs={{0,5},{1,4},{2,7},{3,6},{4,1},{5,0},{6,3},{7,2},{8,13},{9,12},{10,... | collective-permute-start | bytes 798728 | tf_op jit(solution)/shard_map/ppermute | solution.py:242
  61.1 14.9 %collective-permute-start.19 = (bf16[1040,128]{1,0:T(8,128)(2,1)S(1)}, bf16[1040,128]{1,0:T(8,128)(2,1)S(1)}, u32[]{:S(2)}, u32[]{:S(2)}) collective-permute-start(bf16[1040,128]{1,0:T(8,128)(2,1)S(1)} %get-tuple-element.39), channel_id=1, source_target_pairs={{0,4},{1,5},{2,6},{3,7},{4,0},{5,1},{6,2},{7,3},{8,12},{9,13},{10,... | collective-permute-start | bytes 798728 | tf_op jit(solution)/shard_map/ppermute | solution.py:242
  62.0 14.1 %collective-permute-start.18 = (bf16[1040,128]{1,0:T(8,128)(2,1)S(1)}, bf16[1040,128]{1,0:T(8,128)(2,1)S(1)}, u32[]{:S(2)}, u32[]{:S(2)}) collective-permute-start(bf16[1040,128]{1,0:T(8,128)(2,1)S(1)} %get-tuple-element.40), channel_id=1, source_target_pairs={{0,3},{1,2},{2,1},{3,0},{4,7},{5,6},{6,5},{7,4},{8,11},{9,10},{10,... | collective-permute-start | bytes 798728 | tf_op jit(solution)/shard_map/ppermute | solution.py:242
  63.2 13.7 %collective-permute-start.17 = (bf16[1040,128]{1,0:T(8,128)(2,1)S(1)}, bf16[1040,128]{1,0:T(8,128)(2,1)S(1)}, u32[]{:S(2)}, u32[]{:S(2)}) collective-permute-start(bf16[1040,128]{1,0:T(8,128)(2,1)S(1)} %get-tuple-element.41), channel_id=1, source_target_pairs={{0,2},{1,3},{2,0},{3,1},{4,6},{5,7},{6,4},{7,5},{8,10},{9,11},{10,... | collective-permute-start | bytes 798728 | tf_op jit(solution)/shard_map/ppermute | solution.py:242
  63.9 13.0 %collective-permute-start.16 = (bf16[1040,128]{1,0:T(8,128)(2,1)S(1)}, bf16[1040,128]{1,0:T(8,128)(2,1)S(1)}, u32[]{:S(2)}, u32[]{:S(2)}) collective-permute-start(bf16[1040,128]{1,0:T(8,128)(2,1)S(1)} %get-tuple-element.42), channel_id=1, source_target_pairs={{0,1},{1,0},{2,3},{3,2},{4,5},{5,4},{6,7},{7,6},{8,9},{9,8},{10,11... | collective-permute-start | bytes 798728 | tf_op jit(solution)/shard_map/ppermute | solution.py:242
  (18 other events, 144.3 us)

commit v2 on v1

v2 whole, which is shorter than its diff:
```python
import functools
import math

import jax
import jax.numpy as jnp
from jax import lax
from jax.experimental import pallas as pl
from jax.experimental.pallas import tpu as pltpu
from jax.sharding import PartitionSpec as P

LOOK = 2
NEG_FILL = -1e30
NORM_EPS = 1e-06
TAIL = 16
F32 = jnp.float32
BF16 = jnp.bfloat16
AXES = ("ctx", "head")
VMEM = pl.BlockSpec(memory_space=pltpu.VMEM)
SMEM = pl.BlockSpec(memory_space=pltpu.SMEM)
ANY = pl.BlockSpec(memory_space=pl.ANY)


def call(kernel, name, micros, limit_mib, ins, outs, out_specs, scratch=()):
    return pl.pallas_call(
        kernel,
        out_shape=outs,
        in_specs=ins,
        out_specs=out_specs,
        scratch_shapes=list(scratch),
        compiler_params=pltpu.CompilerParams(vmem_limit_bytes=int(limit_mib * 1024 * 1024)),
        cost_estimate=pl.CostEstimate(flops=int(micros * 1e9), bytes_accessed=0, transcendentals=0),
        name=name,
    )


def column(row):
    size = row.shape[1]
    return jnp.transpose(jnp.broadcast_to(row, (size, size)))


def dot(left, right, contract):
    return lax.dot_general(left, right, (contract, ((), ())), preferred_element_type=F32)


def split(value):
    high = value.astype(BF16)
    return high, (value - high.astype(F32)).astype(BF16)


def pack_kernel(at_ref, sid_ref, key_ref, value_ref, query_ref, keep_ref, give_ref, query_give, key_in, value_in, stage, sems):
    tokens, kv_heads, width = key_in.shape
    half, heads = kv_heads // LOOK, query_ref.shape[1] // LOOK
    core = at_ref[0]
    other = LOOK - 1 - core
    copies = [
        pltpu.make_async_copy(key_ref, key_in, sems.at[0]),
        pltpu.make_async_copy(value_ref, value_in, sems.at[1]),
        pltpu.make_async_copy(
            query_ref.at[:, pl.ds(pl.multiple_of(other * heads, heads), heads), :], query_give, sems.at[2]
        ),
    ]
    for copy in copies:
        copy.start()
    tail = jnp.broadcast_to((sid_ref[...] + 1).astype(F32), (TAIL, tokens)).astype(BF16)
    for at, ref in enumerate((key_in, value_in)):
        copies[at].wait()
        stage[...] = jnp.swapaxes(ref[...], 0, 1)
        for j in range(half):
            rows = pl.ds((at * half + j) * tokens, tokens)
            keep_ref[rows, :] = stage[core * half + j]
            give_ref[rows, :] = stage[other * half + j]
    keep_ref[pl.ds(2 * half * tokens, TAIL), :] = tail
    give_ref[pl.ds(2 * half * tokens, TAIL), :] = tail
    copies[2].wait()


def mix_kernel(places, at_ref, mine, theirs, mine_before, theirs_before, home_ref, *outs):
    core, place = at_ref[0], at_ref[1]
    home_ref[2 * core] = mine[...]
    home_ref[2 * (1 - core)] = theirs[...]
    home_ref[2 * core + 1] = mine_before[...]
    home_ref[2 * (1 - core) + 1] = theirs_before[...]
    for k in range(1, places):
        out = outs[k - 1]
        later = ((place ^ k) > place).astype(jnp.int32)
        out[0] = home_ref[0]
        out[1] = home_ref[3]
        out[2] = home_ref[1 + later]


def source_kernel(members, at_ref, rate_ref, sid_ref, key_ref, value_ref, *rest):
    outs, keys_by_head, values_by_head = rest[:members], rest[members], rest[members + 1]
    key_in, value_in, sems = rest[members + 2 :]
    heads, tokens, width = keys_by_head.shape
    per = heads // members
    me = at_ref[2]
    copies = [
        pltpu.make_async_copy(key_ref, key_in, sems.at[0]),
        pltpu.make_async_copy(value_ref, value_in, sems.at[1]),
    ]
    for copy in copies:
        copy.start()
    sid_row = (sid_ref[...] + 1).astype(F32)
    tail = jnp.broadcast_to(sid_row, (TAIL, tokens)).astype(BF16)
    open_row = (sid_row == jnp.max(sid_row, axis=1, keepdims=True)).astype(F32)
    behind = (tokens - 1 - lax.broadcasted_iota(jnp.int32, (1, tokens), 1)).astype(F32)
    copies[0].wait()
    keys_by_head[...] = jnp.swapaxes(key_in[...], 0, 1)
    copies[1].wait()
    values_by_head[...] = jnp.swapaxes(value_in[...], 0, 1)
    for k in range(members):
        for j in range(per):
            head = (me ^ k) * per + j
            values = values_by_head[head]
            weighted = jnp.transpose(keys_by_head[head].astype(F32)) * (open_row * jnp.exp(-rate_ref[head] * behind))
            high, low = split(weighted)
            state = dot(jnp.concatenate([high, low], 1), jnp.concatenate([values, values], 0), ((1,), (0,)))
            outs[k][pl.ds(j * width, width), :] = state.astype(BF16)
        outs[k][pl.ds(per * width, TAIL), :] = tail


def gather_slots(members, me, pays, slots):
    for k in range(members):
        slots[me ^ k] = pays[k][...]


def advance(slots, block, per, width, tokens, rates, state, last):
    tail = slots[block, pl.ds(per * width, TAIL), :].astype(F32)
    now = jnp.max(tail, axis=(0, 1), keepdims=True)
    same = (now == last).astype(F32)
    state = [
        slots[block, pl.ds(j * width, width), :].astype(F32)
        + (same * jnp.exp(jnp.full((1, width), -rates[j] * tokens, F32))) * state[j]
        for j in range(per)
    ]
    return state, now


def ending_kernel(members, tokens, at_ref, rate_ref, *rest):
    pays, out_ref, slots = rest[:members], rest[members], rest[members + 1]
    width = out_ref.shape[1]
    per = (out_ref.shape[0] - TAIL) // width
    me = at_ref[2]
    gather_slots(members, me, pays, slots)
    rates = [rate_ref[me * per + j] for j in range(per)]
    state = [jnp.zeros((width, width), F32)] * per
    last = jnp.zeros((1, 1), F32)
    for block in range(members):
        state, last = advance(slots, block, per, width, tokens, rates, state, last)
    for j in range(per):
        out_ref[pl.ds(j * width, width), :] = state[j].astype(BF16)
    out_ref[pl.ds(per * width, TAIL), :] = jnp.broadcast_to(last, (TAIL, width)).astype(BF16)


def prefix_kernel(members, tokens, at_ref, rate_ref, entry_ref, *rest):
    pays, outs = rest[:members], rest[members : 2 * members]
    slots, results = rest[2 * members :]
    width = entry_ref.shape[1]
    per = (entry_ref.shape[0] - TAIL) // width
    me = at_ref[2]
    gather_slots(members, me, pays, slots)
    rates = [rate_ref[me * per + j] for j in range(per)]
    state = [entry_ref[pl.ds(j * width, width), :].astype(F32) for j in range(per)]
    last = jnp.max(entry_ref[pl.ds(per * width, TAIL), :].astype(F32), axis=(0, 1), keepdims=True)
    for block in range(members):
        for j in range(per):
            results[block, pl.ds(j * width, width), :] = state[j].astype(BF16)
        results[block, pl.ds(per * width, TAIL), :] = jnp.broadcast_to(last, (TAIL, width)).astype(BF16)
        if block < members - 1:
            state, last = advance(slots, block, per, width, tokens, rates, state, last)
    for k in range(members):
        outs[k][...] = results[me ^ k]


def prep_kernel(rate_ref, sid_ref, query_ref, keys_by_head, left_ref):
    heads, tokens, _ = keys_by_head.shape
    sid_row = (sid_ref[...] + 1).astype(F32)
    row_at = lax.broadcasted_iota(jnp.int32, (tokens, tokens), 0)
    lane = lax.broadcasted_iota(jnp.int32, (tokens, tokens), 1)
    allowed = ((row_at >= lane) & (column(sid_row) == sid_row)).astype(F32)
    ahead = (lax.broadcasted_iota(jnp.int32, (1, tokens), 1) + 1).astype(F32)
    left_ref[:, :, tokens:] = jnp.swapaxes(query_ref[...], 0, 1)
    for head in range(heads):
        weights = dot(left_ref[head, :, tokens:], keys_by_head[head], ((1,), (1,)))
        weights = weights * allowed * jnp.exp(rate_ref[head] * ahead)
        left_ref[head, :, :tokens] = weights.astype(BF16)


def final_kernel(members, at_ref, rate_ref, sid_ref, gain_ref, left_ref, values_by_head, keep_ref, got_ref, *rest):
    pays, light_ref, soft_ref, by_head = rest[:members], rest[members], rest[members + 1], rest[members + 2]
    tokens, heads, width = light_ref.shape
    per, half = heads // members, heads // LOOK
    core, me = at_ref[0], at_ref[2]
    soft_ref[:, pl.ds(pl.multiple_of(core * half, half), half), :] = keep_ref[...]
    soft_ref[:, pl.ds(pl.multiple_of((1 - core) * half, half), half), :] = got_ref[...]
    sid_column = column((sid_ref[...] + 1).astype(F32))
    entry = jnp.max(pays[0][pl.ds(per * width, TAIL), :].astype(F32), axis=(0, 1), keepdims=True)
    continues = (sid_column == entry).astype(BF16)
    ahead = (lax.broadcasted_iota(jnp.int32, (tokens, 1), 0) + 1).astype(F32)
    for k in range(members):
        for j in range(per):
            head = (me ^ k) * per + j
            left = jnp.concatenate([left_ref[head, :, :tokens], left_ref[head, :, tokens:] * continues], 1)
            right = jnp.concatenate([values_by_head[head], pays[k][pl.ds(j * width, width), :]], 0)
            raw = dot(left, right, ((1,), (0,)))
            lead = jnp.exp(-rate_ref[head] * ahead)
            mean_square = jnp.mean(raw * raw, axis=1, keepdims=True) * (lead * lead)
            out = raw * (lead * lax.rsqrt(mean_square + NORM_EPS)) * gain_ref[pl.ds(head, 1), :]
            by_head[head] = out.astype(BF16)
    light_ref[...] = jnp.swapaxes(by_head[...], 0, 1)


def soft_kernel(places, chunk, own, at_ref, query_ref, home_ref, *rest):
    pays, out_ref = rest[: places - 1], rest[places - 1]
    marks, codes, fills = rest[places:]
    tokens, heads, width = out_ref.shape
    kv_heads = (home_ref.shape[1] - TAIL) // (2 * tokens)
    share = heads // kv_heads
    core, place = at_ref[0], at_ref[1]
    block = core if own else 1 - core
    first_head = pl.multiple_of(core * heads, heads) if own else 0
    picks = [(home_ref, 1 - block), (home_ref, 3)]
    for k in range(1, places):
        later = ((place ^ k) > place).astype(jnp.int32)
        picks.append((pays[k - 1], 2 * later * (1 - block)))
        picks.append((pays[k - 1], 1 + (1 - later) * block))
    picks.append((home_ref, 2 * block))
    blocks = len(picks)
    lane = lax.broadcasted_iota(jnp.int32, (tokens, tokens), 1)
    lane_wide = lane.astype(F32)

    def spread(value):
        value = jnp.broadcast_to(value.reshape(tokens, 1, tokens), (tokens, share, tokens))
        return value.reshape(tokens * share, tokens)

    for at, (ref, slot) in enumerate(picks):
        sids = column(ref[slot, pl.ds(2 * kv_heads * tokens, TAIL), :].astype(F32)[0:1, :])
        codes[pl.ds(at * tokens, tokens), :] = (sids == lane_wide).astype(BF16)
        if at == blocks - 1:
            marks[...] = spread(jnp.where(sids == lane_wide, 0.0, NEG_FILL)).astype(BF16)
    row_at = lax.broadcasted_iota(jnp.int32, (tokens, tokens), 0)
    fills[...] = spread(jnp.where(row_at >= lane, 0.0, NEG_FILL))
    factor = width ** (-0.5) * math.log2(math.e)
    last = (blocks - 1) * tokens
    ones = jnp.ones((blocks * tokens, width), BF16)

    def step(at, carry):
        start = at * chunk
        rows = pl.ds(start * share, chunk * share)
        query_wide = query_ref[pl.ds(start, chunk), pl.ds(first_head, heads), :].astype(F32)
        mixed = []
        for g in range(kv_heads):
            query = query_wide[:, g * share : (g + 1) * share, :].reshape(chunk * share, width).astype(BF16)
            query = jnp.concatenate([query, marks[rows, :]], 1)
            keys = jnp.concatenate([ref[slot, pl.ds(g * tokens, tokens), :] for ref, slot in picks], 0)
            scores = dot(query, jnp.concatenate([keys, codes[...]], 1), ((1,), (1,)))
            scores = jnp.concatenate([scores[:, :last], scores[:, last:] + fills[rows, :]], 1)
            peak = jnp.max(scores, axis=1, keepdims=True)
            probs = jnp.exp2((scores - peak) * factor).astype(BF16)
            values = jnp.concatenate([ref[slot, pl.ds((kv_heads + g) * tokens, tokens), :] for ref, slot in picks], 0)
            out = dot(probs, jnp.concatenate([values, ones], 1), ((1,), (0,)))
            mixed.append((out[:, :width] / out[:, width:]).reshape(chunk, share, width))
        out_ref[pl.ds(start, chunk), :, :] = jnp.concatenate(mixed, 1).astype(BF16)
        return carry

    for at in range(tokens // chunk):
        step(at, 0)


def body(
    light_query,
    light_keys,
    light_values,
    decay_rate,
    norm_gain,
    soft_query,
    soft_keys,
    soft_values,
    segment_ids,
):
    places = lax.axis_size("head")
    n_all = lax.axis_size("ctx") * places
    members = LOOK * places
    core = lax.rem(lax.axis_index("ctx"), LOOK)
    place = lax.axis_index("head")
    at = jnp.stack([core, place, core * places + place]).astype(jnp.int32)
    tokens, heads, width = light_query.shape
    kv_heads = soft_keys.shape[1]
    per, half, kv_half = heads // members, heads // LOOK, kv_heads // LOOK
    sid_row = segment_ids.reshape(1, tokens)

    def partner(value, k):
        pairs = [(i, i - i % members + ((i % members) ^ k)) for i in range(n_all)]
        return lax.ppermute(value, AXES, pairs)

    def across(value):
        return partner(value, places)

    def onward(value):
        return lax.ppermute(value, AXES, [(i, i + members) for i in range(n_all - members)])

    def shape(*dims):
        return jax.ShapeDtypeStruct(dims, BF16)

    def room(*dims, dtype=BF16):
        return pltpu.VMEM(dims, dtype)

    def semaphores(count):
        return pltpu.SemaphoreType.DMA((count,))

    pay = shape(2 * kv_half * tokens + TAIL, width)
    state = shape(per * width + TAIL, width)
    by_head = shape(heads, tokens, width)
    half_out = shape(tokens, half, width)
    slots = room(members, *state.shape)

    keep, give, query_give = call(
        pack_kernel, "pack", 2, 8, [SMEM, VMEM, ANY, ANY, ANY], [pay, pay, half_out], [VMEM, VMEM, ANY],
        [room(tokens, kv_heads, width)] * 2 + [room(kv_heads, tokens, width), semaphores(3)],
    )(at, sid_row, soft_keys, soft_values, soft_query)
    theirs = across(give)
    made = call(
        functools.partial(source_kernel, members), "source", 5, 16, [SMEM, SMEM, VMEM, ANY, ANY],
        [state] * members + [by_head] * 2, [VMEM] * (members + 2),
        [room(tokens, heads, width)] * 2 + [semaphores(2)],
    )(at, decay_rate, sid_row, light_keys, light_values)
    states, keys_by_head, values_by_head = made[:members], made[members], made[members + 1]
    states = [states[0]] + [partner(states[k], k) for k in range(1, members)]
    keep_before, theirs_before = onward(keep), onward(theirs)
    query_got = across(query_give)

    left = call(
        prep_kernel, "prep", 4, 16, [SMEM, VMEM, VMEM, VMEM], shape(heads, tokens, tokens + width), VMEM
    )(decay_rate, sid_row, light_query, keys_by_head)

    mixed = call(
        functools.partial(mix_kernel, places), "mix", 1, 8, [SMEM] + [VMEM] * 4,
        [shape(4, *pay.shape)] + [shape(3, *pay.shape)] * (places - 1), [VMEM] * places,
    )(at, keep, theirs, keep_before, theirs_before)
    home, parcels = mixed[0], mixed[1:]
    parcels = [partner(parcels[k - 1], k) for k in range(1, places)]

    ending = call(
        functools.partial(ending_kernel, members, tokens), "ending", 1, 8, [SMEM] * 2 + [VMEM] * members, state, VMEM, [slots]
    )(at, decay_rate, *states)
    entry = onward(ending)
    entries = call(
        functools.partial(prefix_kernel, members, tokens), "prefix", 1, 12, [SMEM] * 2 + [VMEM] * (members + 1),
        [state] * members, [VMEM] * members, [slots, slots],
    )(at, decay_rate, entry, *states)
    entries = [entries[0]] + [partner(entries[k], k) for k in range(1, members)]

    share = half // kv_half
    blocks = 2 * places + 1
    limit = (blocks * tokens * tokens * share * 14 + 8 * half_out.size) / 2**20 + 8

    def soft(own, query):
        return call(
            functools.partial(soft_kernel, places, tokens, own), "soft", 5, limit, [SMEM] + [VMEM] * (places + 1), half_out, VMEM,
            [room(tokens * share, tokens), room(blocks * tokens, width), room(tokens * share, tokens, dtype=F32)],
        )(at, query, home, *parcels)

    soft_got = across(soft(False, query_got))
    soft_kept = soft(True, soft_query)

    whole = shape(tokens, heads, width)
    return tuple(
        call(
            functools.partial(final_kernel, members), "final", 4, 16, [SMEM] * 2 + [VMEM] * (6 + members), [whole, whole],
            [VMEM, VMEM], [room(heads, tokens, width)],
        )(at, decay_rate, sid_row, norm_gain, left, values_by_head, soft_kept, soft_got, *entries)
    )


def solution(mesh):
    placed = P(("ctx", "head"), None, None)
    return jax.shard_map(
        body,
        mesh=mesh,
        in_specs=(placed, placed, placed, P(), P(), placed, placed, placed, P(("ctx", "head"))),
        out_specs=(placed, placed),
        check_vma=False,
    )
```

time: 93.1 us -> 68.8 us (0.74)
  waiting for transfers between devices: 26.5 us -> 12.2 us
  Pallas kernels: 30.9 us -> 21.8 us
  local copies, waits for them, and re-layouts: 6.92 us -> 3.72 us
  starting transfers between devices: 27.4 us -> 29.9 us
    ppermute x21 -> x20, waiting for transfers between devices: 23.6 us -> 9.76 us  [partner(): return lax.ppermute(value, AXES, pairs)]
    pallas_call x5 -> x9, Pallas kernels: 30.9 us -> 21.8 us  [the longest x2 10.3 us: soft(): call(functools.partial(soft_kernel, places, tokens, own), 'soft', 5, limi...]
    ppermute x2 -> x3, starting transfers between devices: 7.42 us -> 11.3 us  [onward(): lax.ppermute(value, AXES, [(i, i + members) for i in range(n_all - member...]
    unnamed x38 -> x22, local copies, waits for them, and re-layouts: 6.92 us -> 3.72 us
    ppermute x21 -> x20, starting transfers between devices: 20 us -> 18.6 us  [partner(): return lax.ppermute(value, AXES, pairs)]
    ppermute x2 -> x3, waiting for transfers between devices: 2.9 us -> 2.46 us  [onward(): lax.ppermute(value, AXES, [(i, i + members) for i in range(n_all - member...]
  transfers between devices with their start and end apart: 23 -> 23, of which waited for: 10 -> 5; matrix products, arithmetic and copies ran while one was open for 0% -> 0% of each run, Pallas kernels for 14% -> 25%
where the time goes in v2:
time: 68.8 us; the launch traced here: 68.6 us
  starting transfers between devices  29.9 us (43%)
  Pallas kernels  21.8 us (32%)
  waiting for transfers between devices  12.2 us (18%)
  local copies, waits for them, and re-layouts  3.72 us (5%)
  between operations  0.85 us (1%)
    ppermute x20, starting transfers between devices, partner(): return lax.ppermute(value, AXES, pairs)  18.6 us
    ppermute x3, starting transfers between devices, onward(): lax.ppermute(value, AXES, [(i, i + members) for i in range(n_all - member...  11.3 us
    pallas_call x2, Pallas kernels, soft(): call(functools.partial(soft_kernel, places, tokens, own), 'soft', 5, limi...  10.3 us
    ppermute x20, waiting for transfers between devices, partner(): return lax.ppermute(value, AXES, pairs)  9.76 us
    pallas_call x1, Pallas kernels, body(): call(functools.partial(final_kernel, members), 'final', 4, 16, [SMEM] * 2...  3.8 us
    unnamed x22, local copies, waits for them, and re-layouts  3.72 us
    ppermute x3, waiting for transfers between devices, onward(): lax.ppermute(value, AXES, [(i, i + members) for i in range(n_all - member...  2.46 us
    pallas_call x1, Pallas kernels, body(): call(functools.partial(source_kernel, members), 'source', 5, 16, [SMEM, S...  2.38 us
  transfers between devices with their start and end apart: 23, of which 5 were waited for; matrix products, arithmetic and copies ran while one was open for 0% of the time, Pallas kernels for 25%

profile of v2, /device:TPU:0, one launch (start us, length us, event | category | flops | bytes accessed | tf_op | source)
XLA Modules:
  0.0 68.6 jit_solution(15963260882910788104)
XLA Ops:
  0.7 1.2 %copy-done.3 = bf16[128,32,128]{2,1,0:T(8,128)(2,1)S(1)} copy-done((bf16[128,32,128]{2,1,0:T(8,128)(2,1)S(1)}, bf16[128,32,128]{2,1,0:T(8,128)(2,1)}, u32[]{:S(2)}) %copy-start.3) | copy-done | bytes 1048600
  4.4 1.2 %pack.1 = (bf16[528,128]{1,0:T(8,128)(2,1)S(1)}, bf16[528,128]{1,0:T(8,128)(2,1)S(1)}, bf16[128,16,128]{2,1,0:T(8,128)(2,1)S(1)}) custom-call(s32[3]{0:T(128)S(1)} %pad_add_fusion.at_ref, s32[1,128]{1,0:T(1,128)S(1)} %bitcast.4, bf16[128,4,128]{2,1,0:T(4,128)(2,1)S(1)} %copy-done.5, bf16[128,4,128]{2,1,0:T(4,128)(2,1)S(1)} %copy-done.6, ...), custom_call_target="tpu_custom_call" | custom-call | flops 2000000000 | tf_op jit(solution)/shard_map/pack/pallas_call | solution.py:317
  6.1 4.5 %collective-permute-start.1 = (bf16[528,128]{1,0:T(8,128)(2,1)S(1)}, bf16[528,128]{1,0:T(8,128)(2,1)S(1)}, u32[]{:S(2)}, u32[]{:S(2)}) collective-permute-start(bf16[528,128]{1,0:T(8,128)(2,1)S(1)} %get-tuple-element.29.mine), channel_id=1, source_target_pairs={{0,8},{1,9},{2,10},{3,11},{4,12},{5,13},{6,14},{7,15},{8,16},{9,17... | collective-permute-start | bytes 405512 | tf_op jit(solution)/shard_map/ppermute | solution.py:300
  10.7 2.4 %source.1 = (bf16[528,128]{1,0:T(8,128)(2,1)S(1)}, bf16[528,128]{1,0:T(8,128)(2,1)S(1)}, bf16[528,128]{1,0:T(8,128)(2,1)S(1)}, bf16[528,128]{1,0:T(8,128)(2,1)S(...) custom-call(s32[3]{0:T(128)S(1)} %pad_add_fusion.at_ref, ...), custom_call_target="tpu_custom_call" | custom-call | flops 5000000000 | tf_op jit(solution)/shard_map/source/pallas_call | solution.py:322
  13.1 1.6 %collective-permute-start.8 = (bf16[528,128]{1,0:T(8,128)(2,1)S(1)}, bf16[528,128]{1,0:T(8,128)(2,1)S(1)}, u32[]{:S(2)}, u32[]{:S(2)}) collective-permute-start(bf16[528,128]{1,0:T(8,128)(2,1)S(1)} %get-tuple-element.37), channel_id=1, source_target_pairs={{0,1},{1,0},{2,3},{3,2},{4,5},{5,4},{6,7},{7,6},{8,9},{9,8},{10,11... | collective-permute-start | bytes 405512 | tf_op jit(solution)/shard_map/ppermute | solution.py:294
  14.6 1.5 %collective-permute-start.9 = (bf16[528,128]{1,0:T(8,128)(2,1)S(1)}, bf16[528,128]{1,0:T(8,128)(2,1)S(1)}, u32[]{:S(2)}, u32[]{:S(2)}) collective-permute-start(bf16[528,128]{1,0:T(8,128)(2,1)S(1)} %get-tuple-element.38), channel_id=1, source_target_pairs={{0,2},{1,3},{2,0},{3,1},{4,6},{5,7},{6,4},{7,5},{8,10},{9,11},{10,... | collective-permute-start | bytes 405512 | tf_op jit(solution)/shard_map/ppermute | solution.py:294
  16.6 3.5 %collective-permute-start.2 = (bf16[528,128]{1,0:T(8,128)(2,1)S(1)}, bf16[528,128]{1,0:T(8,128)(2,1)S(1)}, u32[]{:S(2)}, u32[]{:S(2)}) collective-permute-start(bf16[528,128]{1,0:T(8,128)(2,1)S(1)} %collective-permute-done.theirs), channel_id=1, source_target_pairs={{0,8},{1,9},{2,10},{3,11},{4,12},{5,13},{6,14},{7,15},{8,16},{9,17... | collective-permute-start | bytes 405512 | tf_op jit(solution)/shard_map/ppermute | solution.py:300
  20.2 1.6 %collective-permute-start.12 = (bf16[528,128]{1,0:T(8,128)(2,1)S(1)}, bf16[528,128]{1,0:T(8,128)(2,1)S(1)}, u32[]{:S(2)}, u32[]{:S(2)}) collective-permute-start(bf16[528,128]{1,0:T(8,128)(2,1)S(1)} %get-tuple-element.41), channel_id=1, source_target_pairs={{0,5},{1,4},{2,7},{3,6},{4,1},{5,0},{6,3},{7,2},{8,13},{9,12},{10,... | collective-permute-start | bytes 405512 | tf_op jit(solution)/shard_map/ppermute | solution.py:294
  21.8 1.1 %collective-permute-done.9.rest_2_ = bf16[528,128]{1,0:T(8,128)(2,1)S(1)} collective-permute-done((bf16[528,128]{1,0:T(8,128)(2,1)S(1)}, bf16[528,128]{1,0:T(8,128)(2,1)S(1)}, u32[]{:S(2)}, u32[]{:S(2)}) %collective-permute-start.9) | collective-permute-done | bytes 135200 | tf_op jit(solution)/shard_map/ppermute | solution.py:294
  23.1 1.4 %collective-permute-start.6 = (bf16[128,16,128]{2,1,0:T(8,128)(2,1)S(1)}, bf16[128,16,128]{2,1,0:T(8,128)(2,1)S(1)}, u32[]{:S(2)}, u32[]{:S(2)}) collective-permute-start(bf16[128,16,128]{2,1,0:T(8,128)(2,1)S(1)} %get-tuple-element.35), channel_id=1, source_target_pairs={{0,4},{1,5},{2,6},{3,7},{4,0},{5,1},{6,2},{7,3},{8,12},{9,13},{10,... | collective-permute-start | bytes 1572872 | tf_op jit(solution)/shard_map/ppermute | solution.py:294
  25.3 1.7 %collective-permute-start.3 = (bf16[3,528,128]{2,1,0:T(8,128)(2,1)S(1)}, bf16[3,528,128]{2,1,0:T(8,128)(2,1)S(1)}, u32[]{:S(2)}, u32[]{:S(2)}) collective-permute-start(bf16[3,528,128]{2,1,0:T(8,128)(2,1)S(1)} %get-tuple-element.32), channel_id=1, source_target_pairs={{0,1},{1,0},{2,3},{3,2},{4,5},{5,4},{6,7},{7,6},{8,9},{9,8},{10,11... | collective-permute-start | bytes 1216520 | tf_op jit(solution)/shard_map/ppermute | solution.py:294
  27.0 1.5 %collective-permute-start.4 = (bf16[3,528,128]{2,1,0:T(8,128)(2,1)S(1)}, bf16[3,528,128]{2,1,0:T(8,128)(2,1)S(1)}, u32[]{:S(2)}, u32[]{:S(2)}) collective-permute-start(bf16[3,528,128]{2,1,0:T(8,128)(2,1)S(1)} %get-tuple-element.33), channel_id=1, source_target_pairs={{0,2},{1,3},{2,0},{3,1},{4,6},{5,7},{6,4},{7,5},{8,10},{9,11},{10,... | collective-permute-start | bytes 1216520 | tf_op jit(solution)/shard_map/ppermute | solution.py:294
  28.5 3.1 %collective-permute-done.13.rest_6_ = bf16[528,128]{1,0:T(8,128)(2,1)S(1)} collective-permute-done((bf16[528,128]{1,0:T(8,128)(2,1)S(1)}, bf16[528,128]{1,0:T(8,128)(2,1)S(1)}, u32[]{:S(2)}, u32[]{:S(2)}) %collective-permute-start.13) | collective-permute-done | bytes 135200 | tf_op jit(solution)/shard_map/ppermute | solution.py:294
  33.5 3.4 %collective-permute-start.15 = (bf16[528,128]{1,0:T(8,128)(2,1)S(1)}, bf16[528,128]{1,0:T(8,128)(2,1)S(1)}, u32[]{:S(2)}, u32[]{:S(2)}) collective-permute-start(bf16[528,128]{1,0:T(8,128)(2,1)S(1)} %ending.1), channel_id=1, source_target_pairs={{0,8},{1,9},{2,10},{3,11},{4,12},{5,13},{6,14},{7,15},{8,16},{9,17... | collective-permute-start | bytes 405512 | tf_op jit(solution)/shard_map/ppermute | solution.py:300
  36.9 2.5 %collective-permute-done.15.entry_ref = bf16[528,128]{1,0:T(8,128)(2,1)S(1)} collective-permute-done((bf16[528,128]{1,0:T(8,128)(2,1)S(1)}, bf16[528,128]{1,0:T(8,128)(2,1)S(1)}, u32[]{:S(2)}, u32[]{:S(2)}) %collective-permute-start.15) | collective-permute-done | bytes 135200 | tf_op jit(solution)/shard_map/ppermute | solution.py:300
  39.3 1.0 %prefix.1 = (bf16[528,128]{1,0:T(8,128)(2,1)S(1)}, bf16[528,128]{1,0:T(8,128)(2,1)S(1)}, bf16[528,128]{1,0:T(8,128)(2,1)S(1)}, bf16[528,128]{1,0:T(8,128)(2,1)S(...) custom-call(s32[3]{0:T(128)S(1)} %pad_add_fusion.at_ref, ...), custom_call_target="tpu_custom_call" | custom-call | flops 1000000000 | tf_op jit(solution)/shard_map/prefix/pallas_call | solution.py:347
  40.4 1.9 %collective-permute-start.16 = (bf16[528,128]{1,0:T(8,128)(2,1)S(1)}, bf16[528,128]{1,0:T(8,128)(2,1)S(1)}, u32[]{:S(2)}, u32[]{:S(2)}) collective-permute-start(bf16[528,128]{1,0:T(8,128)(2,1)S(1)} %get-tuple-element.45), channel_id=1, source_target_pairs={{0,1},{1,0},{2,3},{3,2},{4,5},{5,4},{6,7},{7,6},{8,9},{9,8},{10,11... | collective-permute-start | bytes 405512 | tf_op jit(solution)/shard_map/ppermute | solution.py:294
  42.3 1.3 %collective-permute-start.17 = (bf16[528,128]{1,0:T(8,128)(2,1)S(1)}, bf16[528,128]{1,0:T(8,128)(2,1)S(1)}, u32[]{:S(2)}, u32[]{:S(2)}) collective-permute-start(bf16[528,128]{1,0:T(8,128)(2,1)S(1)} %get-tuple-element.46), channel_id=1, source_target_pairs={{0,2},{1,3},{2,0},{3,1},{4,6},{5,7},{6,4},{7,5},{8,10},{9,11},{10,... | collective-permute-start | bytes 405512 | tf_op jit(solution)/shard_map/ppermute | solution.py:294
  43.9 5.2 %collective-permute-done.4.rest_1_ = bf16[3,528,128]{2,1,0:T(8,128)(2,1)S(1)} collective-permute-done((bf16[3,528,128]{2,1,0:T(8,128)(2,1)S(1)}, bf16[3,528,128]{2,1,0:T(8,128)(2,1)S(1)}, u32[]{:S(2)}, u32[]{:S(2)}) %collective-permute-start.4) | collective-permute-done | bytes 405536 | tf_op jit(solution)/shard_map/ppermute | solution.py:294
  49.2 5.2 %soft.3 = bf16[128,16,128]{2,1,0:T(8,128)(2,1)S(1)} custom-call(s32[3]{0:T(128)S(1)} %pad_add_fusion.at_ref, bf16[128,16,128]{2,1,0:T(8,128)(2,1)S(1)} %collective-permute-done.6.query_ref, bf16[4,528,128]{2,1,0:T(8,128)(2,1)S(1)} %get-tuple-element.31.home_ref, bf16[3,528,128]{2,1,0:T(8,128)(2,1)S(1)} %collective-permute-done.3.rest_0_, ...), custom_call_target="tpu_custom_call" | custom-call | flops 5000000000 | tf_op jit(solution)/shard_map/soft/pallas_call | solution.py:358
  54.5 1.4 %prep.1.left_ref = bf16[32,128,256]{2,1,0:T(8,128)(2,1)S(1)} custom-call(f32[32]{0:T(128)S(1)} %copy-done.8, s32[1,128]{1,0:T(1,128)S(1)} %bitcast.6, bf16[128,32,128]{2,1,0:T(8,128)(2,1)S(1)} %copy-done.2, bf16[32,128,128]{2,1,0:T(8,128)(2,1)S(1)} %get-tuple-element.27.keys_by_head), custom_call_target="tpu_custom_call" | custom-call | flops 4000000000 | tf_op jit(solution)/shard_map/prep/pallas_call | solution.py:332
  57.2 2.1 %collective-permute-start.22 = (bf16[528,128]{1,0:T(8,128)(2,1)S(1)}, bf16[528,128]{1,0:T(8,128)(2,1)S(1)}, u32[]{:S(2)}, u32[]{:S(2)}) collective-permute-start(bf16[528,128]{1,0:T(8,128)(2,1)S(1)} %get-tuple-element.51), channel_id=1, source_target_pairs={{0,7},{1,6},{2,5},{3,4},{4,3},{5,2},{6,1},{7,0},{8,15},{9,14},{10,... | collective-permute-start | bytes 405512 | tf_op jit(solution)/shard_map/ppermute | solution.py:294
  59.4 5.1 %soft.2.keep_ref = bf16[128,16,128]{2,1,0:T(8,128)(2,1)S(1)} custom-call(s32[3]{0:T(128)S(1)} %pad_add_fusion.at_ref, bf16[128,32,128]{2,1,0:T(8,128)(2,1)S(1)} %copy-done.4, bf16[4,528,128]{2,1,0:T(8,128)(2,1)S(1)} %get-tuple-element.31.home_ref, bf16[3,528,128]{2,1,0:T(8,128)(2,1)S(1)} %collective-permute-done.3.rest_0_, ...), custom_call_target="tpu_custom_call" | custom-call | flops 5000000000 | tf_op jit(solution)/shard_map/soft/pallas_call | solution.py:358
  64.8 3.8 %final.1 = (bf16[128,32,128]{2,1,0:T(8,128)(2,1)}, bf16[128,32,128]{2,1,0:T(8,128)(2,1)}) custom-call(s32[3]{0:T(128)S(1)} %pad_add_fusion.at_ref, f32[32]{0:T(128)S(1)} %copy-done.8, s32[1,128]{1,0:T(1,128)S(1)} %bitcast.7, f32[32,128]{1,0:T(8,128)S(1)} %copy-done.7, bf16[32,128,256]{2,1,0:T(8,128)(2,1)S(1)} %prep.1.left_ref, ...), custom_call_target="tpu_custom_call" | custom-call | flops 4000000000 | tf_op jit(solution)/shard_map/final/pallas_call | solution.py:368
  (54 shorter events, 8.3 us)
Async XLA Ops:
  5.6 11.0 %collective-permute-start = (bf16[528,128]{1,0:T(8,128)(2,1)S(1)}, bf16[528,128]{1,0:T(8,128)(2,1)S(1)}, u32[]{:S(2)}, u32[]{:S(2)}) collective-permute-start(bf16[528,128]{1,0:T(8,128)(2,1)S(1)} %get-tuple-element.30), channel_id=1, source_target_pairs={{0,4},{1,5},{2,6},{3,7},{4,0},{5,1},{6,2},{7,3},{8,12},{9,13},{10,... | collective-permute-start | bytes 405512 | tf_op jit(solution)/shard_map/ppermute | solution.py:294
  6.1 14.0 %collective-permute-start.1 = (bf16[528,128]{1,0:T(8,128)(2,1)S(1)}, bf16[528,128]{1,0:T(8,128)(2,1)S(1)}, u32[]{:S(2)}, u32[]{:S(2)}) collective-permute-start(bf16[528,128]{1,0:T(8,128)(2,1)S(1)} %get-tuple-element.29.mine), channel_id=1, source_target_pairs={{0,8},{1,9},{2,10},{3,11},{4,12},{5,13},{6,14},{7,15},{8,16},{9,17... | collective-permute-start | bytes 405512 | tf_op jit(solution)/shard_map/ppermute | solution.py:300
  13.1 7.1 %collective-permute-start.8 = (bf16[528,128]{1,0:T(8,128)(2,1)S(1)}, bf16[528,128]{1,0:T(8,128)(2,1)S(1)}, u32[]{:S(2)}, u32[]{:S(2)}) collective-permute-start(bf16[528,128]{1,0:T(8,128)(2,1)S(1)} %get-tuple-element.37), channel_id=1, source_target_pairs={{0,1},{1,0},{2,3},{3,2},{4,5},{5,4},{6,7},{7,6},{8,9},{9,8},{10,11... | collective-permute-start | bytes 405512 | tf_op jit(solution)/shard_map/ppermute | solution.py:294
  14.6 8.3 %collective-permute-start.9 = (bf16[528,128]{1,0:T(8,128)(2,1)S(1)}, bf16[528,128]{1,0:T(8,128)(2,1)S(1)}, u32[]{:S(2)}, u32[]{:S(2)}) collective-permute-start(bf16[528,128]{1,0:T(8,128)(2,1)S(1)} %get-tuple-element.38), channel_id=1, source_target_pairs={{0,2},{1,3},{2,0},{3,1},{4,6},{5,7},{6,4},{7,5},{8,10},{9,11},{10,... | collective-permute-start | bytes 405512 | tf_op jit(solution)/shard_map/ppermute | solution.py:294
  16.1 7.0 %collective-permute-start.10 = (bf16[528,128]{1,0:T(8,128)(2,1)S(1)}, bf16[528,128]{1,0:T(8,128)(2,1)S(1)}, u32[]{:S(2)}, u32[]{:S(2)}) collective-permute-start(bf16[528,128]{1,0:T(8,128)(2,1)S(1)} %get-tuple-element.39), channel_id=1, source_target_pairs={{0,3},{1,2},{2,1},{3,0},{4,7},{5,6},{6,5},{7,4},{8,11},{9,10},{10,... | collective-permute-start | bytes 405512 | tf_op jit(solution)/shard_map/ppermute | solution.py:294
  16.6 8.0 %collective-permute-start.2 = (bf16[528,128]{1,0:T(8,128)(2,1)S(1)}, bf16[528,128]{1,0:T(8,128)(2,1)S(1)}, u32[]{:S(2)}, u32[]{:S(2)}) collective-permute-start(bf16[528,128]{1,0:T(8,128)(2,1)S(1)} %collective-permute-done.theirs), channel_id=1, source_target_pairs={{0,8},{1,9},{2,10},{3,11},{4,12},{5,13},{6,14},{7,15},{8,16},{9,17... | collective-permute-start | bytes 405512 | tf_op jit(solution)/shard_map/ppermute | solution.py:300
  20.1 5.2 %collective-permute-start.11 = (bf16[528,128]{1,0:T(8,128)(2,1)S(1)}, bf16[528,128]{1,0:T(8,128)(2,1)S(1)}, u32[]{:S(2)}, u32[]{:S(2)}) collective-permute-start(bf16[528,128]{1,0:T(8,128)(2,1)S(1)} %get-tuple-element.40), channel_id=1, source_target_pairs={{0,4},{1,5},{2,6},{3,7},{4,0},{5,1},{6,2},{7,3},{8,12},{9,13},{10,... | collective-permute-start | bytes 405512 | tf_op jit(solution)/shard_map/ppermute | solution.py:294
  20.2 6.8 %collective-permute-start.12 = (bf16[528,128]{1,0:T(8,128)(2,1)S(1)}, bf16[528,128]{1,0:T(8,128)(2,1)S(1)}, u32[]{:S(2)}, u32[]{:S(2)}) collective-permute-start(bf16[528,128]{1,0:T(8,128)(2,1)S(1)} %get-tuple-element.41), channel_id=1, source_target_pairs={{0,5},{1,4},{2,7},{3,6},{4,1},{5,0},{6,3},{7,2},{8,13},{9,12},{10,... | collective-permute-start | bytes 405512 | tf_op jit(solution)/shard_map/ppermute | solution.py:294
  22.9 8.7 %collective-permute-start.13 = (bf16[528,128]{1,0:T(8,128)(2,1)S(1)}, bf16[528,128]{1,0:T(8,128)(2,1)S(1)}, u32[]{:S(2)}, u32[]{:S(2)}) collective-permute-start(bf16[528,128]{1,0:T(8,128)(2,1)S(1)} %get-tuple-element.42), channel_id=1, source_target_pairs={{0,6},{1,7},{2,4},{3,5},{4,2},{5,3},{6,0},{7,1},{8,14},{9,15},{10,... | collective-permute-start | bytes 405512 | tf_op jit(solution)/shard_map/ppermute | solution.py:294
  23.1 19.2 %collective-permute-start.6 = (bf16[128,16,128]{2,1,0:T(8,128)(2,1)S(1)}, bf16[128,16,128]{2,1,0:T(8,128)(2,1)S(1)}, u32[]{:S(2)}, u32[]{:S(2)}) collective-permute-start(bf16[128,16,128]{2,1,0:T(8,128)(2,1)S(1)} %get-tuple-element.35), channel_id=1, source_target_pairs={{0,4},{1,5},{2,6},{3,7},{4,0},{5,1},{6,2},{7,3},{8,12},{9,13},{10,... | collective-permute-start | bytes 1572872 | tf_op jit(solution)/shard_map/ppermute | solution.py:294
  24.6 8.0 %collective-permute-start.14 = (bf16[528,128]{1,0:T(8,128)(2,1)S(1)}, bf16[528,128]{1,0:T(8,128)(2,1)S(1)}, u32[]{:S(2)}, u32[]{:S(2)}) collective-permute-start(bf16[528,128]{1,0:T(8,128)(2,1)S(1)} %get-tuple-element.43), channel_id=1, source_target_pairs={{0,7},{1,6},{2,5},{3,4},{4,3},{5,2},{6,1},{7,0},{8,15},{9,14},{10,... | collective-permute-start | bytes 405512 | tf_op jit(solution)/shard_map/ppermute | solution.py:294
  25.3 18.4 %collective-permute-start.3 = (bf16[3,528,128]{2,1,0:T(8,128)(2,1)S(1)}, bf16[3,528,128]{2,1,0:T(8,128)(2,1)S(1)}, u32[]{:S(2)}, u32[]{:S(2)}) collective-permute-start(bf16[3,528,128]{2,1,0:T(8,128)(2,1)S(1)} %get-tuple-element.32), channel_id=1, source_target_pairs={{0,1},{1,0},{2,3},{3,2},{4,5},{5,4},{6,7},{7,6},{8,9},{9,8},{10,11... | collective-permute-start | bytes 1216520 | tf_op jit(solution)/shard_map/ppermute | solution.py:294
  27.0 22.2 %collective-permute-start.4 = (bf16[3,528,128]{2,1,0:T(8,128)(2,1)S(1)}, bf16[3,528,128]{2,1,0:T(8,128)(2,1)S(1)}, u32[]{:S(2)}, u32[]{:S(2)}) collective-permute-start(bf16[3,528,128]{2,1,0:T(8,128)(2,1)S(1)} %get-tuple-element.33), channel_id=1, source_target_pairs={{0,2},{1,3},{2,0},{3,1},{4,6},{5,7},{6,4},{7,5},{8,10},{9,11},{10,... | collective-permute-start | bytes 1216520 | tf_op jit(solution)/shard_map/ppermute | solution.py:294
  31.6 17.5 %collective-permute-start.5 = (bf16[3,528,128]{2,1,0:T(8,128)(2,1)S(1)}, bf16[3,528,128]{2,1,0:T(8,128)(2,1)S(1)}, u32[]{:S(2)}, u32[]{:S(2)}) collective-permute-start(bf16[3,528,128]{2,1,0:T(8,128)(2,1)S(1)} %get-tuple-element.34), channel_id=1, source_target_pairs={{0,3},{1,2},{2,1},{3,0},{4,7},{5,6},{6,5},{7,4},{8,11},{9,10},{10,... | collective-permute-start | bytes 1216520 | tf_op jit(solution)/shard_map/ppermute | solution.py:294
  33.5 5.8 %collective-permute-start.15 = (bf16[528,128]{1,0:T(8,128)(2,1)S(1)}, bf16[528,128]{1,0:T(8,128)(2,1)S(1)}, u32[]{:S(2)}, u32[]{:S(2)}) collective-permute-start(bf16[528,128]{1,0:T(8,128)(2,1)S(1)} %ending.1), channel_id=1, source_target_pairs={{0,8},{1,9},{2,10},{3,11},{4,12},{5,13},{6,14},{7,15},{8,16},{9,17... | collective-permute-start | bytes 405512 | tf_op jit(solution)/shard_map/ppermute | solution.py:300
  40.4 16.1 %collective-permute-start.16 = (bf16[528,128]{1,0:T(8,128)(2,1)S(1)}, bf16[528,128]{1,0:T(8,128)(2,1)S(1)}, u32[]{:S(2)}, u32[]{:S(2)}) collective-permute-start(bf16[528,128]{1,0:T(8,128)(2,1)S(1)} %get-tuple-element.45), channel_id=1, source_target_pairs={{0,1},{1,0},{2,3},{3,2},{4,5},{5,4},{6,7},{7,6},{8,9},{9,8},{10,11... | collective-permute-start | bytes 405512 | tf_op jit(solution)/shard_map/ppermute | solution.py:294
  42.3 14.2 %collective-permute-start.17 = (bf16[528,128]{1,0:T(8,128)(2,1)S(1)}, bf16[528,128]{1,0:T(8,128)(2,1)S(1)}, u32[]{:S(2)}, u32[]{:S(2)}) collective-permute-start(bf16[528,128]{1,0:T(8,128)(2,1)S(1)} %get-tuple-element.46), channel_id=1, source_target_pairs={{0,2},{1,3},{2,0},{3,1},{4,6},{5,7},{6,4},{7,5},{8,10},{9,11},{10,... | collective-permute-start | bytes 405512 | tf_op jit(solution)/shard_map/ppermute | solution.py:294
  43.7 13.6 %collective-permute-start.18 = (bf16[528,128]{1,0:T(8,128)(2,1)S(1)}, bf16[528,128]{1,0:T(8,128)(2,1)S(1)}, u32[]{:S(2)}, u32[]{:S(2)}) collective-permute-start(bf16[528,128]{1,0:T(8,128)(2,1)S(1)} %get-tuple-element.47), channel_id=1, source_target_pairs={{0,3},{1,2},{2,1},{3,0},{4,7},{5,6},{6,5},{7,4},{8,11},{9,10},{10,... | collective-permute-start | bytes 405512 | tf_op jit(solution)/shard_map/ppermute | solution.py:294
  54.4 10.4 %collective-permute-start.7 = (bf16[128,16,128]{2,1,0:T(8,128)(2,1)S(1)}, bf16[128,16,128]{2,1,0:T(8,128)(2,1)S(1)}, u32[]{:S(2)}, u32[]{:S(2)}) collective-permute-start(bf16[128,16,128]{2,1,0:T(8,128)(2,1)S(1)} %soft.3), channel_id=1, source_target_pairs={{0,4},{1,5},{2,6},{3,7},{4,0},{5,1},{6,2},{7,3},{8,12},{9,13},{10,... | collective-permute-start | bytes 1572872 | tf_op jit(solution)/shard_map/ppermute | solution.py:294
  55.9 8.6 %collective-permute-start.19 = (bf16[528,128]{1,0:T(8,128)(2,1)S(1)}, bf16[528,128]{1,0:T(8,128)(2,1)S(1)}, u32[]{:S(2)}, u32[]{:S(2)}) collective-permute-start(bf16[528,128]{1,0:T(8,128)(2,1)S(1)} %get-tuple-element.48), channel_id=1, source_target_pairs={{0,4},{1,5},{2,6},{3,7},{4,0},{5,1},{6,2},{7,3},{8,12},{9,13},{10,... | collective-permute-start | bytes 405512 | tf_op jit(solution)/shard_map/ppermute | solution.py:294
  56.5 8.0 %collective-permute-start.20 = (bf16[528,128]{1,0:T(8,128)(2,1)S(1)}, bf16[528,128]{1,0:T(8,128)(2,1)S(1)}, u32[]{:S(2)}, u32[]{:S(2)}) collective-permute-start(bf16[528,128]{1,0:T(8,128)(2,1)S(1)} %get-tuple-element.49), channel_id=1, source_target_pairs={{0,5},{1,4},{2,7},{3,6},{4,1},{5,0},{6,3},{7,2},{8,13},{9,12},{10,... | collective-permute-start | bytes 405512 | tf_op jit(solution)/shard_map/ppermute | solution.py:294
  56.5 8.0 %collective-permute-start.21 = (bf16[528,128]{1,0:T(8,128)(2,1)S(1)}, bf16[528,128]{1,0:T(8,128)(2,1)S(1)}, u32[]{:S(2)}, u32[]{:S(2)}) collective-permute-start(bf16[528,128]{1,0:T(8,128)(2,1)S(1)} %get-tuple-element.50), channel_id=1, source_target_pairs={{0,6},{1,7},{2,4},{3,5},{4,2},{5,3},{6,0},{7,1},{8,14},{9,15},{10,... | collective-permute-start | bytes 405512 | tf_op jit(solution)/shard_map/ppermute | solution.py:294
  57.2 7.6 %copy-start.7 = (f32[32,128]{1,0:T(8,128)S(1)}, f32[32,128]{1,0:T(8,128)}, u32[]{:S(2)}) copy-start(f32[32,128]{1,0:T(8,128)} %gain_ref.1) | copy-start | bytes 49156
  57.2 7.5 %collective-permute-start.22 = (bf16[528,128]{1,0:T(8,128)(2,1)S(1)}, bf16[528,128]{1,0:T(8,128)(2,1)S(1)}, u32[]{:S(2)}, u32[]{:S(2)}) collective-permute-start(bf16[528,128]{1,0:T(8,128)(2,1)S(1)} %get-tuple-element.51), channel_id=1, source_target_pairs={{0,7},{1,6},{2,5},{3,4},{4,3},{5,2},{6,1},{7,0},{8,15},{9,14},{10,... | collective-permute-start | bytes 405512 | tf_op jit(solution)/shard_map/ppermute | solution.py:294
  (10 other events, 38.8 us)

commit v3 on v2

v3 whole, which is shorter than its diff:
```python
import functools
import math

import jax
import jax.numpy as jnp
from jax import lax
from jax.experimental import pallas as pl
from jax.experimental.pallas import tpu as pltpu
from jax.sharding import PartitionSpec as P

LOOK = 2
NEG_FILL = -1e30
NORM_EPS = 1e-06
TAIL = 16
F32 = jnp.float32
BF16 = jnp.bfloat16
AXES = ("ctx", "head")
VMEM = pl.BlockSpec(memory_space=pltpu.VMEM)
SMEM = pl.BlockSpec(memory_space=pltpu.SMEM)
ANY = pl.BlockSpec(memory_space=pl.ANY)
HBM = pl.BlockSpec(memory_space=pltpu.HBM)


def call(kernel, name, micros, limit_mib, ins, outs, out_specs, scratch=(), aliases=None, after=()):
    count = len(ins)

    def run(*refs):
        kernel(*refs[:count], *refs[count + len(after) :])

    made = pl.pallas_call(
        run,
        out_shape=outs,
        in_specs=list(ins) + [ANY] * len(after),
        out_specs=out_specs,
        scratch_shapes=list(scratch),
        input_output_aliases=aliases or {},
        compiler_params=pltpu.CompilerParams(vmem_limit_bytes=int(limit_mib * 1024 * 1024)),
        cost_estimate=pl.CostEstimate(flops=int(micros * 1e9), bytes_accessed=0, transcendentals=0),
        name=name,
    )
    return lambda *args: made(*args, *after)


def column(row):
    size = row.shape[1]
    return jnp.transpose(jnp.broadcast_to(row, (size, size)))


def dot(left, right, contract):
    return lax.dot_general(left, right, (contract, ((), ())), preferred_element_type=F32)


def split(value):
    high = value.astype(BF16)
    return high, (value - high.astype(F32)).astype(BF16)


def source_kernel(places, at_ref, rate_hbm, sid_hbm, key_hbm, value_hbm, soft_key_hbm, soft_value_hbm, soft_query_hbm, *rest):
    outs, rest = rest[:places], rest[places:]
    keys_by_head, values_by_head, mine_ref, other_ref, give_ref, rate_ref, sid_ref, key_in, value_in, soft_key_in, soft_value_in, stage, sems = rest
    heads, tokens, width = keys_by_head.shape
    per, half = heads // places, heads // LOOK
    kv_heads = soft_key_in.shape[1]
    kv_half = kv_heads // LOOK
    rows = mine_ref.shape[0]
    core, place = at_ref[0], at_ref[1]
    theirs = pl.ds(pl.multiple_of((LOOK - 1 - core) * half, half), half)
    moves = (
        (soft_key_hbm, soft_key_in),
        (soft_value_hbm, soft_value_in),
        (sid_hbm, sid_ref),
        (rate_hbm, rate_ref),
        (key_hbm, key_in),
        (value_hbm, value_in),
        (soft_query_hbm.at[:, theirs, :], give_ref.at[pl.ds(rows // half, tokens)]),
    )
    copies = [pltpu.make_async_copy(src, dst, sems.at[n]) for n, (src, dst) in enumerate(moves)]
    for copy in copies:
        copy.start()
    for at, ref in enumerate((soft_key_in, soft_value_in)):
        copies[at].wait()
        stage[...] = jnp.swapaxes(ref[...], 0, 1)
        for j in range(kv_half):
            start = (at * kv_half + j) * tokens
            mine_ref[pl.ds(start, tokens), :] = stage[core * kv_half + j]
            block = stage[(LOOK - 1 - core) * kv_half + j]
            other_ref[pl.ds(start, tokens), :] = block
            give_ref[pl.ds(start // half, tokens // half)] = block.reshape(tokens // half, half, width)
    copies[2].wait()
    sid_row = (sid_ref[...] + 1).astype(F32)
    tail = jnp.broadcast_to(sid_row, (TAIL, tokens)).astype(BF16)
    for ref in (mine_ref, other_ref):
        ref[pl.ds(2 * kv_half * tokens, TAIL), :] = tail
    give_ref[pl.ds(2 * kv_half * tokens // half, TAIL // half)] = tail.reshape(TAIL // half, half, tokens)
    open_row = (sid_row == jnp.max(sid_row, axis=1, keepdims=True)).astype(F32)
    behind = (tokens - 1 - lax.broadcasted_iota(jnp.int32, (1, tokens), 1)).astype(F32)
    copies[3].wait()
    copies[4].wait()
    keys_by_head[...] = jnp.swapaxes(key_in[...], 0, 1)
    copies[5].wait()
    values_by_head[...] = jnp.swapaxes(value_in[...], 0, 1)
    for k in range(places):
        for j in range(per):
            head = (place ^ k) * per + j
            values = values_by_head[head]
            weighted = jnp.transpose(keys_by_head[head].astype(F32)) * (open_row * jnp.exp(-rate_ref[head] * behind))
            high, low = split(weighted)
            state = dot(jnp.concatenate([high, low], 1), jnp.concatenate([values, values], 0), ((1,), (0,)))
            outs[k][pl.ds(j * width, width), :] = state.astype(BF16)
        outs[k][pl.ds(per * width, TAIL), :] = tail
    copies[6].wait()


def mix_kernel(places, at_ref, mine_ref, got_ref, before_ref, theirs_before_ref, home_ref, *outs):
    core, place = at_ref[0], at_ref[1]
    rows, width = mine_ref.shape
    heads = got_ref.shape[1]
    home_ref[2 * core] = mine_ref[...]
    home_ref[2 * core + 1] = before_ref[...]
    home_ref[2 * (1 - core)] = got_ref[pl.ds(0, rows // heads)].reshape(rows, width)
    home_ref[2 * (1 - core) + 1] = theirs_before_ref[...]
    for k in range(1, places):
        out = outs[k - 1]
        later = ((place ^ k) > place).astype(jnp.int32)
        out[0] = home_ref[0]
        out[1] = home_ref[3]
        out[2] = home_ref[1 + later]


def gather_slots(places, at_ref, pays, slots):
    for k in range(places):
        slots[at_ref[1] ^ k] = pays[k][...]


def last_of(pay, per, width):
    return jnp.max(pay[pl.ds(per * width, TAIL), :].astype(F32), axis=(0, 1), keepdims=True)


def advance(pay, per, width, span, rates, state, last):
    now = last_of(pay, per, width)
    same = (now == last).astype(F32)
    state = [
        pay[pl.ds(j * width, width), :].astype(F32) + (same * jnp.exp(jnp.full((1, width), -rates[j] * span, F32))) * state[j]
        for j in range(per)
    ]
    return state, now


def store_state(ref, state, last):
    width = ref.shape[1]
    for j, value in enumerate(state):
        ref[pl.ds(j * width, width), :] = value.astype(BF16)
    ref[pl.ds(len(state) * width, TAIL), :] = jnp.broadcast_to(last, (TAIL, width)).astype(BF16)


def ending_kernel(places, tokens, at_ref, rate_ref, *rest):
    pays, out_ref, slots = rest[:places], rest[places], rest[places + 1]
    width = out_ref.shape[1]
    per = (out_ref.shape[0] - TAIL) // width
    gather_slots(places, at_ref, pays, slots)
    rates = [rate_ref[at_ref[1] * per + j] for j in range(per)]
    state = [jnp.zeros((width, width), F32)] * per
    last = jnp.zeros((1, 1), F32)
    for block in range(places):
        state, last = advance(slots.at[block], per, width, tokens, rates, state, last)
    store_state(out_ref, state, last)


def prefix_kernel(places, tokens, at_ref, rate_ref, *rest):
    ahead, pays, outs = rest[:LOOK], rest[LOOK : LOOK + places], rest[LOOK + places : LOOK + 2 * places]
    slots, results = rest[LOOK + 2 * places :]
    width = ahead[0].shape[1]
    per = (ahead[0].shape[0] - TAIL) // width
    gather_slots(places, at_ref, pays, slots)
    rates = [rate_ref[at_ref[1] * per + j] for j in range(per)]
    state = [ahead[-1][pl.ds(j * width, width), :].astype(F32) for j in range(per)]
    last = last_of(ahead[-1], per, width)
    for group in reversed(ahead[:-1]):
        state, last = advance(group, per, width, places * tokens, rates, state, last)
    for block in range(places):
        store_state(results.at[block], state, last)
        if block < places - 1:
            state, last = advance(slots.at[block], per, width, tokens, rates, state, last)
    for k in range(places):
        outs[k][...] = results[at_ref[1] ^ k]


def prep_kernel(rate_ref, sid_ref, query_ref, keys_by_head, left_ref):
    heads, tokens, _ = keys_by_head.shape
    sid_row = (sid_ref[...] + 1).astype(F32)
    row_at = lax.broadcasted_iota(jnp.int32, (tokens, tokens), 0)
    lane = lax.broadcasted_iota(jnp.int32, (tokens, tokens), 1)
    allowed = ((row_at >= lane) & (column(sid_row) == sid_row)).astype(F32)
    ahead = (lax.broadcasted_iota(jnp.int32, (1, tokens), 1) + 1).astype(F32)
    left_ref[:, :, tokens:] = jnp.swapaxes(query_ref[...], 0, 1)
    for head in range(heads):
        weights = dot(left_ref[head, :, tokens:], keys_by_head[head], ((1,), (1,)))
        weights = weights * allowed * jnp.exp(rate_ref[head] * ahead)
        left_ref[head, :, :tokens] = weights.astype(BF16)


def final_kernel(places, at_ref, rate_ref, sid_ref, gain_ref, left_ref, values_by_head, keep_ref, *rest):
    pays, rest = rest[:places], rest[places:]
    light_hbm, soft_hbm, by_head, stage, sems = rest
    heads, tokens, width = values_by_head.shape
    half, per = heads // LOOK, heads // places
    core, place = at_ref[0], at_ref[1]

    def columns(which):
        return pl.ds(pl.multiple_of(which * half, half), half)

    copies = [pltpu.make_async_copy(keep_ref, soft_hbm.at[:, columns(core), :], sems.at[LOOK])]
    copies[0].start()
    sid_column = column((sid_ref[...] + 1).astype(F32))
    entry = last_of(pays[0], per, width)
    continues = (sid_column == entry).astype(BF16)
    ahead = (lax.broadcasted_iota(jnp.int32, (tokens, 1), 0) + 1).astype(F32)
    span = places // LOOK
    for part in range(LOOK):
        which = (place // span) ^ part
        for k in range(part * span, (part + 1) * span):
            for j in range(per):
                head = (place ^ k) * per + j
                left = jnp.concatenate([left_ref[head, :, :tokens], left_ref[head, :, tokens:] * continues], 1)
                right = jnp.concatenate([values_by_head[head], pays[k][pl.ds(j * width, width), :]], 0)
                raw = dot(left, right, ((1,), (0,)))
                lead = jnp.exp(-rate_ref[head] * ahead)
                mean_square = jnp.mean(raw * raw, axis=1, keepdims=True) * (lead * lead)
                out = raw * (lead * lax.rsqrt(mean_square + NORM_EPS)) * gain_ref[pl.ds(head, 1), :]
                by_head[head] = out.astype(BF16)
        stage[part] = jnp.swapaxes(by_head[pl.ds(which * half, half)], 0, 1)
        copies.append(pltpu.make_async_copy(stage.at[part], light_hbm.at[:, columns(which), :], sems.at[part]))
        copies[-1].start()
    for copy in copies:
        copy.wait()


def beside_kernel(at_ref, got_ref, _, out_hbm, sem):
    half = got_ref.shape[1]
    columns = pl.ds(pl.multiple_of((LOOK - 1 - at_ref[0]) * half, half), half)
    copy = pltpu.make_async_copy(got_ref, out_hbm.at[:, columns, :], sem)
    copy.start()
    copy.wait()


class Soft:
    def __init__(self, places, at_ref, tokens, share, heads, rows, marks, codes, fills):
        self.places, self.core, self.place = places, at_ref[0], at_ref[1]
        self.tokens, self.share, self.heads, self.rows = tokens, share, heads, rows
        self.kv_heads = heads // share
        self.marks, self.codes, self.fills = marks, codes, fills
        self.lane = lax.broadcasted_iota(jnp.int32, (tokens, tokens), 1)

    def spread(self, value):
        tokens, share = self.tokens, self.share
        value = jnp.broadcast_to(value.reshape(tokens, 1, tokens), (tokens, share, tokens))
        return value.reshape(tokens * share, tokens)

    def sids(self, pick):
        ref, slot = pick
        return column(ref[slot, pl.ds(2 * self.kv_heads * self.tokens, TAIL), :].astype(F32)[0:1, :])

    def far(self, block, ks, pays):
        picks = []
        for k, pay in zip(ks, pays):
            later = ((self.place ^ k) > self.place).astype(jnp.int32)
            picks.append((pay, 2 * later * (1 - block)))
            picks.append((pay, 1 + (1 - later) * block))
        return picks

    def setup(self, picks, own, causal):
        tokens, lanes = self.tokens, self.lane.astype(F32)
        for at, pick in enumerate(picks):
            self.codes[pl.ds(at * tokens, tokens), :] = (self.sids(pick) == lanes).astype(BF16)
        self.marks[...] = self.spread(jnp.where(self.sids(own) == lanes, 0.0, NEG_FILL)).astype(BF16)
        if causal:
            row_at = lax.broadcasted_iota(jnp.int32, (tokens, tokens), 0)
            self.fills[...] = self.spread(jnp.where(row_at >= self.lane, 0.0, NEG_FILL))

    def query(self, ref, first_token, first_head):
        wide = ref[pl.ds(first_token, self.tokens), pl.ds(first_head, self.heads), :].astype(F32)
        width, share = wide.shape[2], self.share
        return [
            wide[:, g * share : (g + 1) * share, :].reshape(self.tokens * share, width).astype(BF16)
            for g in range(self.kv_heads)
        ]

    def scores(self, g, query, picks, causal):
        tokens = self.tokens
        query = jnp.concatenate([query, self.marks[...]], 1)
        keys = jnp.concatenate([ref[slot, pl.ds(g * tokens, tokens), :] for ref, slot in picks], 0)
        codes = self.codes[pl.ds(0, len(picks) * tokens), :]
        scores = dot(query, jnp.concatenate([keys, codes], 1), ((1,), (1,)))
        if causal:
            last = (len(picks) - 1) * tokens
            scores = jnp.concatenate([scores[:, :last], scores[:, last:] + self.fills[...]], 1)
        return scores

    def mixed(self, g, probs, picks):
        tokens = self.tokens
        rows = pl.ds((self.kv_heads + g) * tokens, tokens)
        values = jnp.concatenate([ref[slot, rows, :] for ref, slot in picks], 0)
        return dot(probs.astype(BF16), jnp.concatenate([values, jnp.ones_like(values)], 1), ((1,), (0,)))


    def queries(self, own, got_ref, query_ref):
        if own:
            return self.query(query_ref, 0, pl.multiple_of(self.core * self.heads, self.heads))
        return self.query(got_ref, self.rows // self.heads, 0)

    def added(self, g, query, picks, sums, before):
        width = before.shape[1]
        factor = width ** (-0.5) * math.log2(math.e)
        scores = self.scores(g, query, picks, False)
        peak = jnp.maximum(before, jnp.max(scores, axis=1, keepdims=True))
        probs = jnp.exp2((scores - peak[:, 0:1]) * factor)
        scale = jnp.exp2((before - peak) * factor)
        return self.mixed(g, probs, picks) + sums * jnp.concatenate([scale, scale], 1), peak


def home_kernel(places, share, at_ref, got_ref, query_ref, home_ref, sums_ref, peaks_ref, *rooms):
    tokens, width = query_ref.shape[0], query_ref.shape[2]
    soft = Soft(places, at_ref, tokens, share, got_ref.shape[1], home_ref.shape[1], *rooms)
    factor = width ** (-0.5) * math.log2(math.e)
    for own in (False, True):
        block = soft.core if own else 1 - soft.core
        mine = (home_ref, 2 * block)
        picks = [(home_ref, 1 - block), (home_ref, 3), mine]
        soft.setup(picks, mine, True)
        for g, query in enumerate(soft.queries(own, got_ref, query_ref)):
            scores = soft.scores(g, query, picks, True)
            peak = jnp.max(scores, axis=1, keepdims=True)
            at = (soft.kv_heads if own else 0) + g
            sums_ref[at] = soft.mixed(g, jnp.exp2((scores - peak) * factor), picks)
            peaks_ref[at] = jnp.broadcast_to(peak, (tokens * share, width))


def near_kernel(places, near, share, at_ref, got_ref, query_ref, home_ref, sums_in, peaks_in, *rest):
    pays, sums_ref, peaks_ref = rest[: len(near)], rest[len(near)], rest[len(near) + 1]
    soft = Soft(places, at_ref, query_ref.shape[0], share, got_ref.shape[1], home_ref.shape[1], *rest[len(near) + 2 :])
    for own in (False, True):
        block = soft.core if own else 1 - soft.core
        picks = soft.far(block, near, pays)
        soft.setup(picks, (home_ref, 2 * block), False)
        for g, query in enumerate(soft.queries(own, got_ref, query_ref)):
            at = (soft.kv_heads if own else 0) + g
            sums_ref[at], peaks_ref[at] = soft.added(g, query, picks, sums_in[at], peaks_in[at])


def far_kernel(places, far, share, at_ref, got_ref, query_ref, home_ref, sums_ref, peaks_ref, *rest):
    pays, outs, rooms = rest[: len(far)], rest[len(far) : len(far) + 2], rest[len(far) + 2 :]
    tokens, heads, width = query_ref.shape[0], got_ref.shape[1], query_ref.shape[2]
    soft = Soft(places, at_ref, tokens, share, heads, home_ref.shape[1], *rooms)
    for own in (False, True):
        block = soft.core if own else 1 - soft.core
        picks = soft.far(block, far, pays)
        soft.setup(picks, (home_ref, 2 * block), False)
        mixed = []
        for g, query in enumerate(soft.queries(own, got_ref, query_ref)):
            at = (soft.kv_heads if own else 0) + g
            out, _ = soft.added(g, query, picks, sums_ref[at], peaks_ref[at])
            mixed.append((out[:, :width] / out[:, width:]).reshape(tokens, share, width))
        outs[own][...] = jnp.concatenate(mixed, 1).astype(BF16)


def body(
    light_query,
    light_keys,
    light_values,
    decay_rate,
    norm_gain,
    soft_query,
    soft_keys,
    soft_values,
    segment_ids,
):
    places = lax.axis_size("head")
    n_all = lax.axis_size("ctx") * places
    members = LOOK * places
    core = lax.rem(lax.axis_index("ctx"), LOOK)
    place = lax.axis_index("head")
    at = jnp.stack([core, place, core * places + place]).astype(jnp.int32)
    tokens, heads, width = light_query.shape
    kv_heads = soft_keys.shape[1]
    per, half, kv_half = heads // places, heads // LOOK, kv_heads // LOOK
    sid_row = segment_ids.reshape(1, tokens)

    def partner(value, k):
        pairs = [(i, i - i % members + ((i % members) ^ k)) for i in range(n_all)]
        return lax.ppermute(value, AXES, pairs)

    def across(value):
        return partner(value, places)

    def to_places(values):
        return [values[0]] + [partner(values[k], k) for k in range(1, places)]

    def onward(value, groups):
        step = groups * places
        return lax.ppermute(value, AXES, [(i, i + step) for i in range(n_all - step)])

    def onward_across(value):
        pairs = [(i, i + members + (places if i // places % LOOK == 0 else -places)) for i in range(n_all - members)]
        return lax.ppermute(value, AXES, pairs)

    def shape(*dims):
        return jax.ShapeDtypeStruct(dims, BF16)

    def room(*dims, dtype=BF16):
        return pltpu.VMEM(dims, dtype)

    def semaphores(count):
        return pltpu.SemaphoreType.DMA((count,))

    pay = shape(2 * kv_half * tokens + TAIL, width)
    given = shape(pay.shape[0] // half + tokens, half, width)
    state = shape(per * width + TAIL, width)
    by_head = shape(heads, tokens, width)
    half_out = shape(tokens, half, width)
    slots = room(places, *state.shape)
    sid_room = room(1, tokens, dtype=jnp.int32)

    def held(value):
        return pltpu.with_memory_space_constraint(value, pltpu.HBM)

    made = call(
        functools.partial(source_kernel, places), "source", 0, 16, [SMEM] + [HBM] * 7,
        [state] * places + [by_head] * 2 + [pay, pay, given], [VMEM] * (places + 5),
        [pltpu.SMEM((heads,), F32), sid_room] + [room(tokens, heads, width)] * 2 + [room(tokens, kv_heads, width)] * 2
        + [room(kv_heads, tokens, width), semaphores(7)],
    )(at, *[held(x) for x in (decay_rate, sid_row, light_keys, light_values, soft_keys, soft_values, soft_query)])
    keys_by_head, values_by_head, mine, other, give = made[places:]
    states = to_places(made[:places])
    got = across(give)
    before = onward(mine, LOOK)
    theirs_before = onward_across(other)

    left = call(
        prep_kernel, "prep", 0, 16, [SMEM, VMEM, VMEM, VMEM], shape(heads, tokens, tokens + width), VMEM
    )(decay_rate, sid_row, light_query, keys_by_head)
    mixed = call(
        functools.partial(mix_kernel, places), "mix", 0, 8, [SMEM] + [VMEM] * 4,
        [shape(4, *pay.shape)] + [shape(3, *pay.shape)] * (places - 1), [VMEM] * places, after=[left, *states[places // 2 + 1 :]],
    )(at, mine, got, before, theirs_before)
    home = mixed[0]
    parcels = to_places(mixed)

    ending = call(
        functools.partial(ending_kernel, places, tokens), "ending", 0, 8, [SMEM] * 2 + [VMEM] * places, state, VMEM,
        [slots], after=[home],
    )(at, decay_rate, *states)
    ahead = [onward(ending, groups) for groups in range(1, LOOK + 1)]
    share = half // kv_half
    near, far = range(1, places // 2 + 1), range(places // 2 + 1, places)
    queries = tokens * share

    def soft_rooms(blocks):
        return [room(queries, tokens), room(blocks * tokens, width), room(queries, tokens, dtype=F32)]

    def limit(blocks):
        return (blocks * tokens * queries * 14 + 8 * half_out.size) / 2**20 + 8

    sums_like = [
        jax.ShapeDtypeStruct((LOOK * kv_half, queries, 2 * width), F32),
        jax.ShapeDtypeStruct((LOOK * kv_half, queries, width), F32),
    ]
    sums, peaks = call(
        functools.partial(home_kernel, places, share), "home", 0, limit(3), [SMEM] + [VMEM] * 3, sums_like, [VMEM, VMEM],
        soft_rooms(3), after=[ending],
    )(at, got, soft_query, home)
    prefixed = call(
        functools.partial(prefix_kernel, places, tokens), "prefix", 0, 12, [SMEM] * 2 + [VMEM] * (places + LOOK),
        [state] * places, [VMEM] * places, [slots, slots], after=[sums],
    )(at, decay_rate, *ahead, *states)
    entries = to_places(prefixed)

    sums, peaks = call(
        functools.partial(near_kernel, places, near, share), "near", 30, limit(2 * len(near)), [SMEM] + [VMEM] * (5 + len(near)),
        sums_like, [VMEM, VMEM], soft_rooms(2 * len(near)), aliases={4: 0, 5: 1}, after=[prefixed[0]],
    )(at, got, soft_query, home, sums, peaks, *[parcels[k] for k in near])

    soft_theirs, soft_kept = call(
        functools.partial(far_kernel, places, far, share), "far", 0, limit(2 * len(far)), [SMEM] + [VMEM] * (5 + len(far)),
        [half_out] * 2, [VMEM] * 2, soft_rooms(2 * len(far)),
    )(at, got, soft_query, home, sums, peaks, *[parcels[k] for k in far])
    soft_got = across(soft_theirs)

    whole = shape(tokens, heads, width)
    light_out, soft_out = call(
        functools.partial(final_kernel, places), "final", 15, 16, [SMEM] * 2 + [VMEM] * (5 + places), [whole, whole],
        [HBM, HBM], [room(heads, tokens, width), room(LOOK, tokens, half, width), semaphores(LOOK + 1)],
    )(at, decay_rate, sid_row, norm_gain, left, values_by_head, soft_kept, *entries)
    soft_out = call(
        beside_kernel, "beside", 0, 8, [SMEM, VMEM, HBM], whole, HBM, [pltpu.SemaphoreType.DMA], aliases={2: 0}
    )(at, soft_got, soft_out)
    return (light_out, soft_out)


def solution(mesh):
    placed = P(("ctx", "head"), None, None)
    return jax.shard_map(
        body,
        mesh=mesh,
        in_specs=(placed, placed, placed, P(), P(), placed, placed, placed, P(("ctx", "head"))),
        out_specs=(placed, placed),
        check_vma=False,
    )
```

time: 68.8 us -> 61.1 us (0.89)
  the two profiles are of different devices: /device:TPU:0 before, /device:TPU:25 now
where the time goes in v3:
time: 61.1 us; the launch traced here: 60.9 us
  Pallas kernels  29.2 us (48%)
  starting transfers between devices  15.4 us (25%)
  waiting for transfers between devices  15.2 us (25%)
  between operations  0.98 us (2%)
    pallas_call x10, Pallas kernels, call(): return lambda *args: made(*args, *after)  29.2 us
    ppermute x11, starting transfers between devices, partner(): return lax.ppermute(value, AXES, pairs)  10.1 us
    ppermute x11, waiting for transfers between devices, partner(): return lax.ppermute(value, AXES, pairs)  7.14 us
    ppermute x1, waiting for transfers between devices, onward_across(): return lax.ppermute(value, AXES, pairs)  5.15 us
    ppermute x3, starting transfers between devices, onward(): lax.ppermute(value, AXES, [(i, i + step) for i in range(n_all - step)])  4.06 us
    ppermute x3, waiting for transfers between devices, onward(): lax.ppermute(value, AXES, [(i, i + step) for i in range(n_all - step)])  2.89 us
    ppermute x1, starting transfers between devices, onward_across(): return lax.ppermute(value, AXES, pairs)  1.28 us
  transfers between devices with their start and end apart: 15, of which 6 were waited for; matrix products, arithmetic and copies ran while one was open for 0% of the time, Pallas kernels for 40%

profile of v3, /device:TPU:25, one launch (start us, length us, event | category | flops | bytes accessed | tf_op | source)
XLA Modules:
  0.0 60.9 jit_solution(1855806769518220151)
XLA Ops:
  0.7 3.6 %source.1 = (bf16[1040,128]{1,0:T(8,128)(2,1)S(1)}, bf16[1040,128]{1,0:T(8,128)(2,1)S(1)}, bf16[1040,128]{1,0:T(8,128)(2,1)S(1)}, bf16[1040,128]{1,0:T(8,128)(2,...) custom-call(s32[3]{0:T(128)S(1)} %pad_add_fusion.refs_0_, ...), custom_call_target="tpu_custom_call" | custom-call | tf_op jit(solution)/shard_map/source/pallas_call | solution.py:41
  4.3 0.7 %collective-permute-start = (bf16[161,16,128]{2,1,0:T(8,128)(2,1)S(1)}, bf16[161,16,128]{2,1,0:T(8,128)(2,1)S(1)}, u32[]{:S(2)}, u32[]{:S(2)}) collective-permute-start(bf16[161,16,128]{2,1,0:T(8,128)(2,1)S(1)} %get-tuple-element.29), channel_id=1, source_target_pairs={{0,4},{1,5},{2,6},{3,7},{4,0},{5,1},{6,2},{7,3},{8,12},{9,13},{10,... | collective-permute-start | bytes 1978376 | tf_op jit(solution)/shard_map/ppermute | solution.py:390
  5.1 2.2 %collective-permute-start.3 = (bf16[1040,128]{1,0:T(8,128)(2,1)S(1)}, bf16[1040,128]{1,0:T(8,128)(2,1)S(1)}, u32[]{:S(2)}, u32[]{:S(2)}) collective-permute-start(bf16[1040,128]{1,0:T(8,128)(2,1)S(1)} %get-tuple-element.32), channel_id=1, source_target_pairs={{0,3},{1,2},{2,1},{3,0},{4,7},{5,6},{6,5},{7,4},{8,11},{9,10},{10,... | collective-permute-start | bytes 798728 | tf_op jit(solution)/shard_map/ppermute | solution.py:390
  7.3 1.3 %collective-permute-start.2 = (bf16[528,128]{1,0:T(8,128)(2,1)S(1)}, bf16[528,128]{1,0:T(8,128)(2,1)S(1)}, u32[]{:S(2)}, u32[]{:S(2)}) collective-permute-start(bf16[528,128]{1,0:T(8,128)(2,1)S(1)} %get-tuple-element.31), channel_id=1, source_target_pairs={{0,12},{1,13},{2,14},{3,15},{4,8},{5,9},{6,10},{7,11},{8,20},{9,21... | collective-permute-start | bytes 405512 | tf_op jit(solution)/shard_map/ppermute | solution.py:404
  8.6 1.3 %collective-permute-start.1 = (bf16[528,128]{1,0:T(8,128)(2,1)S(1)}, bf16[528,128]{1,0:T(8,128)(2,1)S(1)}, u32[]{:S(2)}, u32[]{:S(2)}) collective-permute-start(bf16[528,128]{1,0:T(8,128)(2,1)S(1)} %get-tuple-element.30.refs_1_), channel_id=1, source_target_pairs={{0,8},{1,9},{2,10},{3,11},{4,12},{5,13},{6,14},{7,15},{8,16},{9,17... | collective-permute-start | bytes 405512 | tf_op jit(solution)/shard_map/ppermute | solution.py:400
  10.2 5.2 %collective-permute-done.2.refs_4_ = bf16[528,128]{1,0:T(8,128)(2,1)S(1)} collective-permute-done((bf16[528,128]{1,0:T(8,128)(2,1)S(1)}, bf16[528,128]{1,0:T(8,128)(2,1)S(1)}, u32[]{:S(2)}, u32[]{:S(2)}) %collective-permute-start.2) | collective-permute-done | bytes 135200 | tf_op jit(solution)/shard_map/ppermute | solution.py:404
  15.6 1.4 %prep.1.refs_5_.refs_4_ = bf16[32,128,256]{2,1,0:T(8,128)(2,1)S(1)} custom-call(f32[32]{0:T(128)S(1)} %copy-done.2, s32[1,128]{1,0:T(1,128)S(1)} %bitcast.5, bf16[128,32,128]{2,1,0:T(8,128)(2,1)S(1)} %copy-done.1, bf16[32,128,128]{2,1,0:T(8,128)(2,1)S(1)} %get-tuple-element.27.refs_3_), custom_call_target="tpu_custom_call" | custom-call | tf_op jit(solution)/shard_map/prep/pallas_call | solution.py:41
  17.0 0.5 collective-permute-done.1.refs_3_
  17.5 0.7 %mix.1 = (bf16[4,528,128]{2,1,0:T(8,128)(2,1)S(1)}, bf16[3,528,128]{2,1,0:T(8,128)(2,1)S(1)}, bf16[3,528,128]{2,1,0:T(8,128)(2,1)S(1)}, bf16[3,528,128]{2,1,0:T(8,128)(2,1)S(1)}) custom-call(s32[3]{0:T(128)S(1)} %pad_add_fusion.refs_0_, bf16[528,128]{1,0:T(8,128)(2,1)S(1)} %get-tuple-element.30.refs_1_, ...), custom_call_target="tpu_custom_call" | custom-call | tf_op jit(solution)/shard_map/mix/pallas_call | solution.py:41
  18.6 0.7 %collective-permute-start.7 = (bf16[3,528,128]{2,1,0:T(8,128)(2,1)S(1)}, bf16[3,528,128]{2,1,0:T(8,128)(2,1)S(1)}, u32[]{:S(2)}, u32[]{:S(2)}) collective-permute-start(bf16[3,528,128]{2,1,0:T(8,128)(2,1)S(1)} %get-tuple-element.40), channel_id=1, source_target_pairs={{0,2},{1,3},{2,0},{3,1},{4,6},{5,7},{6,4},{7,5},{8,10},{9,11},{10,... | collective-permute-start | bytes 1216520 | tf_op jit(solution)/shard_map/ppermute | solution.py:390
  19.7 3.9 %collective-permute-done.5.refs_4_.refs_6_ = bf16[1040,128]{1,0:T(8,128)(2,1)S(1)} collective-permute-done((bf16[1040,128]{1,0:T(8,128)(2,1)S(1)}, bf16[1040,128]{1,0:T(8,128)(2,1)S(1)}, u32[]{:S(2)}, u32[]{:S(2)}) %collective-permute-start.5) | collective-permute-done | bytes 266272 | tf_op jit(solution)/shard_map/ppermute | solution.py:390
  23.6 1.0 %ending.1.refs_4_ = bf16[1040,128]{1,0:T(8,128)(2,1)S(1)} custom-call(s32[3]{0:T(128)S(1)} %pad_add_fusion.refs_0_, f32[32]{0:T(128)S(1)} %copy-done.2, bf16[1040,128]{1,0:T(8,128)(2,1)S(1)} %get-tuple-element.34.refs_2_.refs_4_, bf16[1040,128]{1,0:T(8,128)(2,1)S(1)} %collective-permute-done.4.refs_3_.refs_5_, ...), custom_call_target="tpu_custom_call" | custom-call | tf_op jit(solution)/shard_map/ending/pallas_call | solution.py:41
  24.5 1.3 %collective-permute-start.9 = (bf16[1040,128]{1,0:T(8,128)(2,1)S(1)}, bf16[1040,128]{1,0:T(8,128)(2,1)S(1)}, u32[]{:S(2)}, u32[]{:S(2)}) collective-permute-start(bf16[1040,128]{1,0:T(8,128)(2,1)S(1)} %ending.1.refs_4_), channel_id=1, source_target_pairs={{0,8},{1,9},{2,10},{3,11},{4,12},{5,13},{6,14},{7,15},{8,16},{9,17... | collective-permute-start | bytes 798728 | tf_op jit(solution)/shard_map/ppermute | solution.py:400
  25.8 1.5 %collective-permute-start.8 = (bf16[1040,128]{1,0:T(8,128)(2,1)S(1)}, bf16[1040,128]{1,0:T(8,128)(2,1)S(1)}, u32[]{:S(2)}, u32[]{:S(2)}) collective-permute-start(bf16[1040,128]{1,0:T(8,128)(2,1)S(1)} %ending.1.refs_4_), channel_id=1, source_target_pairs={{0,4},{1,5},{2,6},{3,7},{4,8},{5,9},{6,10},{7,11},{8,12},{9,13},{1... | collective-permute-start | bytes 798728 | tf_op jit(solution)/shard_map/ppermute | solution.py:400
  27.6 3.7 %home.1 = (f32[4,1024,256]{2,1,0:T(8,128)S(1)}, f32[4,1024,128]{2,1,0:T(8,128)S(1)}) custom-call(s32[3]{0:T(128)S(1)} %pad_add_fusion.refs_0_, bf16[161,16,128]{2,1,0:T(8,128)(2,1)S(1)} %collective-permute-done.refs_2_.refs_1_, bf16[128,32,128]{2,1,0:T(8,128)(2,1)S(1)} %copy-done, bf16[4,528,128]{2,1,0:T(8,128)(2,1)S(1)} %get-tuple-element.33.refs_6_.refs_3_, ...), custom_call_target="tpu_custom_call" | custom-call | tf_op jit(solution)/shard_map/home/pallas_call | solution.py:41
  31.3 2.3 %collective-permute-done.9.refs_3_ = bf16[1040,128]{1,0:T(8,128)(2,1)S(1)} collective-permute-done((bf16[1040,128]{1,0:T(8,128)(2,1)S(1)}, bf16[1040,128]{1,0:T(8,128)(2,1)S(1)}, u32[]{:S(2)}, u32[]{:S(2)}) %collective-permute-start.9) | collective-permute-done | bytes 266272 | tf_op jit(solution)/shard_map/ppermute | solution.py:400
  33.6 1.1 %prefix.1 = (bf16[1040,128]{1,0:T(8,128)(2,1)S(1)}, bf16[1040,128]{1,0:T(8,128)(2,1)S(1)}, bf16[1040,128]{1,0:T(8,128)(2,1)S(1)}, bf16[1040,128]{1,0:T(8,128)(2,1)S(1)}) custom-call(s32[3]{0:T(128)S(1)} %pad_add_fusion.refs_0_, f32[32]{0:T(128)S(1)} %copy-done.2, bf16[1040,128]{1,0:T(8,128)(2,1)S(1)} %collective-permute-done.8.refs_2_, ...), custom_call_target="tpu_custom_call" | custom-call | tf_op jit(solution)/shard_map/prefix/pallas_call | solution.py:41
  35.3 2.2 %collective-permute-start.13 = (bf16[1040,128]{1,0:T(8,128)(2,1)S(1)}, bf16[1040,128]{1,0:T(8,128)(2,1)S(1)}, u32[]{:S(2)}, u32[]{:S(2)}) collective-permute-start(bf16[1040,128]{1,0:T(8,128)(2,1)S(1)} %get-tuple-element.48), channel_id=1, source_target_pairs={{0,3},{1,2},{2,1},{3,0},{4,7},{5,6},{6,5},{7,4},{8,11},{9,10},{10,... | collective-permute-start | bytes 798728 | tf_op jit(solution)/shard_map/ppermute | solution.py:390
  37.5 2.8 %collective-permute-done.7.refs_7_ = bf16[3,528,128]{2,1,0:T(8,128)(2,1)S(1)} collective-permute-done((bf16[3,528,128]{2,1,0:T(8,128)(2,1)S(1)}, bf16[3,528,128]{2,1,0:T(8,128)(2,1)S(1)}, u32[]{:S(2)}, u32[]{:S(2)}) %collective-permute-start.7) | collective-permute-done | bytes 405536 | tf_op jit(solution)/shard_map/ppermute | solution.py:390
  40.3 6.6 %near.1 = (f32[4,1024,256]{2,1,0:T(8,128)S(1)}, f32[4,1024,128]{2,1,0:T(8,128)S(1)}) custom-call(s32[3]{0:T(128)S(1)} %pad_add_fusion.refs_0_, bf16[161,16,128]{2,1,0:T(8,128)(2,1)S(1)} %collective-permute-done.refs_2_.refs_1_, bf16[128,32,128]{2,1,0:T(8,128)(2,1)S(1)} %copy-done, ...), custom_call_target="tpu_custom_call", output_to_operand_aliasing={{0}: (4, {}), {1}: (5, {})} | custom-call | flops 30000001024 | tf_op jit(solution)/shard_map/near/pallas_call | solution.py:41
  46.9 6.5 %far.1 = (bf16[128,16,128]{2,1,0:T(8,128)(2,1)S(1)}, bf16[128,16,128]{2,1,0:T(8,128)(2,1)S(1)}) custom-call(s32[3]{0:T(128)S(1)} %pad_add_fusion.refs_0_, bf16[161,16,128]{2,1,0:T(8,128)(2,1)S(1)} %collective-permute-done.refs_2_.refs_1_, bf16[128,32,128]{2,1,0:T(8,128)(2,1)S(1)} %copy-done, bf16[4,528,128]{2,1,0:T(8,128)(2,1)S(1)} %get-tuple-element.33.refs_6_.refs_3_, ...), custom_call_target="tpu_custom_call" | custom-call | tf_op jit(solution)/shard_map/far/pallas_call | solution.py:41
  53.5 2.6 %collective-permute-start.14 = (bf16[128,16,128]{2,1,0:T(8,128)(2,1)S(1)}, bf16[128,16,128]{2,1,0:T(8,128)(2,1)S(1)}, u32[]{:S(2)}, u32[]{:S(2)}) collective-permute-start(bf16[128,16,128]{2,1,0:T(8,128)(2,1)S(1)} %get-tuple-element.50), channel_id=1, source_target_pairs={{0,4},{1,5},{2,6},{3,7},{4,0},{5,1},{6,2},{7,3},{8,12},{9,13},{10,... | collective-permute-start | bytes 1572872 | tf_op jit(solution)/shard_map/ppermute | solution.py:390
  56.1 3.3 %final.1 = (bf16[128,32,128]{2,1,0:T(8,128)(2,1)}, bf16[128,32,128]{2,1,0:T(8,128)(2,1)}) custom-call(s32[3]{0:T(128)S(1)} %pad_add_fusion.refs_0_, f32[32]{0:T(128)S(1)} %copy-done.2, s32[1,128]{1,0:T(1,128)S(1)} %bitcast.6, f32[32,128]{1,0:T(8,128)S(1)} %copy-done.4, bf16[32,128,256]{2,1,0:T(8,128)(2,1)S(1)} %prep.1.refs_5_.refs_4_, ...), custom_call_target="tpu_custom_call" | custom-call | flops 15000000512 | tf_op jit(solution)/shard_map/final/pallas_call | solution.py:41
  59.4 1.4 %beside.1 = bf16[128,32,128]{2,1,0:T(8,128)(2,1)} custom-call(s32[3]{0:T(128)S(1)} %pad_add_fusion.refs_0_, bf16[128,16,128]{2,1,0:T(8,128)(2,1)S(1)} %collective-permute-done.14.refs_1_, bf16[128,32,128]{2,1,0:T(8,128)(2,1)} %get-tuple-element.51.refs_2_), custom_call_target="tpu_custom_call", output_to_operand_aliasing={{}: (2, {})} | custom-call | tf_op jit(solution)/shard_map/beside/pallas_call | solution.py:41
  (27 shorter events, 2.2 us)
Async XLA Ops:
  0.6 14.9 %copy-start.2 = (f32[32]{0:T(128)S(1)}, f32[32]{0:T(128)}, u32[]{:S(2)}) copy-start(f32[32]{0:T(128)} %refs_1_.7) | copy-start | bytes 388
  0.6 14.9 %copy-start.3 = (s32[128]{0:T(128)S(1)}, s32[128]{0:T(128)}, u32[]{:S(2)}) copy-start(s32[128]{0:T(128)} %param.17) | copy-start | bytes 1540
  0.7 14.9 %copy-start.1 = (bf16[128,32,128]{2,1,0:T(8,128)(2,1)S(1)}, bf16[128,32,128]{2,1,0:T(8,128)(2,1)}, u32[]{:S(2)}) copy-start(bf16[128,32,128]{2,1,0:T(8,128)(2,1)} %refs_2_.4) | copy-start | bytes 3145732
  4.3 13.2 %collective-permute-start = (bf16[161,16,128]{2,1,0:T(8,128)(2,1)S(1)}, bf16[161,16,128]{2,1,0:T(8,128)(2,1)S(1)}, u32[]{:S(2)}, u32[]{:S(2)}) collective-permute-start(bf16[161,16,128]{2,1,0:T(8,128)(2,1)S(1)} %get-tuple-element.29), channel_id=1, source_target_pairs={{0,4},{1,5},{2,6},{3,7},{4,0},{5,1},{6,2},{7,3},{8,12},{9,13},{10,... | collective-permute-start | bytes 1978376 | tf_op jit(solution)/shard_map/ppermute | solution.py:390
  5.1 12.5 %collective-permute-start.3 = (bf16[1040,128]{1,0:T(8,128)(2,1)S(1)}, bf16[1040,128]{1,0:T(8,128)(2,1)S(1)}, u32[]{:S(2)}, u32[]{:S(2)}) collective-permute-start(bf16[1040,128]{1,0:T(8,128)(2,1)S(1)} %get-tuple-element.32), channel_id=1, source_target_pairs={{0,3},{1,2},{2,1},{3,0},{4,7},{5,6},{6,5},{7,4},{8,11},{9,10},{10,... | collective-permute-start | bytes 798728 | tf_op jit(solution)/shard_map/ppermute | solution.py:390
  7.3 8.1 %collective-permute-start.2 = (bf16[528,128]{1,0:T(8,128)(2,1)S(1)}, bf16[528,128]{1,0:T(8,128)(2,1)S(1)}, u32[]{:S(2)}, u32[]{:S(2)}) collective-permute-start(bf16[528,128]{1,0:T(8,128)(2,1)S(1)} %get-tuple-element.31), channel_id=1, source_target_pairs={{0,12},{1,13},{2,14},{3,15},{4,8},{5,9},{6,10},{7,11},{8,20},{9,21... | collective-permute-start | bytes 405512 | tf_op jit(solution)/shard_map/ppermute | solution.py:404
  8.6 9.0 %collective-permute-start.1 = (bf16[528,128]{1,0:T(8,128)(2,1)S(1)}, bf16[528,128]{1,0:T(8,128)(2,1)S(1)}, u32[]{:S(2)}, u32[]{:S(2)}) collective-permute-start(bf16[528,128]{1,0:T(8,128)(2,1)S(1)} %get-tuple-element.30.refs_1_), channel_id=1, source_target_pairs={{0,8},{1,9},{2,10},{3,11},{4,12},{5,13},{6,14},{7,15},{8,16},{9,17... | collective-permute-start | bytes 405512 | tf_op jit(solution)/shard_map/ppermute | solution.py:400
  9.9 9.9 %collective-permute-start.4 = (bf16[1040,128]{1,0:T(8,128)(2,1)S(1)}, bf16[1040,128]{1,0:T(8,128)(2,1)S(1)}, u32[]{:S(2)}, u32[]{:S(2)}) collective-permute-start(bf16[1040,128]{1,0:T(8,128)(2,1)S(1)} %get-tuple-element.35), channel_id=1, source_target_pairs={{0,1},{1,0},{2,3},{3,2},{4,5},{5,4},{6,7},{7,6},{8,9},{9,8},{10,11... | collective-permute-start | bytes 798728 | tf_op jit(solution)/shard_map/ppermute | solution.py:390
  15.3 8.2 %collective-permute-start.5 = (bf16[1040,128]{1,0:T(8,128)(2,1)S(1)}, bf16[1040,128]{1,0:T(8,128)(2,1)S(1)}, u32[]{:S(2)}, u32[]{:S(2)}) collective-permute-start(bf16[1040,128]{1,0:T(8,128)(2,1)S(1)} %get-tuple-element.36), channel_id=1, source_target_pairs={{0,2},{1,3},{2,0},{3,1},{4,6},{5,7},{6,4},{7,5},{8,10},{9,11},{10,... | collective-permute-start | bytes 798728 | tf_op jit(solution)/shard_map/ppermute | solution.py:390
  17.0 10.6 %copy-start = (bf16[128,32,128]{2,1,0:T(8,128)(2,1)S(1)}, bf16[128,32,128]{2,1,0:T(8,128)(2,1)}, u32[]{:S(2)}) copy-start(bf16[128,32,128]{2,1,0:T(8,128)(2,1)} %refs_2_.7) | copy-start | bytes 3145732
  18.2 17.1 %collective-permute-start.6 = (bf16[3,528,128]{2,1,0:T(8,128)(2,1)S(1)}, bf16[3,528,128]{2,1,0:T(8,128)(2,1)S(1)}, u32[]{:S(2)}, u32[]{:S(2)}) collective-permute-start(bf16[3,528,128]{2,1,0:T(8,128)(2,1)S(1)} %get-tuple-element.39), channel_id=1, source_target_pairs={{0,1},{1,0},{2,3},{3,2},{4,5},{5,4},{6,7},{7,6},{8,9},{9,8},{10,11... | collective-permute-start | bytes 1216520 | tf_op jit(solution)/shard_map/ppermute | solution.py:390
  18.6 21.8 %collective-permute-start.7 = (bf16[3,528,128]{2,1,0:T(8,128)(2,1)S(1)}, bf16[3,528,128]{2,1,0:T(8,128)(2,1)S(1)}, u32[]{:S(2)}, u32[]{:S(2)}) collective-permute-start(bf16[3,528,128]{2,1,0:T(8,128)(2,1)S(1)} %get-tuple-element.40), channel_id=1, source_target_pairs={{0,2},{1,3},{2,0},{3,1},{4,6},{5,7},{6,4},{7,5},{8,10},{9,11},{10,... | collective-permute-start | bytes 1216520 | tf_op jit(solution)/shard_map/ppermute | solution.py:390
  24.5 9.1 %collective-permute-start.9 = (bf16[1040,128]{1,0:T(8,128)(2,1)S(1)}, bf16[1040,128]{1,0:T(8,128)(2,1)S(1)}, u32[]{:S(2)}, u32[]{:S(2)}) collective-permute-start(bf16[1040,128]{1,0:T(8,128)(2,1)S(1)} %ending.1.refs_4_), channel_id=1, source_target_pairs={{0,8},{1,9},{2,10},{3,11},{4,12},{5,13},{6,14},{7,15},{8,16},{9,17... | collective-permute-start | bytes 798728 | tf_op jit(solution)/shard_map/ppermute | solution.py:400
  25.8 7.8 %collective-permute-start.8 = (bf16[1040,128]{1,0:T(8,128)(2,1)S(1)}, bf16[1040,128]{1,0:T(8,128)(2,1)S(1)}, u32[]{:S(2)}, u32[]{:S(2)}) collective-permute-start(bf16[1040,128]{1,0:T(8,128)(2,1)S(1)} %ending.1.refs_4_), channel_id=1, source_target_pairs={{0,4},{1,5},{2,6},{3,7},{4,8},{5,9},{6,10},{7,11},{8,12},{9,13},{1... | collective-permute-start | bytes 798728 | tf_op jit(solution)/shard_map/ppermute | solution.py:400
  27.3 19.5 %collective-permute-start.10 = (bf16[3,528,128]{2,1,0:T(8,128)(2,1)S(1)}, bf16[3,528,128]{2,1,0:T(8,128)(2,1)S(1)}, u32[]{:S(2)}, u32[]{:S(2)}) collective-permute-start(bf16[3,528,128]{2,1,0:T(8,128)(2,1)S(1)} %get-tuple-element.44), channel_id=1, source_target_pairs={{0,3},{1,2},{2,1},{3,0},{4,7},{5,6},{6,5},{7,4},{8,11},{9,10},{10,... | collective-permute-start | bytes 1216520 | tf_op jit(solution)/shard_map/ppermute | solution.py:390
  34.8 21.3 %collective-permute-start.11 = (bf16[1040,128]{1,0:T(8,128)(2,1)S(1)}, bf16[1040,128]{1,0:T(8,128)(2,1)S(1)}, u32[]{:S(2)}, u32[]{:S(2)}) collective-permute-start(bf16[1040,128]{1,0:T(8,128)(2,1)S(1)} %get-tuple-element.46), channel_id=1, source_target_pairs={{0,1},{1,0},{2,3},{3,2},{4,5},{5,4},{6,7},{7,6},{8,9},{9,8},{10,11... | collective-permute-start | bytes 798728 | tf_op jit(solution)/shard_map/ppermute | solution.py:390
  35.1 21.0 %collective-permute-start.12 = (bf16[1040,128]{1,0:T(8,128)(2,1)S(1)}, bf16[1040,128]{1,0:T(8,128)(2,1)S(1)}, u32[]{:S(2)}, u32[]{:S(2)}) collective-permute-start(bf16[1040,128]{1,0:T(8,128)(2,1)S(1)} %get-tuple-element.47), channel_id=1, source_target_pairs={{0,2},{1,3},{2,0},{3,1},{4,6},{5,7},{6,4},{7,5},{8,10},{9,11},{10,... | collective-permute-start | bytes 798728 | tf_op jit(solution)/shard_map/ppermute | solution.py:390
  35.3 20.7 %collective-permute-start.13 = (bf16[1040,128]{1,0:T(8,128)(2,1)S(1)}, bf16[1040,128]{1,0:T(8,128)(2,1)S(1)}, u32[]{:S(2)}, u32[]{:S(2)}) collective-permute-start(bf16[1040,128]{1,0:T(8,128)(2,1)S(1)} %get-tuple-element.48), channel_id=1, source_target_pairs={{0,3},{1,2},{2,1},{3,0},{4,7},{5,6},{6,5},{7,4},{8,11},{9,10},{10,... | collective-permute-start | bytes 798728 | tf_op jit(solution)/shard_map/ppermute | solution.py:390
  46.9 9.2 %copy-start.4 = (f32[32,128]{1,0:T(8,128)S(1)}, f32[32,128]{1,0:T(8,128)}, u32[]{:S(2)}) copy-start(f32[32,128]{1,0:T(8,128)} %refs_3_.3) | copy-start | bytes 49156
  53.5 5.9 %collective-permute-start.14 = (bf16[128,16,128]{2,1,0:T(8,128)(2,1)S(1)}, bf16[128,16,128]{2,1,0:T(8,128)(2,1)S(1)}, u32[]{:S(2)}, u32[]{:S(2)}) collective-permute-start(bf16[128,16,128]{2,1,0:T(8,128)(2,1)S(1)} %get-tuple-element.50), channel_id=1, source_target_pairs={{0,4},{1,5},{2,6},{3,7},{4,0},{5,1},{6,2},{7,3},{8,12},{9,13},{10,... | collective-permute-start | bytes 1572872 | tf_op jit(solution)/shard_map/ppermute | solution.py:390

commit v4 on v3

v4 whole, which is shorter than its diff:
```python
import functools
import math

import jax
import jax.numpy as jnp
from jax import lax
from jax.experimental import pallas as pl
from jax.experimental.pallas import tpu as pltpu
from jax.sharding import PartitionSpec as P

LOOK = 2
NEG_FILL = -1e30
NORM_EPS = 1e-06
TAIL = 16
F32 = jnp.float32
BF16 = jnp.bfloat16
AXES = ("ctx", "head")
VMEM = pl.BlockSpec(memory_space=pltpu.VMEM)
SMEM = pl.BlockSpec(memory_space=pltpu.SMEM)
ANY = pl.BlockSpec(memory_space=pl.ANY)
HBM = pl.BlockSpec(memory_space=pltpu.HBM)


def call(kernel, name, micros, limit_mib, ins, outs, out_specs, scratch=(), aliases=None, after=()):
    count = len(ins)

    def run(*refs):
        kernel(*refs[:count], *refs[count + len(after) :])

    made = pl.pallas_call(
        run,
        out_shape=outs,
        in_specs=list(ins) + [ANY] * len(after),
        out_specs=out_specs,
        scratch_shapes=list(scratch),
        input_output_aliases=aliases or {},
        compiler_params=pltpu.CompilerParams(vmem_limit_bytes=int(limit_mib * 1024 * 1024)),
        cost_estimate=pl.CostEstimate(flops=int(micros * 1e9), bytes_accessed=0, transcendentals=0),
        name=name,
    )
    return lambda *args: made(*args, *after)


def column(row):
    size = row.shape[1]
    return jnp.transpose(jnp.broadcast_to(row, (size, size)))


def dot(left, right, contract):
    return lax.dot_general(left, right, (contract, ((), ())), preferred_element_type=F32)


def odd(place):
    for shift in (8, 4, 2, 1):
        place = place ^ (place >> shift)
    return place & 1


def share_of(places, place):
    return odd(place) * (places // 2) + (place >> 1)


def split(value):
    high = value.astype(BF16)
    return high, (value - high.astype(F32)).astype(BF16)


def source_kernel(places, at_ref, rate_hbm, sid_hbm, key_hbm, value_hbm, soft_key_hbm, soft_value_hbm, soft_query_hbm, *rest):
    outs, rest = rest[:places], rest[places:]
    keys_by_head, values_by_head, pair_ref, give_ref, rate_ref, sid_ref, key_in, value_in, soft_key_in, soft_value_in, stage, sems = rest
    heads, tokens, width = keys_by_head.shape
    per, half = heads // places, heads // LOOK
    kv_heads = soft_key_in.shape[1]
    kv_half = kv_heads // LOOK
    span = 2 * kv_half * tokens
    rows = span + TAIL
    core, place = at_ref[0], at_ref[1]
    mine = pl.multiple_of(core * span, TAIL)
    theirs = pl.ds(pl.multiple_of((LOOK - 1 - core) * half, half), half)
    moves = (
        (soft_key_hbm, soft_key_in),
        (soft_value_hbm, soft_value_in),
        (sid_hbm, sid_ref),
        (rate_hbm, rate_ref),
        (key_hbm, key_in),
        (value_hbm, value_in),
        (soft_query_hbm.at[:, theirs, :], give_ref.at[pl.ds(rows // half, tokens)]),
    )
    copies = [pltpu.make_async_copy(src, dst, sems.at[n]) for n, (src, dst) in enumerate(moves)]
    for copy in copies:
        copy.start()
    for at, ref in enumerate((soft_key_in, soft_value_in)):
        copies[at].wait()
        stage[...] = jnp.swapaxes(ref[...], 0, 1)
        for j in range(kv_half):
            start = (at * kv_half + j) * tokens
            pair_ref[pl.ds(mine + start, tokens), :] = stage[core * kv_half + j]
            block = stage[(LOOK - 1 - core) * kv_half + j]
            give_ref[pl.ds(start // half, tokens // half)] = block.reshape(tokens // half, half, width)
    copies[2].wait()
    sid_row = (sid_ref[...] + 1).astype(F32)
    tail = jnp.broadcast_to(sid_row, (TAIL, tokens)).astype(BF16)
    pair_ref[pl.ds(LOOK * span, TAIL), :] = tail
    give_ref[pl.ds(2 * kv_half * tokens // half, TAIL // half)] = tail.reshape(TAIL // half, half, tokens)
    open_row = (sid_row == jnp.max(sid_row, axis=1, keepdims=True)).astype(F32)
    behind = (tokens - 1 - lax.broadcasted_iota(jnp.int32, (1, tokens), 1)).astype(F32)
    copies[3].wait()
    copies[4].wait()
    keys_by_head[...] = jnp.swapaxes(key_in[...], 0, 1)
    copies[5].wait()
    values_by_head[...] = jnp.swapaxes(value_in[...], 0, 1)
    for k in range(places):
        for j in range(per):
            head = share_of(places, place ^ k) * per + j
            values = values_by_head[head]
            weighted = jnp.transpose(keys_by_head[head].astype(F32)) * (open_row * jnp.exp(-rate_ref[head] * behind))
            high, low = split(weighted)
            state = dot(jnp.concatenate([high, low], 1), jnp.concatenate([values, values], 0), ((1,), (0,)))
            outs[k][pl.ds(j * width, width), :] = state.astype(BF16)
        outs[k][pl.ds(per * width, TAIL), :] = tail
        outs[k][pl.ds(per * width + TAIL, TAIL), :] = tail
    copies[6].wait()


def pair_kernel(at_ref, got_ref, _, pair_ref):
    heads = got_ref.shape[1]
    width = pair_ref.shape[1]
    span = (pair_ref.shape[0] - TAIL) // LOOK
    other = 1 - at_ref[0]
    pair_ref[pl.ds(pl.multiple_of(other * span, TAIL), span), :] = got_ref[pl.ds(0, span // heads)].reshape(span, width)
    theirs = got_ref[pl.ds(span // heads, TAIL // heads)].reshape(TAIL, width)
    row_at = lax.broadcasted_iota(jnp.int32, (TAIL, width), 0)
    mine = pair_ref[pl.ds(LOOK * span, TAIL), :].astype(F32)
    tail = jnp.where(row_at // (TAIL // LOOK) == other, theirs.astype(F32), mine)
    pair_ref[pl.ds(LOOK * span, TAIL), :] = tail.astype(BF16)


def mix_kernel(places, at_ref, pair_ref, before_ref, *rest):
    home_ref, outs = rest[-places], rest[1 - places :]
    width = pair_ref.shape[1]
    span = (pair_ref.shape[0] - TAIL) // LOOK
    place = at_ref[1]
    for back, ref in enumerate((pair_ref, before_ref)):
        tails = ref[pl.ds(LOOK * span, TAIL), :].astype(F32)
        for block in range(LOOK):
            slot = LOOK * block + back
            home_ref[slot, pl.ds(0, span), :] = ref[pl.ds(block * span, span), :]
            row = block * (TAIL // LOOK)
            home_ref[slot, pl.ds(span, TAIL), :] = jnp.broadcast_to(tails[row : row + 1], (TAIL, width)).astype(BF16)
    for k in range(1, places):
        out = outs[k - 1]
        later = ((place ^ k) > place).astype(jnp.int32)
        out[0] = home_ref[0]
        out[1] = home_ref[3]
        out[2] = home_ref[1 + later]


def gather_slots(places, at_ref, pays, slots):
    for k in range(places):
        slots[at_ref[1] ^ k] = pays[k][pl.ds(0, slots.shape[1]), :]


def last_of(pay, per, width):
    return jnp.max(pay[pl.ds(per * width, TAIL), :].astype(F32), axis=(0, 1), keepdims=True)


def advance(pay, per, width, span, rates, state, last):
    now = last_of(pay, per, width)
    same = (now == last).astype(F32)
    state = [
        pay[pl.ds(j * width, width), :].astype(F32) + (same * jnp.exp(jnp.full((1, width), -rates[j] * span, F32))) * state[j]
        for j in range(per)
    ]
    return state, now


def store_state(ref, state, last):
    width = ref.shape[1]
    for j, value in enumerate(state):
        ref[pl.ds(j * width, width), :] = value.astype(BF16)
    ref[pl.ds(len(state) * width, TAIL), :] = jnp.broadcast_to(last, (TAIL, width)).astype(BF16)


def ending_kernel(places, tokens, at_ref, rate_ref, *rest):
    pays, out_ref, slots = rest[:places], rest[places], rest[places + 1]
    width = out_ref.shape[1]
    per = (out_ref.shape[0] - TAIL) // width
    gather_slots(places, at_ref, pays, slots)
    rates = [rate_ref[share_of(places, at_ref[1]) * per + j] for j in range(per)]
    state = [jnp.zeros((width, width), F32)] * per
    last = jnp.zeros((1, 1), F32)
    for block in range(places):
        state, last = advance(slots.at[block], per, width, tokens, rates, state, last)
    store_state(out_ref, state, last)


def prefix_kernel(places, tokens, at_ref, rate_ref, *rest):
    ahead, pays, outs = rest[:LOOK], rest[LOOK : LOOK + places], rest[LOOK + places : LOOK + 2 * places]
    slots, results = rest[LOOK + 2 * places :]
    width = ahead[0].shape[1]
    per = (ahead[0].shape[0] - TAIL) // width
    gather_slots(places, at_ref, pays, slots)
    rates = [rate_ref[share_of(places, at_ref[1]) * per + j] for j in range(per)]
    state = [ahead[-1][pl.ds(j * width, width), :].astype(F32) for j in range(per)]
    last = last_of(ahead[-1], per, width)
    for group in reversed(ahead[:-1]):
        state, last = advance(group, per, width, places * tokens, rates, state, last)
    for block in range(places):
        store_state(results.at[block], state, last)
        if block < places - 1:
            state, last = advance(slots.at[block], per, width, tokens, rates, state, last)
    for k in range(places):
        outs[k][...] = results[at_ref[1] ^ k]


def prep_kernel(rate_ref, sid_ref, query_ref, keys_by_head, left_ref):
    heads, tokens, _ = keys_by_head.shape
    sid_row = (sid_ref[...] + 1).astype(F32)
    row_at = lax.broadcasted_iota(jnp.int32, (tokens, tokens), 0)
    lane = lax.broadcasted_iota(jnp.int32, (tokens, tokens), 1)
    allowed = ((row_at >= lane) & (column(sid_row) == sid_row)).astype(F32)
    ahead = (lax.broadcasted_iota(jnp.int32, (1, tokens), 1) + 1).astype(F32)
    left_ref[:, :, tokens:] = jnp.swapaxes(query_ref[...], 0, 1)
    for head in range(heads):
        weights = dot(left_ref[head, :, tokens:], keys_by_head[head], ((1,), (1,)))
        weights = weights * allowed * jnp.exp(rate_ref[head] * ahead)
        left_ref[head, :, :tokens] = weights.astype(BF16)


class Light:
    def __init__(self, places, at_ref, rate_ref, sid_ref, gain_ref, left_ref, values_by_head, pay):
        self.rate_ref, self.gain_ref, self.left_ref, self.values_by_head = rate_ref, gain_ref, left_ref, values_by_head
        heads, self.tokens, self.width = values_by_head.shape
        self.places, self.place, self.core = places, at_ref[1], at_ref[0]
        self.half, self.per = heads // LOOK, heads // places
        sid_column = column((sid_ref[...] + 1).astype(F32))
        self.continues = (sid_column == last_of(pay, self.per, self.width)).astype(BF16)
        self.ahead = (lax.broadcasted_iota(jnp.int32, (self.tokens, 1), 0) + 1).astype(F32)

    def columns(self, which):
        return pl.ds(pl.multiple_of(which * self.half, self.half), self.half)

    def half_out(self, ks, pays, light_hbm, by_head, stage, sem):
        which = odd(self.place ^ ks[0])
        for k, pay in zip(ks, pays):
            for j in range(self.per):
                head = share_of(self.places, self.place ^ k) * self.per + j
                tokens = self.tokens
                left = jnp.concatenate([self.left_ref[head, :, :tokens], self.left_ref[head, :, tokens:] * self.continues], 1)
                right = jnp.concatenate([self.values_by_head[head], pay[pl.ds(j * self.width, self.width), :]], 0)
                raw = dot(left, right, ((1,), (0,)))
                lead = jnp.exp(-self.rate_ref[head] * self.ahead)
                mean_square = jnp.mean(raw * raw, axis=1, keepdims=True) * (lead * lead)
                out = raw * (lead * lax.rsqrt(mean_square + NORM_EPS)) * self.gain_ref[pl.ds(head, 1), :]
                by_head[head - which * self.half] = out.astype(BF16)
        stage[...] = jnp.swapaxes(by_head[...], 0, 1)
        copy = pltpu.make_async_copy(stage, light_hbm.at[:, self.columns(which), :], sem)
        copy.start()
        return copy


def first_kernel(places, ks, at_ref, rate_ref, sid_ref, gain_ref, left_ref, values_by_head, keep_ref, _, *rest):
    pays, (light_hbm, soft_hbm, _, by_head, stage, sems) = rest[: len(ks)], rest[len(ks) :]
    light = Light(places, at_ref, rate_ref, sid_ref, gain_ref, left_ref, values_by_head, pays[0])
    copy = pltpu.make_async_copy(keep_ref, soft_hbm.at[:, light.columns(light.core), :], sems.at[0])
    copy.start()
    light.half_out(ks, pays, light_hbm, by_head, stage, sems.at[1]).wait()
    copy.wait()


def second_kernel(places, ks, at_ref, rate_ref, sid_ref, gain_ref, left_ref, values_by_head, _, *rest):
    pays, (light_hbm, done_ref, by_head, stage, sems) = rest[: len(ks)], rest[len(ks) :]
    done_ref[...] = jnp.zeros_like(done_ref)
    light = Light(places, at_ref, rate_ref, sid_ref, gain_ref, left_ref, values_by_head, pays[0])
    light.half_out(ks, pays, light_hbm, by_head, stage, sems.at[0]).wait()


def beside_kernel(at_ref, got_ref, _, out_hbm, sems):
    tokens, half, _ = got_ref.shape
    columns = pl.ds(pl.multiple_of((LOOK - 1 - at_ref[0]) * half, half), half)
    size = tokens // sems.shape[0]
    copies = []
    for n in range(sems.shape[0]):
        rows = pl.ds(n * size, size)
        copies.append(pltpu.make_async_copy(got_ref.at[rows], out_hbm.at[rows, columns, :], sems.at[n]))
        copies[-1].start()
    for copy in copies:
        copy.wait()


class Soft:
    def __init__(self, places, at_ref, query_ref, got_ref, home_ref, share, codes):
        self.core, self.place = at_ref[0], at_ref[1]
        self.tokens, _, self.width = query_ref.shape
        self.share, self.heads, self.rows = share, got_ref.shape[1], home_ref.shape[1]
        self.kv_heads = self.heads // share
        self.query_ref, self.got_ref, self.codes = query_ref, got_ref, codes
        self.lane = lax.broadcasted_iota(jnp.int32, (self.tokens, self.tokens), 1)
        self.factor = self.width ** (-0.5) * math.log2(math.e)

    def spread(self, value):
        tokens, share = self.tokens, self.share
        value = jnp.broadcast_to(value.reshape(tokens, 1, tokens), (tokens, share, tokens))
        return value.reshape(tokens * share, tokens)

    def marked(self, pick):
        ref, slot = pick
        sids = ref[slot, pl.ds(2 * self.kv_heads * self.tokens, TAIL), :].astype(F32)[0:1, :]
        return column(sids) == self.lane.astype(F32)

    def far(self, block, ks, pays):
        picks = []
        for k, pay in zip(ks, pays):
            later = ((self.place ^ k) > self.place).astype(jnp.int32)
            picks.append((pay, 2 * later * (1 - block)))
            picks.append((pay, 1 + (1 - later) * block))
        return picks

    def code(self, own, picks):
        for at, pick in enumerate(picks):
            self.codes[own, pl.ds(at * self.tokens, self.tokens), :] = self.marked(pick).astype(BF16)

    def query(self, own, g):
        tokens, share = self.tokens, self.share
        if own:
            first = pl.multiple_of(self.core * self.heads, self.heads)
            wide = self.query_ref[:, pl.ds(first, self.heads), :]
        else:
            wide = self.got_ref[pl.ds(self.rows // self.heads, tokens)]
        wide = wide.astype(F32)[:, g * share : (g + 1) * share, :]
        return wide.reshape(tokens * share, self.width).astype(BF16)

    def scores(self, own, g, marks, picks):
        tokens = self.tokens
        query = jnp.concatenate([self.query(own, g), marks], 1)
        keys = jnp.concatenate([ref[slot, pl.ds(g * tokens, tokens), :] for ref, slot in picks], 0)
        codes = self.codes[own, pl.ds(0, len(picks) * tokens), :]
        return dot(query, jnp.concatenate([keys, codes], 1), ((1,), (1,)))

    def probs(self, scores, peak):
        wide = jnp.concatenate([peak] * (scores.shape[1] // self.width), 1)
        return jnp.exp2((scores - wide) * self.factor).astype(BF16)

    def mixed(self, g, probs, picks):
        tokens = self.tokens
        rows = pl.ds((self.kv_heads + g) * tokens, tokens)
        values = jnp.concatenate([ref[slot, rows, :] for ref, slot in picks], 0)
        return dot(probs, jnp.concatenate([values, jnp.ones_like(values)], 1), ((1,), (0,)))

    def top(self, scores):
        return jnp.broadcast_to(jnp.max(scores, axis=1, keepdims=True), (scores.shape[0], self.width))

    def added(self, own, g, marks, picks, sums, before):
        scores = self.scores(own, g, marks, picks)
        peak = jnp.maximum(before, self.top(scores))
        scale = jnp.exp2((before - peak) * self.factor)
        out = self.mixed(g, self.probs(scores, peak), picks) + sums * jnp.concatenate([scale, scale], 1)
        return out, peak


def home_kernel(places, share, at_ref, got_ref, query_ref, home_ref, sums_ref, peaks_ref, marks_ref, codes, fills):
    soft = Soft(places, at_ref, query_ref, got_ref, home_ref, share, codes)
    row_at = lax.broadcasted_iota(jnp.int32, soft.lane.shape, 0)
    fills[...] = soft.spread(jnp.where(row_at >= soft.lane, 0.0, NEG_FILL))
    for own in range(LOOK):
        block = soft.core if own else 1 - soft.core
        mine = (home_ref, 2 * block)
        picks = [(home_ref, 1 - block), (home_ref, 3), mine]
        soft.code(own, picks)
        marks_ref[own] = soft.spread(jnp.where(soft.marked(mine), 0.0, NEG_FILL)).astype(BF16)
        last = (len(picks) - 1) * soft.tokens
        for g in range(soft.kv_heads):
            scores = soft.scores(own, g, marks_ref[own], picks)
            scores = jnp.concatenate([scores[:, :last], scores[:, last:] + fills[...]], 1)
            peak = soft.top(scores)
            at = own * soft.kv_heads + g
            sums_ref[at] = soft.mixed(g, soft.probs(scores, peak), picks)
            peaks_ref[at] = peak


def away_kernel(places, share, at_ref, got_ref, query_ref, home_ref, sums_ref, peaks_ref, marks_ref, *rest):
    pays, outs, codes = rest[: places - 1], rest[places - 1 : places + 1], rest[places + 1]
    soft = Soft(places, at_ref, query_ref, got_ref, home_ref, share, codes)
    for own in range(LOOK):
        picks = soft.far(soft.core if own else 1 - soft.core, range(1, places), pays)
        soft.code(own, picks)
        mixed = []
        for g in range(soft.kv_heads):
            at = own * soft.kv_heads + g
            out, _ = soft.added(own, g, marks_ref[own], picks, sums_ref[at], peaks_ref[at])
            mixed.append((out[:, : soft.width] / out[:, soft.width :]).reshape(soft.tokens, share, soft.width))
        outs[own][...] = jnp.concatenate(mixed, 1).astype(BF16)


def body(
    light_query,
    light_keys,
    light_values,
    decay_rate,
    norm_gain,
    soft_query,
    soft_keys,
    soft_values,
    segment_ids,
):
    places = lax.axis_size("head")
    n_all = lax.axis_size("ctx") * places
    members = LOOK * places
    core = lax.rem(lax.axis_index("ctx"), LOOK)
    place = lax.axis_index("head")
    at = jnp.stack([core, place, core * places + place]).astype(jnp.int32)
    tokens, heads, width = light_query.shape
    kv_heads = soft_keys.shape[1]
    per, half, kv_half = heads // places, heads // LOOK, kv_heads // LOOK
    sid_row = segment_ids.reshape(1, tokens)
    even, uneven = [k for k in range(places) if not odd(k)], [k for k in range(places) if odd(k)]

    def partner(value, k):
        pairs = [(i, i - i % members + ((i % members) ^ k)) for i in range(n_all)]
        return lax.ppermute(value, AXES, pairs)

    def across(value):
        return partner(value, places)

    def to_places(values):
        return [values[0]] + [partner(values[k], k) for k in range(1, places)]

    def onward(value, groups):
        step = groups * places
        return lax.ppermute(value, AXES, [(i, i + step) for i in range(n_all - step)])

    def shape(*dims):
        return jax.ShapeDtypeStruct(dims, BF16)

    def room(*dims, dtype=BF16):
        return pltpu.VMEM(dims, dtype)

    def semaphores(count):
        return pltpu.SemaphoreType.DMA((count,))

    pay = shape(2 * kv_half * tokens + TAIL, width)
    pair = shape(LOOK * (pay.shape[0] - TAIL) + TAIL, width)
    given = shape(pay.shape[0] // half + tokens, half, width)
    state = shape(per * width + TAIL, width)
    by_head = shape(heads, tokens, width)
    half_out = shape(tokens, half, width)
    slots = room(places, *state.shape)
    sid_room = room(1, tokens, dtype=jnp.int32)

    def held(value):
        return pltpu.with_memory_space_constraint(value, pltpu.HBM)

    made = call(
        functools.partial(source_kernel, places), "source", 0, 16, [SMEM] + [HBM] * 7,
        [shape(state.shape[0] + TAIL, width)] * places + [by_head] * 2 + [pair, given], [VMEM] * (places + 4),
        [pltpu.SMEM((heads,), F32), sid_room] + [room(tokens, heads, width)] * 2 + [room(tokens, kv_heads, width)] * 2
        + [room(kv_heads, tokens, width), semaphores(7)],
    )(at, *[held(x) for x in (decay_rate, sid_row, light_keys, light_values, soft_keys, soft_values, soft_query)])
    keys_by_head, values_by_head, own, give = made[places:]
    states = to_places(made[:places])
    got = across(give)
    own = call(pair_kernel, "pair", 0, 8, [SMEM, VMEM, VMEM], pair, VMEM, aliases={2: 0})(at, got, own)
    before = onward(own, LOOK)

    left = call(
        prep_kernel, "prep", 0, 16, [SMEM, VMEM, VMEM, VMEM], shape(heads, tokens, tokens + width), VMEM
    )(decay_rate, sid_row, light_query, keys_by_head)
    mixed = call(
        functools.partial(mix_kernel, places), "mix", 0, 8, [SMEM] + [VMEM] * 2,
        [shape(4, *pay.shape)] + [shape(3, *pay.shape)] * (places - 1), [VMEM] * places, after=[left, *[states[k] for k in even[1:]]],
    )(at, own, before)
    home = mixed[0]
    parcels = to_places(mixed)

    ending = call(
        functools.partial(ending_kernel, places, tokens), "ending", 0, 8, [SMEM] * 2 + [VMEM] * places, state, VMEM,
        [slots], after=[home],
    )(at, decay_rate, *states)
    ahead = [onward(ending, groups) for groups in range(1, LOOK + 1)]
    share = half // kv_half
    queries = tokens * share

    def codes(blocks):
        return room(LOOK, blocks * tokens, width)

    def limit(blocks):
        return (blocks * tokens * queries * 14 + 8 * half_out.size) / 2**20 + 8

    sums_like = [
        jax.ShapeDtypeStruct((LOOK * kv_half, queries, 2 * width), F32),
        jax.ShapeDtypeStruct((LOOK * kv_half, queries, width), F32),
    ]
    sums, peaks, marks = call(
        functools.partial(home_kernel, places, share), "home", 0, limit(3), [SMEM] + [VMEM] * 3,
        sums_like + [shape(LOOK, queries, tokens)], [VMEM] * 3, [codes(3), room(queries, tokens, dtype=F32)], after=[ending],
    )(at, got, soft_query, home)
    prefixed = call(
        functools.partial(prefix_kernel, places, tokens), "prefix", 0, 12, [SMEM] * 2 + [VMEM] * (places + LOOK),
        [state] * places, [VMEM] * places, [slots, slots], after=[sums],
    )(at, decay_rate, *ahead, *states)
    entries = to_places(prefixed)

    blocks = 2 * (places - 1)
    soft_theirs, soft_kept = call(
        functools.partial(away_kernel, places, share), "away", 30, limit(blocks), [SMEM] + [VMEM] * (5 + places),
        [half_out] * 2, [VMEM] * 2, [codes(blocks)], after=[prefixed[0]],
    )(at, got, soft_query, home, sums, peaks, marks, *parcels[1:])

    whole = shape(tokens, heads, width)
    known = (at, decay_rate, sid_row, norm_gain, left, values_by_head)
    rooms = [room(half, tokens, width), room(tokens, half, width)]
    light_out, soft_out, soft_theirs = call(
        functools.partial(first_kernel, places, even), "first", 0, 16, [SMEM] * 2 + [VMEM] * 5 + [ANY] + [VMEM] * len(even),
        [whole, whole, half_out], [HBM, HBM, ANY], rooms + [semaphores(2)], aliases={7: 2},
    )(*known, soft_kept, soft_theirs, *[entries[k] for k in even])
    soft_got = across(soft_theirs)
    light_out, done = call(
        functools.partial(second_kernel, places, uneven), "second", 15, 16, [SMEM] * 2 + [VMEM] * 4 + [HBM] + [VMEM] * len(uneven),
        [whole, shape(TAIL, width)], [HBM, VMEM], rooms + [semaphores(1)], aliases={6: 0},
    )(*known, light_out, *[entries[k] for k in uneven])
    soft_out = call(
        beside_kernel, "beside", 0, 8, [SMEM, VMEM, HBM], whole, HBM, [semaphores(math.gcd(tokens, 4))], aliases={2: 0}, after=[done]
    )(at, soft_got, soft_out)
    return (light_out, soft_out)


def solution(mesh):
    placed = P(("ctx", "head"), None, None)
    return jax.shard_map(
        body,
        mesh=mesh,
        in_specs=(placed, placed, placed, P(), P(), placed, placed, placed, P(("ctx", "head"))),
        out_specs=(placed, placed),
        check_vma=False,
    )
```

time: 61.1 us -> 57.4 us (0.939)
  the two profiles are of different devices: /device:TPU:25 before, /device:TPU:0 now
where the time goes in v4:
time: 57.4 us; the launch traced here: 57.2 us
  Pallas kernels  24 us (42%)
  starting transfers between devices  23.9 us (42%)
  waiting for transfers between devices  8.24 us (14%)
  between operations  0.95 us (2%)
    pallas_call x11, Pallas kernels, call(): return lambda *args: made(*args, *after)  24 us
    ppermute x11, starting transfers between devices, partner(): return lax.ppermute(value, AXES, pairs)  13.9 us
    ppermute x3, starting transfers between devices, onward(): lax.ppermute(value, AXES, [(i, i + step) for i in range(n_all - step)])  10 us
    ppermute x3, waiting for transfers between devices, onward(): lax.ppermute(value, AXES, [(i, i + step) for i in range(n_all - step)])  4.65 us
    ppermute x11, waiting for transfers between devices, partner(): return lax.ppermute(value, AXES, pairs)  3.6 us
  transfers between devices with their start and end apart: 14, of which 5 were waited for; matrix products, arithmetic and copies ran while one was open for 0% of the time, Pallas kernels for 33%

profile of v4, /device:TPU:0, one launch (start us, length us, event | category | flops | bytes accessed | tf_op | source)
XLA Modules:
  0.0 57.2 jit_solution(13659881357246502921)
XLA Ops:
  0.7 3.6 %source.1 = (bf16[1056,128]{1,0:T(8,128)(2,1)S(1)}, bf16[1056,128]{1,0:T(8,128)(2,1)S(1)}, bf16[1056,128]{1,0:T(8,128)(2,1)S(1)}, bf16[1056,128]{1,0:T(8,128)(2,...) custom-call(s32[3]{0:T(128)S(1)} %pad_add_fusion.refs_0_, ...), custom_call_target="tpu_custom_call" | custom-call | tf_op jit(solution)/shard_map/source/pallas_call | solution.py:41
  4.8 3.5 %collective-permute-start.2 = (bf16[1056,128]{1,0:T(8,128)(2,1)S(1)}, bf16[1056,128]{1,0:T(8,128)(2,1)S(1)}, u32[]{:S(2)}, u32[]{:S(2)}) collective-permute-start(bf16[1056,128]{1,0:T(8,128)(2,1)S(1)} %get-tuple-element.32), channel_id=1, source_target_pairs={{0,3},{1,2},{2,1},{3,0},{4,7},{5,6},{6,5},{7,4},{8,11},{9,10},{10,... | collective-permute-start | bytes 811016 | tf_op jit(solution)/shard_map/ppermute | solution.py:420
  8.9 3.5 %collective-permute-start.1 = (bf16[1040,128]{1,0:T(8,128)(2,1)S(1)}, bf16[1040,128]{1,0:T(8,128)(2,1)S(1)}, u32[]{:S(2)}, u32[]{:S(2)}) collective-permute-start(bf16[1040,128]{1,0:T(8,128)(2,1)S(1)} %pair.1.refs_1_), channel_id=1, source_target_pairs={{0,8},{1,9},{2,10},{3,11},{4,12},{5,13},{6,14},{7,15},{8,16},{9,17... | collective-permute-start | bytes 798728 | tf_op jit(solution)/shard_map/ppermute | solution.py:430
  12.4 1.1 %collective-permute-start.3 = (bf16[1056,128]{1,0:T(8,128)(2,1)S(1)}, bf16[1056,128]{1,0:T(8,128)(2,1)S(1)}, u32[]{:S(2)}, u32[]{:S(2)}) collective-permute-start(bf16[1056,128]{1,0:T(8,128)(2,1)S(1)} %get-tuple-element.35), channel_id=1, source_target_pairs={{0,1},{1,0},{2,3},{3,2},{4,5},{5,4},{6,7},{7,6},{8,9},{9,8},{10,11... | collective-permute-start | bytes 811016 | tf_op jit(solution)/shard_map/ppermute | solution.py:420
  13.6 1.5 %collective-permute-start.4 = (bf16[1056,128]{1,0:T(8,128)(2,1)S(1)}, bf16[1056,128]{1,0:T(8,128)(2,1)S(1)}, u32[]{:S(2)}, u32[]{:S(2)}) collective-permute-start(bf16[1056,128]{1,0:T(8,128)(2,1)S(1)} %get-tuple-element.36), channel_id=1, source_target_pairs={{0,2},{1,3},{2,0},{3,1},{4,6},{5,7},{6,4},{7,5},{8,10},{9,11},{10,... | collective-permute-start | bytes 811016 | tf_op jit(solution)/shard_map/ppermute | solution.py:420
  15.1 1.4 %prep.1.refs_3_.refs_4_ = bf16[32,128,256]{2,1,0:T(8,128)(2,1)S(1)} custom-call(f32[32]{0:T(128)S(1)} %copy-done.3, s32[1,128]{1,0:T(1,128)S(1)} %bitcast.5, bf16[128,32,128]{2,1,0:T(8,128)(2,1)S(1)} %copy-done.1, bf16[32,128,128]{2,1,0:T(8,128)(2,1)S(1)} %get-tuple-element.28.refs_3_), custom_call_target="tpu_custom_call" | custom-call | tf_op jit(solution)/shard_map/prep/pallas_call | solution.py:41
  16.6 1.8 %collective-permute-done.1.refs_2_ = bf16[1040,128]{1,0:T(8,128)(2,1)S(1)} collective-permute-done((bf16[1040,128]{1,0:T(8,128)(2,1)S(1)}, bf16[1040,128]{1,0:T(8,128)(2,1)S(1)}, u32[]{:S(2)}, u32[]{:S(2)}) %collective-permute-start.1) | collective-permute-done | bytes 266272 | tf_op jit(solution)/shard_map/ppermute | solution.py:430
  19.1 1.1 %collective-permute-start.5 = (bf16[3,528,128]{2,1,0:T(8,128)(2,1)S(1)}, bf16[3,528,128]{2,1,0:T(8,128)(2,1)S(1)}, u32[]{:S(2)}, u32[]{:S(2)}) collective-permute-start(bf16[3,528,128]{2,1,0:T(8,128)(2,1)S(1)} %get-tuple-element.40), channel_id=1, source_target_pairs={{0,1},{1,0},{2,3},{3,2},{4,5},{5,4},{6,7},{7,6},{8,9},{9,8},{10,11... | collective-permute-start | bytes 1216520 | tf_op jit(solution)/shard_map/ppermute | solution.py:420
  20.2 1.5 %collective-permute-start.6 = (bf16[3,528,128]{2,1,0:T(8,128)(2,1)S(1)}, bf16[3,528,128]{2,1,0:T(8,128)(2,1)S(1)}, u32[]{:S(2)}, u32[]{:S(2)}) collective-permute-start(bf16[3,528,128]{2,1,0:T(8,128)(2,1)S(1)} %get-tuple-element.41), channel_id=1, source_target_pairs={{0,2},{1,3},{2,0},{3,1},{4,6},{5,7},{6,4},{7,5},{8,10},{9,11},{10,... | collective-permute-start | bytes 1216520 | tf_op jit(solution)/shard_map/ppermute | solution.py:420
  21.7 0.9 %collective-permute-start.7 = (bf16[3,528,128]{2,1,0:T(8,128)(2,1)S(1)}, bf16[3,528,128]{2,1,0:T(8,128)(2,1)S(1)}, u32[]{:S(2)}, u32[]{:S(2)}) collective-permute-start(bf16[3,528,128]{2,1,0:T(8,128)(2,1)S(1)} %get-tuple-element.42), channel_id=1, source_target_pairs={{0,3},{1,2},{2,1},{3,0},{4,7},{5,6},{6,5},{7,4},{8,11},{9,10},{10,... | collective-permute-start | bytes 1216520 | tf_op jit(solution)/shard_map/ppermute | solution.py:420
  22.6 1.0 %ending.1.refs_4_ = bf16[1040,128]{1,0:T(8,128)(2,1)S(1)} custom-call(s32[3]{0:T(128)S(1)} %pad_add_fusion.refs_0_, f32[32]{0:T(128)S(1)} %copy-done.3, bf16[1056,128]{1,0:T(8,128)(2,1)S(1)} %get-tuple-element.34.refs_2_.refs_4_, bf16[1056,128]{1,0:T(8,128)(2,1)S(1)} %collective-permute-done.3.refs_3_.refs_5_, ...), custom_call_target="tpu_custom_call" | custom-call | tf_op jit(solution)/shard_map/ending/pallas_call | solution.py:41
  23.6 1.3 %collective-permute-start.8 = (bf16[1040,128]{1,0:T(8,128)(2,1)S(1)}, bf16[1040,128]{1,0:T(8,128)(2,1)S(1)}, u32[]{:S(2)}, u32[]{:S(2)}) collective-permute-start(bf16[1040,128]{1,0:T(8,128)(2,1)S(1)} %ending.1.refs_4_), channel_id=1, source_target_pairs={{0,4},{1,5},{2,6},{3,7},{4,8},{5,9},{6,10},{7,11},{8,12},{9,13},{1... | collective-permute-start | bytes 798728 | tf_op jit(solution)/shard_map/ppermute | solution.py:430
  24.9 5.2 %collective-permute-start.9 = (bf16[1040,128]{1,0:T(8,128)(2,1)S(1)}, bf16[1040,128]{1,0:T(8,128)(2,1)S(1)}, u32[]{:S(2)}, u32[]{:S(2)}) collective-permute-start(bf16[1040,128]{1,0:T(8,128)(2,1)S(1)} %ending.1.refs_4_), channel_id=1, source_target_pairs={{0,8},{1,9},{2,10},{3,11},{4,12},{5,13},{6,14},{7,15},{8,16},{9,17... | collective-permute-start | bytes 798728 | tf_op jit(solution)/shard_map/ppermute | solution.py:430
  30.2 3.8 %home.1 = (f32[4,1024,256]{2,1,0:T(8,128)S(1)}, f32[4,1024,128]{2,1,0:T(8,128)S(1)}, bf16[2,1024,128]{2,1,0:T(8,128)(2,1)S(1)}) custom-call(s32[3]{0:T(128)S(1)} %pad_add_fusion.refs_0_, bf16[161,16,128]{2,1,0:T(8,128)(2,1)S(1)} %collective-permute-done.refs_1_, bf16[128,32,128]{2,1,0:T(8,128)(2,1)S(1)} %copy-done, ...), custom_call_target="tpu_custom_call" | custom-call | tf_op jit(solution)/shard_map/home/pallas_call | solution.py:41
  33.9 2.8 %collective-permute-done.9.refs_3_ = bf16[1040,128]{1,0:T(8,128)(2,1)S(1)} collective-permute-done((bf16[1040,128]{1,0:T(8,128)(2,1)S(1)}, bf16[1040,128]{1,0:T(8,128)(2,1)S(1)}, u32[]{:S(2)}, u32[]{:S(2)}) %collective-permute-start.9) | collective-permute-done | bytes 266272 | tf_op jit(solution)/shard_map/ppermute | solution.py:430
  36.8 1.1 %prefix.1 = (bf16[1040,128]{1,0:T(8,128)(2,1)S(1)}, bf16[1040,128]{1,0:T(8,128)(2,1)S(1)}, bf16[1040,128]{1,0:T(8,128)(2,1)S(1)}, bf16[1040,128]{1,0:T(8,128)(2,1)S(1)}) custom-call(s32[3]{0:T(128)S(1)} %pad_add_fusion.refs_0_, f32[32]{0:T(128)S(1)} %copy-done.3, bf16[1040,128]{1,0:T(8,128)(2,1)S(1)} %collective-permute-done.8.refs_2_, ...), custom_call_target="tpu_custom_call" | custom-call | tf_op jit(solution)/shard_map/prefix/pallas_call | solution.py:41
  37.9 2.1 %collective-permute-start.10 = (bf16[1040,128]{1,0:T(8,128)(2,1)S(1)}, bf16[1040,128]{1,0:T(8,128)(2,1)S(1)}, u32[]{:S(2)}, u32[]{:S(2)}) collective-permute-start(bf16[1040,128]{1,0:T(8,128)(2,1)S(1)} %get-tuple-element.46), channel_id=1, source_target_pairs={{0,3},{1,2},{2,1},{3,0},{4,7},{5,6},{6,5},{7,4},{8,11},{9,10},{10,... | collective-permute-start | bytes 798728 | tf_op jit(solution)/shard_map/ppermute | solution.py:420
  40.5 1.0 %collective-permute-start.12 = (bf16[1040,128]{1,0:T(8,128)(2,1)S(1)}, bf16[1040,128]{1,0:T(8,128)(2,1)S(1)}, u32[]{:S(2)}, u32[]{:S(2)}) collective-permute-start(bf16[1040,128]{1,0:T(8,128)(2,1)S(1)} %get-tuple-element.49), channel_id=1, source_target_pairs={{0,2},{1,3},{2,0},{3,1},{4,6},{5,7},{6,4},{7,5},{8,10},{9,11},{10,... | collective-permute-start | bytes 798728 | tf_op jit(solution)/shard_map/ppermute | solution.py:420
  41.4 5.8 %away.1 = (bf16[128,16,128]{2,1,0:T(8,128)(2,1)S(1)}, bf16[128,16,128]{2,1,0:T(8,128)(2,1)S(1)}) custom-call(s32[3]{0:T(128)S(1)} %pad_add_fusion.refs_0_, bf16[161,16,128]{2,1,0:T(8,128)(2,1)S(1)} %collective-permute-done.refs_1_, bf16[128,32,128]{2,1,0:T(8,128)(2,1)S(1)} %copy-done, bf16[4,528,128]{2,1,0:T(8,128)(2,1)S(1)} %get-tuple-element.33.refs_6_.refs_3_, ...), custom_call_target="tpu_custom_call" | custom-call | flops 30000001024 | tf_op jit(solution)/shard_map/away/pallas_call | solution.py:41
  47.3 0.8 %collective-permute-done.10.refs_9_ = bf16[1040,128]{1,0:T(8,128)(2,1)S(1)} collective-permute-done((bf16[1040,128]{1,0:T(8,128)(2,1)S(1)}, bf16[1040,128]{1,0:T(8,128)(2,1)S(1)}, u32[]{:S(2)}, u32[]{:S(2)}) %collective-permute-start.10) | collective-permute-done | bytes 266272 | tf_op jit(solution)/shard_map/ppermute | solution.py:420
  48.1 2.4 %first.1 = (bf16[128,32,128]{2,1,0:T(8,128)(2,1)}, bf16[128,32,128]{2,1,0:T(8,128)(2,1)}, bf16[128,16,128]{2,1,0:T(8,128)(2,1)S(1)}) custom-call(s32[3]{0:T(128)S(1)} %pad_add_fusion.refs_0_, f32[32]{0:T(128)S(1)} %copy-done.3, s32[1,128]{1,0:T(1,128)S(1)} %bitcast.6, f32[32,128]{1,0:T(8,128)S(1)} %copy-done.2, ...), custom_call_target="tpu_custom_call", output_to_operand_aliasing={{2}: (7, {})} | custom-call | tf_op jit(solution)/shard_map/first/pallas_call | solution.py:41
  50.5 2.4 %collective-permute-done.11.refs_7_ = bf16[1040,128]{1,0:T(8,128)(2,1)S(1)} collective-permute-done((bf16[1040,128]{1,0:T(8,128)(2,1)S(1)}, bf16[1040,128]{1,0:T(8,128)(2,1)S(1)}, u32[]{:S(2)}, u32[]{:S(2)}) %collective-permute-start.11) | collective-permute-done | bytes 266272 | tf_op jit(solution)/shard_map/ppermute | solution.py:420
  53.3 2.3 %second.1 = (bf16[128,32,128]{2,1,0:T(8,128)(2,1)}, bf16[16,128]{1,0:T(8,128)(2,1)S(1)}) custom-call(s32[3]{0:T(128)S(1)} %pad_add_fusion.refs_0_, f32[32]{0:T(128)S(1)} %copy-done.3, s32[1,128]{1,0:T(1,128)S(1)} %bitcast.7, f32[32,128]{1,0:T(8,128)S(1)} %copy-done.2, ...), custom_call_target="tpu_custom_call", output_to_operand_aliasing={{0}: (6, {})} | custom-call | flops 15000000512 | tf_op jit(solution)/shard_map/second/pallas_call | solution.py:41
  55.6 1.4 %beside.1 = bf16[128,32,128]{2,1,0:T(8,128)(2,1)} custom-call(s32[3]{0:T(128)S(1)} %pad_add_fusion.refs_0_, bf16[128,16,128]{2,1,0:T(8,128)(2,1)S(1)} %collective-permute-done.13.refs_1_, bf16[128,32,128]{2,1,0:T(8,128)(2,1)} %get-tuple-element.52.refs_2_, bf16[16,128]{1,0:T(8,128)(2,1)S(1)} %get-tuple-element.53.refs_3_), custom_call_target="tpu_custom_call", output_to_operand_aliasing={{}: (2, {})} | custom-call | tf_op jit(solution)/shard_map/beside/pallas_call | solution.py:41
  (26 shorter events, 2.8 us)
Async XLA Ops:
  0.7 14.4 %copy-start.1 = (bf16[128,32,128]{2,1,0:T(8,128)(2,1)S(1)}, bf16[128,32,128]{2,1,0:T(8,128)(2,1)}, u32[]{:S(2)}) copy-start(bf16[128,32,128]{2,1,0:T(8,128)(2,1)} %refs_2_.3) | copy-start | bytes 3145732
  0.7 14.4 %copy-start.3 = (f32[32]{0:T(128)S(1)}, f32[32]{0:T(128)}, u32[]{:S(2)}) copy-start(f32[32]{0:T(128)} %refs_1_.9) | copy-start | bytes 388
  0.7 14.4 %copy-start.4 = (s32[128]{0:T(128)S(1)}, s32[128]{0:T(128)}, u32[]{:S(2)}) copy-start(s32[128]{0:T(128)} %param.17) | copy-start | bytes 1540
  4.3 4.0 %collective-permute-start = (bf16[161,16,128]{2,1,0:T(8,128)(2,1)S(1)}, bf16[161,16,128]{2,1,0:T(8,128)(2,1)S(1)}, u32[]{:S(2)}, u32[]{:S(2)}) collective-permute-start(bf16[161,16,128]{2,1,0:T(8,128)(2,1)S(1)} %get-tuple-element.30), channel_id=1, source_target_pairs={{0,4},{1,5},{2,6},{3,7},{4,0},{5,1},{6,2},{7,3},{8,12},{9,13},{10,... | collective-permute-start | bytes 1978376 | tf_op jit(solution)/shard_map/ppermute | solution.py:420
  4.8 11.7 %collective-permute-start.2 = (bf16[1056,128]{1,0:T(8,128)(2,1)S(1)}, bf16[1056,128]{1,0:T(8,128)(2,1)S(1)}, u32[]{:S(2)}, u32[]{:S(2)}) collective-permute-start(bf16[1056,128]{1,0:T(8,128)(2,1)S(1)} %get-tuple-element.32), channel_id=1, source_target_pairs={{0,3},{1,2},{2,1},{3,0},{4,7},{5,6},{6,5},{7,4},{8,11},{9,10},{10,... | collective-permute-start | bytes 811016 | tf_op jit(solution)/shard_map/ppermute | solution.py:420
  8.9 9.5 %collective-permute-start.1 = (bf16[1040,128]{1,0:T(8,128)(2,1)S(1)}, bf16[1040,128]{1,0:T(8,128)(2,1)S(1)}, u32[]{:S(2)}, u32[]{:S(2)}) collective-permute-start(bf16[1040,128]{1,0:T(8,128)(2,1)S(1)} %pair.1.refs_1_), channel_id=1, source_target_pairs={{0,8},{1,9},{2,10},{3,11},{4,12},{5,13},{6,14},{7,15},{8,16},{9,17... | collective-permute-start | bytes 798728 | tf_op jit(solution)/shard_map/ppermute | solution.py:430
  12.4 10.2 %collective-permute-start.3 = (bf16[1056,128]{1,0:T(8,128)(2,1)S(1)}, bf16[1056,128]{1,0:T(8,128)(2,1)S(1)}, u32[]{:S(2)}, u32[]{:S(2)}) collective-permute-start(bf16[1056,128]{1,0:T(8,128)(2,1)S(1)} %get-tuple-element.35), channel_id=1, source_target_pairs={{0,1},{1,0},{2,3},{3,2},{4,5},{5,4},{6,7},{7,6},{8,9},{9,8},{10,11... | collective-permute-start | bytes 811016 | tf_op jit(solution)/shard_map/ppermute | solution.py:420
  13.6 9.1 %collective-permute-start.4 = (bf16[1056,128]{1,0:T(8,128)(2,1)S(1)}, bf16[1056,128]{1,0:T(8,128)(2,1)S(1)}, u32[]{:S(2)}, u32[]{:S(2)}) collective-permute-start(bf16[1056,128]{1,0:T(8,128)(2,1)S(1)} %get-tuple-element.36), channel_id=1, source_target_pairs={{0,2},{1,3},{2,0},{3,1},{4,6},{5,7},{6,4},{7,5},{8,10},{9,11},{10,... | collective-permute-start | bytes 811016 | tf_op jit(solution)/shard_map/ppermute | solution.py:420
  16.5 13.6 %copy-start = (bf16[128,32,128]{2,1,0:T(8,128)(2,1)S(1)}, bf16[128,32,128]{2,1,0:T(8,128)(2,1)}, u32[]{:S(2)}) copy-start(bf16[128,32,128]{2,1,0:T(8,128)(2,1)} %refs_2_.5) | copy-start | bytes 3145732
  19.1 21.4 %collective-permute-start.5 = (bf16[3,528,128]{2,1,0:T(8,128)(2,1)S(1)}, bf16[3,528,128]{2,1,0:T(8,128)(2,1)S(1)}, u32[]{:S(2)}, u32[]{:S(2)}) collective-permute-start(bf16[3,528,128]{2,1,0:T(8,128)(2,1)S(1)} %get-tuple-element.40), channel_id=1, source_target_pairs={{0,1},{1,0},{2,3},{3,2},{4,5},{5,4},{6,7},{7,6},{8,9},{9,8},{10,11... | collective-permute-start | bytes 1216520 | tf_op jit(solution)/shard_map/ppermute | solution.py:420
  20.2 21.2 %collective-permute-start.6 = (bf16[3,528,128]{2,1,0:T(8,128)(2,1)S(1)}, bf16[3,528,128]{2,1,0:T(8,128)(2,1)S(1)}, u32[]{:S(2)}, u32[]{:S(2)}) collective-permute-start(bf16[3,528,128]{2,1,0:T(8,128)(2,1)S(1)} %get-tuple-element.41), channel_id=1, source_target_pairs={{0,2},{1,3},{2,0},{3,1},{4,6},{5,7},{6,4},{7,5},{8,10},{9,11},{10,... | collective-permute-start | bytes 1216520 | tf_op jit(solution)/shard_map/ppermute | solution.py:420
  21.7 19.7 %collective-permute-start.7 = (bf16[3,528,128]{2,1,0:T(8,128)(2,1)S(1)}, bf16[3,528,128]{2,1,0:T(8,128)(2,1)S(1)}, u32[]{:S(2)}, u32[]{:S(2)}) collective-permute-start(bf16[3,528,128]{2,1,0:T(8,128)(2,1)S(1)} %get-tuple-element.42), channel_id=1, source_target_pairs={{0,3},{1,2},{2,1},{3,0},{4,7},{5,6},{6,5},{7,4},{8,11},{9,10},{10,... | collective-permute-start | bytes 1216520 | tf_op jit(solution)/shard_map/ppermute | solution.py:420
  23.6 10.3 %collective-permute-start.8 = (bf16[1040,128]{1,0:T(8,128)(2,1)S(1)}, bf16[1040,128]{1,0:T(8,128)(2,1)S(1)}, u32[]{:S(2)}, u32[]{:S(2)}) collective-permute-start(bf16[1040,128]{1,0:T(8,128)(2,1)S(1)} %ending.1.refs_4_), channel_id=1, source_target_pairs={{0,4},{1,5},{2,6},{3,7},{4,8},{5,9},{6,10},{7,11},{8,12},{9,13},{1... | collective-permute-start | bytes 798728 | tf_op jit(solution)/shard_map/ppermute | solution.py:430
  24.9 11.8 %collective-permute-start.9 = (bf16[1040,128]{1,0:T(8,128)(2,1)S(1)}, bf16[1040,128]{1,0:T(8,128)(2,1)S(1)}, u32[]{:S(2)}, u32[]{:S(2)}) collective-permute-start(bf16[1040,128]{1,0:T(8,128)(2,1)S(1)} %ending.1.refs_4_), channel_id=1, source_target_pairs={{0,8},{1,9},{2,10},{3,11},{4,12},{5,13},{6,14},{7,15},{8,16},{9,17... | collective-permute-start | bytes 798728 | tf_op jit(solution)/shard_map/ppermute | solution.py:430
  37.9 10.2 %collective-permute-start.10 = (bf16[1040,128]{1,0:T(8,128)(2,1)S(1)}, bf16[1040,128]{1,0:T(8,128)(2,1)S(1)}, u32[]{:S(2)}, u32[]{:S(2)}) collective-permute-start(bf16[1040,128]{1,0:T(8,128)(2,1)S(1)} %get-tuple-element.46), channel_id=1, source_target_pairs={{0,3},{1,2},{2,1},{3,0},{4,7},{5,6},{6,5},{7,4},{8,11},{9,10},{10,... | collective-permute-start | bytes 798728 | tf_op jit(solution)/shard_map/ppermute | solution.py:420
  39.9 13.0 %collective-permute-start.11 = (bf16[1040,128]{1,0:T(8,128)(2,1)S(1)}, bf16[1040,128]{1,0:T(8,128)(2,1)S(1)}, u32[]{:S(2)}, u32[]{:S(2)}) collective-permute-start(bf16[1040,128]{1,0:T(8,128)(2,1)S(1)} %get-tuple-element.48), channel_id=1, source_target_pairs={{0,1},{1,0},{2,3},{3,2},{4,5},{5,4},{6,7},{7,6},{8,9},{9,8},{10,11... | collective-permute-start | bytes 798728 | tf_op jit(solution)/shard_map/ppermute | solution.py:420
  40.5 12.8 %collective-permute-start.12 = (bf16[1040,128]{1,0:T(8,128)(2,1)S(1)}, bf16[1040,128]{1,0:T(8,128)(2,1)S(1)}, u32[]{:S(2)}, u32[]{:S(2)}) collective-permute-start(bf16[1040,128]{1,0:T(8,128)(2,1)S(1)} %get-tuple-element.49), channel_id=1, source_target_pairs={{0,2},{1,3},{2,0},{3,1},{4,6},{5,7},{6,4},{7,5},{8,10},{9,11},{10,... | collective-permute-start | bytes 798728 | tf_op jit(solution)/shard_map/ppermute | solution.py:420
  41.4 6.6 %copy-start.2 = (f32[32,128]{1,0:T(8,128)S(1)}, f32[32,128]{1,0:T(8,128)}, u32[]{:S(2)}) copy-start(f32[32,128]{1,0:T(8,128)} %refs_3_.5) | copy-start | bytes 49156
  50.4 5.2 %collective-permute-start.13 = (bf16[128,16,128]{2,1,0:T(8,128)(2,1)S(1)}, bf16[128,16,128]{2,1,0:T(8,128)(2,1)S(1)}, u32[]{:S(2)}, u32[]{:S(2)}) collective-permute-start(bf16[128,16,128]{2,1,0:T(8,128)(2,1)S(1)} %get-tuple-element.51), channel_id=1, source_target_pairs={{0,4},{1,5},{2,6},{3,7},{4,0},{5,1},{6,2},{7,3},{8,12},{9,13},{10,... | collective-permute-start | bytes 1572872 | tf_op jit(solution)/shard_map/ppermute | solution.py:420

commit v5 on v4

--- a/solution.py
+++ b/solution.py
@@ -9,6 +9,8 @@
 from jax.sharding import PartitionSpec as P
 
 LOOK = 2
+PARTS = 2
+PIECES = 4
 NEG_FILL = -1e30
 NORM_EPS = 1e-06
 TAIL = 16
@@ -58,6 +60,20 @@
 
 def share_of(places, place):
     return odd(place) * (places // 2) + (place >> 1)
+
+
+def pieces(tokens):
+    return [pl.ds(n * (tokens // PIECES), tokens // PIECES) for n in range(PIECES)]
+
+
+def copy_out(stage, hbm, columns, sems):
+    copies = [
+        pltpu.make_async_copy(stage.at[piece], hbm.at[piece, columns, :], sems.at[n])
+        for n, piece in enumerate(pieces(stage.shape[0]))
+    ]
+    for copy in copies:
+        copy.start()
+    return copies
 
 
 def split(value):
@@ -82,8 +98,7 @@
         (soft_value_hbm, soft_value_in),
         (sid_hbm, sid_ref),
         (rate_hbm, rate_ref),
-        (key_hbm, key_in),
-        (value_hbm, value_in),
+        *[(hbm.at[piece], ref.at[piece]) for piece in pieces(tokens) for hbm, ref in ((key_hbm, key_in), (value_hbm, value_in))],
         (soft_query_hbm.at[:, theirs, :], give_ref.at[pl.ds(rows // half, tokens)]),
     )
     copies = [pltpu.make_async_copy(src, dst, sems.at[n]) for n, (src, dst) in enumerate(moves)]
@@ -105,10 +120,11 @@
     open_row = (sid_row == jnp.max(sid_row, axis=1, keepdims=True)).astype(F32)
     behind = (tokens - 1 - lax.broadcasted_iota(jnp.int32, (1, tokens), 1)).astype(F32)
     copies[3].wait()
-    copies[4].wait()
-    keys_by_head[...] = jnp.swapaxes(key_in[...], 0, 1)
-    copies[5].wait()
-    values_by_head[...] = jnp.swapaxes(value_in[...], 0, 1)
+    for n, piece in enumerate(pieces(tokens)):
+        copies[4 + 2 * n].wait()
+        keys_by_head[:, piece, :] = jnp.swapaxes(key_in[piece], 0, 1)
+        copies[5 + 2 * n].wait()
+        values_by_head[:, piece, :] = jnp.swapaxes(value_in[piece], 0, 1)
     for k in range(places):
         for j in range(per):
             head = share_of(places, place ^ k) * per + j
@@ -119,7 +135,7 @@
             outs[k][pl.ds(j * width, width), :] = state.astype(BF16)
         outs[k][pl.ds(per * width, TAIL), :] = tail
         outs[k][pl.ds(per * width + TAIL, TAIL), :] = tail
-    copies[6].wait()
+    copies[-1].wait()
 
 
 def pair_kernel(at_ref, got_ref, _, pair_ref):
@@ -178,20 +194,22 @@
     width = ref.shape[1]
     for j, value in enumerate(state):
         ref[pl.ds(j * width, width), :] = value.astype(BF16)
-    ref[pl.ds(len(state) * width, TAIL), :] = jnp.broadcast_to(last, (TAIL, width)).astype(BF16)
+    tail = ref.shape[0] - len(state) * width
+    ref[pl.ds(len(state) * width, tail), :] = jnp.broadcast_to(last, (tail, width)).astype(BF16)
 
 
 def ending_kernel(places, tokens, at_ref, rate_ref, *rest):
-    pays, out_ref, slots = rest[:places], rest[places], rest[places + 1]
-    width = out_ref.shape[1]
-    per = (out_ref.shape[0] - TAIL) // width
+    pays, outs, slots = rest[:places], rest[places : places + LOOK], rest[places + LOOK]
+    width = outs[0].shape[1]
+    per = (outs[0].shape[0] - TAIL) // width
     gather_slots(places, at_ref, pays, slots)
     rates = [rate_ref[share_of(places, at_ref[1]) * per + j] for j in range(per)]
     state = [jnp.zeros((width, width), F32)] * per
     last = jnp.zeros((1, 1), F32)
     for block in range(places):
         state, last = advance(slots.at[block], per, width, tokens, rates, state, last)
-    store_state(out_ref, state, last)
+    for out_ref in outs:
+        store_state(out_ref, state, last)
 
 
 def prefix_kernel(places, tokens, at_ref, rate_ref, *rest):
@@ -240,7 +258,7 @@
     def columns(self, which):
         return pl.ds(pl.multiple_of(which * self.half, self.half), self.half)
 
-    def half_out(self, ks, pays, light_hbm, by_head, stage, sem):
+    def half_out(self, ks, pays, light_hbm, by_head, stage, sems):
         which = odd(self.place ^ ks[0])
         for k, pay in zip(ks, pays):
             for j in range(self.per):
@@ -254,36 +272,31 @@
                 out = raw * (lead * lax.rsqrt(mean_square + NORM_EPS)) * self.gain_ref[pl.ds(head, 1), :]
                 by_head[head - which * self.half] = out.astype(BF16)
         stage[...] = jnp.swapaxes(by_head[...], 0, 1)
-        copy = pltpu.make_async_copy(stage, light_hbm.at[:, self.columns(which), :], sem)
-        copy.start()
-        return copy
-
-
-def first_kernel(places, ks, at_ref, rate_ref, sid_ref, gain_ref, left_ref, values_by_head, keep_ref, _, *rest):
-    pays, (light_hbm, soft_hbm, _, by_head, stage, sems) = rest[: len(ks)], rest[len(ks) :]
+        for copy in copy_out(stage, light_hbm, self.columns(which), sems):
+            copy.wait()
+
+
+def first_kernel(places, ks, at_ref, rate_ref, sid_ref, gain_ref, left_ref, values_by_head, keep_ref, *rest):
+    pays, rest = rest[PARTS : PARTS + len(ks)], rest[PARTS + len(ks) :]
+    light_hbm, soft_hbm, (by_head, stage, sems) = rest[0], rest[1], rest[2 + PARTS :]
     light = Light(places, at_ref, rate_ref, sid_ref, gain_ref, left_ref, values_by_head, pays[0])
     copy = pltpu.make_async_copy(keep_ref, soft_hbm.at[:, light.columns(light.core), :], sems.at[0])
     copy.start()
-    light.half_out(ks, pays, light_hbm, by_head, stage, sems.at[1]).wait()
+    light.half_out(ks, pays, light_hbm, by_head, stage, sems.at[pl.ds(1, PIECES)])
     copy.wait()
 
 
-def second_kernel(places, ks, at_ref, rate_ref, sid_ref, gain_ref, left_ref, values_by_head, _, *rest):
-    pays, (light_hbm, done_ref, by_head, stage, sems) = rest[: len(ks)], rest[len(ks) :]
-    done_ref[...] = jnp.zeros_like(done_ref)
+def second_kernel(places, ks, at_ref, rate_ref, sid_ref, gain_ref, left_ref, values_by_head, *rest):
+    got, rest = rest[:PARTS], rest[PARTS + 2 :]
+    pays, (light_hbm, soft_hbm, by_head, stage, sems) = rest[: len(ks)], rest[len(ks) :]
     light = Light(places, at_ref, rate_ref, sid_ref, gain_ref, left_ref, values_by_head, pays[0])
-    light.half_out(ks, pays, light_hbm, by_head, stage, sems.at[0]).wait()
-
-
-def beside_kernel(at_ref, got_ref, _, out_hbm, sems):
-    tokens, half, _ = got_ref.shape
-    columns = pl.ds(pl.multiple_of((LOOK - 1 - at_ref[0]) * half, half), half)
-    size = tokens // sems.shape[0]
+    size = light.tokens // PARTS
     copies = []
-    for n in range(sems.shape[0]):
-        rows = pl.ds(n * size, size)
-        copies.append(pltpu.make_async_copy(got_ref.at[rows], out_hbm.at[rows, columns, :], sems.at[n]))
+    for n in range(PARTS):
+        there = soft_hbm.at[pl.ds(n * size, size), light.columns(LOOK - 1 - light.core), :]
+        copies.append(pltpu.make_async_copy(got[n], there, sems.at[PIECES + n]))
         copies[-1].start()
+    light.half_out(ks, pays, light_hbm, by_head, stage, sems)
     for copy in copies:
         copy.wait()
 
@@ -379,7 +392,8 @@
 
 
 def away_kernel(places, share, at_ref, got_ref, query_ref, home_ref, sums_ref, peaks_ref, marks_ref, *rest):
-    pays, outs, codes = rest[: places - 1], rest[places - 1 : places + 1], rest[places + 1]
+    pays, rest = rest[: places - 1], rest[places - 1 :]
+    given, kept, codes = rest[:PARTS], rest[PARTS], rest[PARTS + 1]
     soft = Soft(places, at_ref, query_ref, got_ref, home_ref, share, codes)
     for own in range(LOOK):
         picks = soft.far(soft.core if own else 1 - soft.core, range(1, places), pays)
@@ -389,7 +403,13 @@
             at = own * soft.kv_heads + g
             out, _ = soft.added(own, g, marks_ref[own], picks, sums_ref[at], peaks_ref[at])
             mixed.append((out[:, : soft.width] / out[:, soft.width :]).reshape(soft.tokens, share, soft.width))
-        outs[own][...] = jnp.concatenate(mixed, 1).astype(BF16)
+        mixed = jnp.concatenate(mixed, 1).astype(BF16)
+        if own:
+            kept[...] = mixed
+        else:
+            size = soft.tokens // PARTS
+            for n in range(PARTS):
+                given[n][...] = mixed[n * size : (n + 1) * size]
 
 
 def body(
@@ -454,7 +474,7 @@
         functools.partial(source_kernel, places), "source", 0, 16, [SMEM] + [HBM] * 7,
         [shape(state.shape[0] + TAIL, width)] * places + [by_head] * 2 + [pair, given], [VMEM] * (places + 4),
         [pltpu.SMEM((heads,), F32), sid_room] + [room(tokens, heads, width)] * 2 + [room(tokens, kv_heads, width)] * 2
-        + [room(kv_heads, tokens, width), semaphores(7)],
+        + [room(kv_heads, tokens, width), semaphores(5 + 2 * PIECES)],
     )(at, *[held(x) for x in (decay_rate, sid_row, light_keys, light_values, soft_keys, soft_values, soft_query)])
     keys_by_head, values_by_head, own, give = made[places:]
     states = to_places(made[:places])
@@ -473,10 +493,10 @@
     parcels = to_places(mixed)
 
     ending = call(
-        functools.partial(ending_kernel, places, tokens), "ending", 0, 8, [SMEM] * 2 + [VMEM] * places, state, VMEM,
-        [slots], after=[home],
+        functools.partial(ending_kernel, places, tokens), "ending", 0, 8, [SMEM] * 2 + [VMEM] * places,
+        [state] * LOOK, [VMEM] * LOOK, [slots], after=[home],
     )(at, decay_rate, *states)
-    ahead = [onward(ending, groups) for groups in range(1, LOOK + 1)]
+    ahead = [onward(ending[n], n + 1) for n in range(LOOK)]
     share = half // kv_half
     queries = tokens * share
 
@@ -492,7 +512,7 @@
     ]
     sums, peaks, marks = call(
         functools.partial(home_kernel, places, share), "home", 0, limit(3), [SMEM] + [VMEM] * 3,
-        sums_like + [shape(LOOK, queries, tokens)], [VMEM] * 3, [codes(3), room(queries, tokens, dtype=F32)], after=[ending],
+        sums_like + [shape(LOOK, queries, tokens)], [VMEM] * 3, [codes(3), room(queries, tokens, dtype=F32)], after=[ending[0]],
     )(at, got, soft_query, home)
     prefixed = call(
         functools.partial(prefix_kernel, places, tokens), "prefix", 0, 12, [SMEM] * 2 + [VMEM] * (places + LOOK),
@@ -501,27 +521,29 @@
     entries = to_places(prefixed)
 
     blocks = 2 * (places - 1)
-    soft_theirs, soft_kept = call(
+    part_out = shape(tokens // PARTS, half, width)
+    made = call(
         functools.partial(away_kernel, places, share), "away", 30, limit(blocks), [SMEM] + [VMEM] * (5 + places),
-        [half_out] * 2, [VMEM] * 2, [codes(blocks)], after=[prefixed[0]],
+        [part_out] * PARTS + [half_out], [VMEM] * (PARTS + 1), [codes(blocks)], after=[prefixed[0]],
     )(at, got, soft_query, home, sums, peaks, marks, *parcels[1:])
+    soft_theirs, soft_kept = made[:PARTS], made[PARTS]
 
     whole = shape(tokens, heads, width)
     known = (at, decay_rate, sid_row, norm_gain, left, values_by_head)
     rooms = [room(half, tokens, width), room(tokens, half, width)]
-    light_out, soft_out, soft_theirs = call(
-        functools.partial(first_kernel, places, even), "first", 0, 16, [SMEM] * 2 + [VMEM] * 5 + [ANY] + [VMEM] * len(even),
-        [whole, whole, half_out], [HBM, HBM, ANY], rooms + [semaphores(2)], aliases={7: 2},
-    )(*known, soft_kept, soft_theirs, *[entries[k] for k in even])
-    soft_got = across(soft_theirs)
-    light_out, done = call(
-        functools.partial(second_kernel, places, uneven), "second", 15, 16, [SMEM] * 2 + [VMEM] * 4 + [HBM] + [VMEM] * len(uneven),
-        [whole, shape(TAIL, width)], [HBM, VMEM], rooms + [semaphores(1)], aliases={6: 0},
-    )(*known, light_out, *[entries[k] for k in uneven])
-    soft_out = call(
-        beside_kernel, "beside", 0, 8, [SMEM, VMEM, HBM], whole, HBM, [semaphores(math.gcd(tokens, 4))], aliases={2: 0}, after=[done]
-    )(at, soft_got, soft_out)
-    return (light_out, soft_out)
+    made = call(
+        functools.partial(first_kernel, places, even), "first", 0, 16,
+        [SMEM] * 2 + [VMEM] * 5 + [ANY] * PARTS + [VMEM] * len(even), [whole, whole] + [part_out] * PARTS, [HBM, HBM] + [ANY] * PARTS,
+        rooms + [semaphores(1 + PIECES)], aliases={7 + n: 2 + n for n in range(PARTS)},
+    )(*known, soft_kept, *soft_theirs, *[entries[k] for k in even])
+    soft_got = [across(x) for x in made[2:]]
+    return tuple(
+        call(
+            functools.partial(second_kernel, places, uneven), "second", 15, 16,
+            [SMEM] * 2 + [VMEM] * (4 + PARTS) + [HBM] * 2 + [VMEM] * len(uneven), [whole, whole], [HBM, HBM],
+            rooms + [semaphores(PIECES + PARTS)], aliases={6 + PARTS: 0, 7 + PARTS: 1},
+        )(*known, *soft_got, made[0], made[1], *[entries[k] for k in uneven])
+    )
 
 
 def solution(mesh):

time: 57.4 us -> 55.8 us (0.972)
  Pallas kernels: 24 us -> 22.5 us
    pallas_call x11 -> x10, Pallas kernels: 24 us -> 22.5 us  [call(): return lambda *args: made(*args, *after)]
    ppermute x11 -> x12, waiting for transfers between devices: 3.6 us -> 3.09 us  [partner(): return lax.ppermute(value, AXES, pairs)]
    ppermute x11 -> x12, starting transfers between devices: 13.9 us -> 14.4 us  [partner(): return lax.ppermute(value, AXES, pairs)]
  transfers between devices with their start and end apart: 14 -> 15, of which waited for: 5 -> 5; matrix products, arithmetic and copies ran while one was open for 0% -> 0% of each run, Pallas kernels for 33% -> 30%
where the time goes in v5:
time: 55.8 us; the launch traced here: 55.6 us
  starting transfers between devices  24.4 us (44%)
  Pallas kernels  22.5 us (40%)
  waiting for transfers between devices  7.73 us (14%)
  between operations  0.93 us (2%)
    pallas_call x10, Pallas kernels, call(): return lambda *args: made(*args, *after)  22.5 us
    ppermute x12, starting transfers between devices, partner(): return lax.ppermute(value, AXES, pairs)  14.4 us
    ppermute x3, starting transfers between devices, onward(): lax.ppermute(value, AXES, [(i, i + step) for i in range(n_all - step)])  10 us
    ppermute x3, waiting for transfers between devices, onward(): lax.ppermute(value, AXES, [(i, i + step) for i in range(n_all - step)])  4.65 us
    ppermute x12, waiting for transfers between devices, partner(): return lax.ppermute(value, AXES, pairs)  3.09 us
  transfers between devices with their start and end apart: 15, of which 5 were waited for; matrix products, arithmetic and copies ran while one was open for 0% of the time, Pallas kernels for 30%

profile of v5, /device:TPU:0, one launch (start us, length us, event | category | flops | bytes accessed | tf_op | source)
XLA Modules:
  0.0 55.6 jit_solution(10534215710210916763)
XLA Ops:
  0.7 3.4 %source.1 = (bf16[1056,128]{1,0:T(8,128)(2,1)S(1)}, bf16[1056,128]{1,0:T(8,128)(2,1)S(1)}, bf16[1056,128]{1,0:T(8,128)(2,1)S(1)}, bf16[1056,128]{1,0:T(8,128)(2,...) custom-call(s32[3]{0:T(128)S(1)} %pad_add_fusion.refs_0_, ...), custom_call_target="tpu_custom_call" | custom-call | tf_op jit(solution)/shard_map/source/pallas_call | solution.py:43
  4.6 3.5 %collective-permute-start.2 = (bf16[1056,128]{1,0:T(8,128)(2,1)S(1)}, bf16[1056,128]{1,0:T(8,128)(2,1)S(1)}, u32[]{:S(2)}, u32[]{:S(2)}) collective-permute-start(bf16[1056,128]{1,0:T(8,128)(2,1)S(1)} %get-tuple-element.34), channel_id=1, source_target_pairs={{0,3},{1,2},{2,1},{3,0},{4,7},{5,6},{6,5},{7,4},{8,11},{9,10},{10,... | collective-permute-start | bytes 811016 | tf_op jit(solution)/shard_map/ppermute | solution.py:440
  8.7 3.5 %collective-permute-start.1 = (bf16[1040,128]{1,0:T(8,128)(2,1)S(1)}, bf16[1040,128]{1,0:T(8,128)(2,1)S(1)}, u32[]{:S(2)}, u32[]{:S(2)}) collective-permute-start(bf16[1040,128]{1,0:T(8,128)(2,1)S(1)} %pair.1.refs_1_), channel_id=1, source_target_pairs={{0,8},{1,9},{2,10},{3,11},{4,12},{5,13},{6,14},{7,15},{8,16},{9,17... | collective-permute-start | bytes 798728 | tf_op jit(solution)/shard_map/ppermute | solution.py:450
  12.2 1.1 %collective-permute-start.3 = (bf16[1056,128]{1,0:T(8,128)(2,1)S(1)}, bf16[1056,128]{1,0:T(8,128)(2,1)S(1)}, u32[]{:S(2)}, u32[]{:S(2)}) collective-permute-start(bf16[1056,128]{1,0:T(8,128)(2,1)S(1)} %get-tuple-element.37), channel_id=1, source_target_pairs={{0,1},{1,0},{2,3},{3,2},{4,5},{5,4},{6,7},{7,6},{8,9},{9,8},{10,11... | collective-permute-start | bytes 811016 | tf_op jit(solution)/shard_map/ppermute | solution.py:440
  13.3 1.5 %collective-permute-start.4 = (bf16[1056,128]{1,0:T(8,128)(2,1)S(1)}, bf16[1056,128]{1,0:T(8,128)(2,1)S(1)}, u32[]{:S(2)}, u32[]{:S(2)}) collective-permute-start(bf16[1056,128]{1,0:T(8,128)(2,1)S(1)} %get-tuple-element.38), channel_id=1, source_target_pairs={{0,2},{1,3},{2,0},{3,1},{4,6},{5,7},{6,4},{7,5},{8,10},{9,11},{10,... | collective-permute-start | bytes 811016 | tf_op jit(solution)/shard_map/ppermute | solution.py:440
  14.9 1.4 %prep.1.refs_3_.refs_4_ = bf16[32,128,256]{2,1,0:T(8,128)(2,1)S(1)} custom-call(f32[32]{0:T(128)S(1)} %copy-done.3, s32[1,128]{1,0:T(1,128)S(1)} %bitcast.5, bf16[128,32,128]{2,1,0:T(8,128)(2,1)S(1)} %copy-done.1, bf16[32,128,128]{2,1,0:T(8,128)(2,1)S(1)} %get-tuple-element.30.refs_3_), custom_call_target="tpu_custom_call" | custom-call | tf_op jit(solution)/shard_map/prep/pallas_call | solution.py:43
  16.3 1.8 %collective-permute-done.1.refs_2_ = bf16[1040,128]{1,0:T(8,128)(2,1)S(1)} collective-permute-done((bf16[1040,128]{1,0:T(8,128)(2,1)S(1)}, bf16[1040,128]{1,0:T(8,128)(2,1)S(1)}, u32[]{:S(2)}, u32[]{:S(2)}) %collective-permute-start.1) | collective-permute-done | bytes 266272 | tf_op jit(solution)/shard_map/ppermute | solution.py:450
  18.1 0.7 %mix.1 = (bf16[4,528,128]{2,1,0:T(8,128)(2,1)S(1)}, bf16[3,528,128]{2,1,0:T(8,128)(2,1)S(1)}, bf16[3,528,128]{2,1,0:T(8,128)(2,1)S(1)}, bf16[3,528,128]{2,1,0:T(8,128)(2,1)S(1)}) custom-call(s32[3]{0:T(128)S(1)} %pad_add_fusion.refs_0_, bf16[1040,128]{1,0:T(8,128)(2,1)S(1)} %pair.1.refs_1_, bf16[1040,128]{1,0:T(8,128)(2,1)S(1)} %collective-permute-done.1.refs_2_, ...), custom_call_target="tpu_custom_call" | custom-call | tf_op jit(solution)/shard_map/mix/pallas_call | solution.py:43
  18.8 1.1 %collective-permute-start.5 = (bf16[3,528,128]{2,1,0:T(8,128)(2,1)S(1)}, bf16[3,528,128]{2,1,0:T(8,128)(2,1)S(1)}, u32[]{:S(2)}, u32[]{:S(2)}) collective-permute-start(bf16[3,528,128]{2,1,0:T(8,128)(2,1)S(1)} %get-tuple-element.43), channel_id=1, source_target_pairs={{0,1},{1,0},{2,3},{3,2},{4,5},{5,4},{6,7},{7,6},{8,9},{9,8},{10,11... | collective-permute-start | bytes 1216520 | tf_op jit(solution)/shard_map/ppermute | solution.py:440
  19.9 1.5 %collective-permute-start.6 = (bf16[3,528,128]{2,1,0:T(8,128)(2,1)S(1)}, bf16[3,528,128]{2,1,0:T(8,128)(2,1)S(1)}, u32[]{:S(2)}, u32[]{:S(2)}) collective-permute-start(bf16[3,528,128]{2,1,0:T(8,128)(2,1)S(1)} %get-tuple-element.44), channel_id=1, source_target_pairs={{0,2},{1,3},{2,0},{3,1},{4,6},{5,7},{6,4},{7,5},{8,10},{9,11},{10,... | collective-permute-start | bytes 1216520 | tf_op jit(solution)/shard_map/ppermute | solution.py:440
  21.5 0.9 %collective-permute-start.7 = (bf16[3,528,128]{2,1,0:T(8,128)(2,1)S(1)}, bf16[3,528,128]{2,1,0:T(8,128)(2,1)S(1)}, u32[]{:S(2)}, u32[]{:S(2)}) collective-permute-start(bf16[3,528,128]{2,1,0:T(8,128)(2,1)S(1)} %get-tuple-element.45), channel_id=1, source_target_pairs={{0,3},{1,2},{2,1},{3,0},{4,7},{5,6},{6,5},{7,4},{8,11},{9,10},{10,... | collective-permute-start | bytes 1216520 | tf_op jit(solution)/shard_map/ppermute | solution.py:440
  22.4 1.0 %ending.1 = (bf16[1040,128]{1,0:T(8,128)(2,1)S(1)}, bf16[1040,128]{1,0:T(8,128)(2,1)S(1)}) custom-call(s32[3]{0:T(128)S(1)} %pad_add_fusion.refs_0_, f32[32]{0:T(128)S(1)} %copy-done.3, bf16[1056,128]{1,0:T(8,128)(2,1)S(1)} %get-tuple-element.36.refs_2_.refs_4_, bf16[1056,128]{1,0:T(8,128)(2,1)S(1)} %collective-permute-done.3.refs_3_.refs_5_, ...), custom_call_target="tpu_custom_call" | custom-call | tf_op jit(solution)/shard_map/ending/pallas_call | solution.py:43
  23.4 1.3 %collective-permute-start.8 = (bf16[1040,128]{1,0:T(8,128)(2,1)S(1)}, bf16[1040,128]{1,0:T(8,128)(2,1)S(1)}, u32[]{:S(2)}, u32[]{:S(2)}) collective-permute-start(bf16[1040,128]{1,0:T(8,128)(2,1)S(1)} %get-tuple-element.39.refs_4_), channel_id=1, source_target_pairs={{0,4},{1,5},{2,6},{3,7},{4,8},{5,9},{6,10},{7,11},{8,12},{9,13},{1... | collective-permute-start | bytes 798728 | tf_op jit(solution)/shard_map/ppermute | solution.py:450
  24.7 5.2 %collective-permute-start.9 = (bf16[1040,128]{1,0:T(8,128)(2,1)S(1)}, bf16[1040,128]{1,0:T(8,128)(2,1)S(1)}, u32[]{:S(2)}, u32[]{:S(2)}) collective-permute-start(bf16[1040,128]{1,0:T(8,128)(2,1)S(1)} %get-tuple-element.46), channel_id=1, source_target_pairs={{0,8},{1,9},{2,10},{3,11},{4,12},{5,13},{6,14},{7,15},{8,16},{9,17... | collective-permute-start | bytes 798728 | tf_op jit(solution)/shard_map/ppermute | solution.py:450
  29.9 3.8 %home.1 = (f32[4,1024,256]{2,1,0:T(8,128)S(1)}, f32[4,1024,128]{2,1,0:T(8,128)S(1)}, bf16[2,1024,128]{2,1,0:T(8,128)(2,1)S(1)}) custom-call(s32[3]{0:T(128)S(1)} %pad_add_fusion.refs_0_, bf16[161,16,128]{2,1,0:T(8,128)(2,1)S(1)} %collective-permute-done.refs_1_, bf16[128,32,128]{2,1,0:T(8,128)(2,1)S(1)} %copy-done, ...), custom_call_target="tpu_custom_call" | custom-call | tf_op jit(solution)/shard_map/home/pallas_call | solution.py:43
  33.7 2.8 %collective-permute-done.9.refs_3_ = bf16[1040,128]{1,0:T(8,128)(2,1)S(1)} collective-permute-done((bf16[1040,128]{1,0:T(8,128)(2,1)S(1)}, bf16[1040,128]{1,0:T(8,128)(2,1)S(1)}, u32[]{:S(2)}, u32[]{:S(2)}) %collective-permute-start.9) | collective-permute-done | bytes 266272 | tf_op jit(solution)/shard_map/ppermute | solution.py:450
  36.5 1.1 %prefix.1 = (bf16[1040,128]{1,0:T(8,128)(2,1)S(1)}, bf16[1040,128]{1,0:T(8,128)(2,1)S(1)}, bf16[1040,128]{1,0:T(8,128)(2,1)S(1)}, bf16[1040,128]{1,0:T(8,128)(2,1)S(1)}) custom-call(s32[3]{0:T(128)S(1)} %pad_add_fusion.refs_0_, f32[32]{0:T(128)S(1)} %copy-done.3, bf16[1040,128]{1,0:T(8,128)(2,1)S(1)} %collective-permute-done.8.refs_2_, ...), custom_call_target="tpu_custom_call" | custom-call | tf_op jit(solution)/shard_map/prefix/pallas_call | solution.py:43
  37.6 2.1 %collective-permute-start.10 = (bf16[1040,128]{1,0:T(8,128)(2,1)S(1)}, bf16[1040,128]{1,0:T(8,128)(2,1)S(1)}, u32[]{:S(2)}, u32[]{:S(2)}) collective-permute-start(bf16[1040,128]{1,0:T(8,128)(2,1)S(1)} %get-tuple-element.51), channel_id=1, source_target_pairs={{0,3},{1,2},{2,1},{3,0},{4,7},{5,6},{6,5},{7,4},{8,11},{9,10},{10,... | collective-permute-start | bytes 798728 | tf_op jit(solution)/shard_map/ppermute | solution.py:440
  40.2 1.0 %collective-permute-start.14 = (bf16[1040,128]{1,0:T(8,128)(2,1)S(1)}, bf16[1040,128]{1,0:T(8,128)(2,1)S(1)}, u32[]{:S(2)}, u32[]{:S(2)}) collective-permute-start(bf16[1040,128]{1,0:T(8,128)(2,1)S(1)} %get-tuple-element.57), channel_id=1, source_target_pairs={{0,2},{1,3},{2,0},{3,1},{4,6},{5,7},{6,4},{7,5},{8,10},{9,11},{10,... | collective-permute-start | bytes 798728 | tf_op jit(solution)/shard_map/ppermute | solution.py:440
  41.2 5.8 %away.1 = (bf16[64,16,128]{2,1,0:T(8,128)(2,1)S(1)}, bf16[64,16,128]{2,1,0:T(8,128)(2,1)S(1)}, bf16[128,16,128]{2,1,0:T(8,128)(2,1)S(1)}) custom-call(s32[3]{0:T(128)S(1)} %pad_add_fusion.refs_0_, bf16[161,16,128]{2,1,0:T(8,128)(2,1)S(1)} %collective-permute-done.refs_1_, bf16[128,32,128]{2,1,0:T(8,128)(2,1)S(1)} %copy-done, ...), custom_call_target="tpu_custom_call" | custom-call | flops 30000001024 | tf_op jit(solution)/shard_map/away/pallas_call | solution.py:43
  47.0 0.8 %collective-permute-done.10.refs_10_ = bf16[1040,128]{1,0:T(8,128)(2,1)S(1)} collective-permute-done((bf16[1040,128]{1,0:T(8,128)(2,1)S(1)}, bf16[1040,128]{1,0:T(8,128)(2,1)S(1)}, u32[]{:S(2)}, u32[]{:S(2)}) %collective-permute-start.10) | collective-permute-done | bytes 266272 | tf_op jit(solution)/shard_map/ppermute | solution.py:440
  47.8 2.4 %first.1 = (bf16[128,32,128]{2,1,0:T(8,128)(2,1)}, bf16[128,32,128]{2,1,0:T(8,128)(2,1)}, bf16[64,16,128]{2,1,0:T(8,128)(2,1)S(1)}, bf16[64,16,128]{2,1,0:T(8,128)(2,1)S(1)}) custom-call(s32[3]{0:T(128)S(1)} %pad_add_fusion.refs_0_, f32[32]{0:T(128)S(1)} %copy-done.3, s32[1,128]{1,0:T(1,128)S(1)} %bitcast.6, ...), custom_call_target="tpu_custom_call", output_to_operand_aliasing={{2}: (7, {}), {3}: (8, {})} | custom-call | tf_op jit(solution)/shard_map/first/pallas_call | solution.py:43
  50.8 1.9 %collective-permute-done.13.refs_10_ = bf16[1040,128]{1,0:T(8,128)(2,1)S(1)} collective-permute-done((bf16[1040,128]{1,0:T(8,128)(2,1)S(1)}, bf16[1040,128]{1,0:T(8,128)(2,1)S(1)}, u32[]{:S(2)}, u32[]{:S(2)}) %collective-permute-start.13) | collective-permute-done | bytes 266272 | tf_op jit(solution)/shard_map/ppermute | solution.py:440
  53.1 2.4 %second.1 = (bf16[128,32,128]{2,1,0:T(8,128)(2,1)}, bf16[128,32,128]{2,1,0:T(8,128)(2,1)}) custom-call(s32[3]{0:T(128)S(1)} %pad_add_fusion.refs_0_, f32[32]{0:T(128)S(1)} %copy-done.3, s32[1,128]{1,0:T(1,128)S(1)} %bitcast.7, f32[32,128]{1,0:T(8,128)S(1)} %copy-done.2, ...), custom_call_target="tpu_custom_call", output_to_operand_aliasing={{0}: (8, {}), {1}: (9, {})} | custom-call | flops 15000000512 | tf_op jit(solution)/shard_map/second/pallas_call | solution.py:43
  (27 shorter events, 2.6 us)
Async XLA Ops:
  0.7 14.1 %copy-start.1 = (bf16[128,32,128]{2,1,0:T(8,128)(2,1)S(1)}, bf16[128,32,128]{2,1,0:T(8,128)(2,1)}, u32[]{:S(2)}) copy-start(bf16[128,32,128]{2,1,0:T(8,128)(2,1)} %refs_2_.3) | copy-start | bytes 3145732
  0.7 14.1 %copy-start.3 = (f32[32]{0:T(128)S(1)}, f32[32]{0:T(128)}, u32[]{:S(2)}) copy-start(f32[32]{0:T(128)} %refs_1_.9) | copy-start | bytes 388
  0.7 14.1 %copy-start.4 = (s32[128]{0:T(128)S(1)}, s32[128]{0:T(128)}, u32[]{:S(2)}) copy-start(s32[128]{0:T(128)} %param.17) | copy-start | bytes 1540
  4.1 4.0 %collective-permute-start = (bf16[161,16,128]{2,1,0:T(8,128)(2,1)S(1)}, bf16[161,16,128]{2,1,0:T(8,128)(2,1)S(1)}, u32[]{:S(2)}, u32[]{:S(2)}) collective-permute-start(bf16[161,16,128]{2,1,0:T(8,128)(2,1)S(1)} %get-tuple-element.32), channel_id=1, source_target_pairs={{0,4},{1,5},{2,6},{3,7},{4,0},{5,1},{6,2},{7,3},{8,12},{9,13},{10,... | collective-permute-start | bytes 1978376 | tf_op jit(solution)/shard_map/ppermute | solution.py:440
  4.6 11.7 %collective-permute-start.2 = (bf16[1056,128]{1,0:T(8,128)(2,1)S(1)}, bf16[1056,128]{1,0:T(8,128)(2,1)S(1)}, u32[]{:S(2)}, u32[]{:S(2)}) collective-permute-start(bf16[1056,128]{1,0:T(8,128)(2,1)S(1)} %get-tuple-element.34), channel_id=1, source_target_pairs={{0,3},{1,2},{2,1},{3,0},{4,7},{5,6},{6,5},{7,4},{8,11},{9,10},{10,... | collective-permute-start | bytes 811016 | tf_op jit(solution)/shard_map/ppermute | solution.py:440
  8.7 9.5 %collective-permute-start.1 = (bf16[1040,128]{1,0:T(8,128)(2,1)S(1)}, bf16[1040,128]{1,0:T(8,128)(2,1)S(1)}, u32[]{:S(2)}, u32[]{:S(2)}) collective-permute-start(bf16[1040,128]{1,0:T(8,128)(2,1)S(1)} %pair.1.refs_1_), channel_id=1, source_target_pairs={{0,8},{1,9},{2,10},{3,11},{4,12},{5,13},{6,14},{7,15},{8,16},{9,17... | collective-permute-start | bytes 798728 | tf_op jit(solution)/shard_map/ppermute | solution.py:450
  12.2 10.2 %collective-permute-start.3 = (bf16[1056,128]{1,0:T(8,128)(2,1)S(1)}, bf16[1056,128]{1,0:T(8,128)(2,1)S(1)}, u32[]{:S(2)}, u32[]{:S(2)}) collective-permute-start(bf16[1056,128]{1,0:T(8,128)(2,1)S(1)} %get-tuple-element.37), channel_id=1, source_target_pairs={{0,1},{1,0},{2,3},{3,2},{4,5},{5,4},{6,7},{7,6},{8,9},{9,8},{10,11... | collective-permute-start | bytes 811016 | tf_op jit(solution)/shard_map/ppermute | solution.py:440
  13.3 9.1 %collective-permute-start.4 = (bf16[1056,128]{1,0:T(8,128)(2,1)S(1)}, bf16[1056,128]{1,0:T(8,128)(2,1)S(1)}, u32[]{:S(2)}, u32[]{:S(2)}) collective-permute-start(bf16[1056,128]{1,0:T(8,128)(2,1)S(1)} %get-tuple-element.38), channel_id=1, source_target_pairs={{0,2},{1,3},{2,0},{3,1},{4,6},{5,7},{6,4},{7,5},{8,10},{9,11},{10,... | collective-permute-start | bytes 811016 | tf_op jit(solution)/shard_map/ppermute | solution.py:440
  16.3 13.6 %copy-start = (bf16[128,32,128]{2,1,0:T(8,128)(2,1)S(1)}, bf16[128,32,128]{2,1,0:T(8,128)(2,1)}, u32[]{:S(2)}) copy-start(bf16[128,32,128]{2,1,0:T(8,128)(2,1)} %refs_2_.5) | copy-start | bytes 3145732
  18.8 21.4 %collective-permute-start.5 = (bf16[3,528,128]{2,1,0:T(8,128)(2,1)S(1)}, bf16[3,528,128]{2,1,0:T(8,128)(2,1)S(1)}, u32[]{:S(2)}, u32[]{:S(2)}) collective-permute-start(bf16[3,528,128]{2,1,0:T(8,128)(2,1)S(1)} %get-tuple-element.43), channel_id=1, source_target_pairs={{0,1},{1,0},{2,3},{3,2},{4,5},{5,4},{6,7},{7,6},{8,9},{9,8},{10,11... | collective-permute-start | bytes 1216520 | tf_op jit(solution)/shard_map/ppermute | solution.py:440
  19.9 21.2 %collective-permute-start.6 = (bf16[3,528,128]{2,1,0:T(8,128)(2,1)S(1)}, bf16[3,528,128]{2,1,0:T(8,128)(2,1)S(1)}, u32[]{:S(2)}, u32[]{:S(2)}) collective-permute-start(bf16[3,528,128]{2,1,0:T(8,128)(2,1)S(1)} %get-tuple-element.44), channel_id=1, source_target_pairs={{0,2},{1,3},{2,0},{3,1},{4,6},{5,7},{6,4},{7,5},{8,10},{9,11},{10,... | collective-permute-start | bytes 1216520 | tf_op jit(solution)/shard_map/ppermute | solution.py:440
  21.5 19.7 %collective-permute-start.7 = (bf16[3,528,128]{2,1,0:T(8,128)(2,1)S(1)}, bf16[3,528,128]{2,1,0:T(8,128)(2,1)S(1)}, u32[]{:S(2)}, u32[]{:S(2)}) collective-permute-start(bf16[3,528,128]{2,1,0:T(8,128)(2,1)S(1)} %get-tuple-element.45), channel_id=1, source_target_pairs={{0,3},{1,2},{2,1},{3,0},{4,7},{5,6},{6,5},{7,4},{8,11},{9,10},{10,... | collective-permute-start | bytes 1216520 | tf_op jit(solution)/shard_map/ppermute | solution.py:440
  23.4 10.3 %collective-permute-start.8 = (bf16[1040,128]{1,0:T(8,128)(2,1)S(1)}, bf16[1040,128]{1,0:T(8,128)(2,1)S(1)}, u32[]{:S(2)}, u32[]{:S(2)}) collective-permute-start(bf16[1040,128]{1,0:T(8,128)(2,1)S(1)} %get-tuple-element.39.refs_4_), channel_id=1, source_target_pairs={{0,4},{1,5},{2,6},{3,7},{4,8},{5,9},{6,10},{7,11},{8,12},{9,13},{1... | collective-permute-start | bytes 798728 | tf_op jit(solution)/shard_map/ppermute | solution.py:450
  24.7 11.8 %collective-permute-start.9 = (bf16[1040,128]{1,0:T(8,128)(2,1)S(1)}, bf16[1040,128]{1,0:T(8,128)(2,1)S(1)}, u32[]{:S(2)}, u32[]{:S(2)}) collective-permute-start(bf16[1040,128]{1,0:T(8,128)(2,1)S(1)} %get-tuple-element.46), channel_id=1, source_target_pairs={{0,8},{1,9},{2,10},{3,11},{4,12},{5,13},{6,14},{7,15},{8,16},{9,17... | collective-permute-start | bytes 798728 | tf_op jit(solution)/shard_map/ppermute | solution.py:450
  37.6 10.2 %collective-permute-start.10 = (bf16[1040,128]{1,0:T(8,128)(2,1)S(1)}, bf16[1040,128]{1,0:T(8,128)(2,1)S(1)}, u32[]{:S(2)}, u32[]{:S(2)}) collective-permute-start(bf16[1040,128]{1,0:T(8,128)(2,1)S(1)} %get-tuple-element.51), channel_id=1, source_target_pairs={{0,3},{1,2},{2,1},{3,0},{4,7},{5,6},{6,5},{7,4},{8,11},{9,10},{10,... | collective-permute-start | bytes 798728 | tf_op jit(solution)/shard_map/ppermute | solution.py:440
  39.7 13.0 %collective-permute-start.13 = (bf16[1040,128]{1,0:T(8,128)(2,1)S(1)}, bf16[1040,128]{1,0:T(8,128)(2,1)S(1)}, u32[]{:S(2)}, u32[]{:S(2)}) collective-permute-start(bf16[1040,128]{1,0:T(8,128)(2,1)S(1)} %get-tuple-element.56), channel_id=1, source_target_pairs={{0,1},{1,0},{2,3},{3,2},{4,5},{5,4},{6,7},{7,6},{8,9},{9,8},{10,11... | collective-permute-start | bytes 798728 | tf_op jit(solution)/shard_map/ppermute | solution.py:440
  40.2 12.8 %collective-permute-start.14 = (bf16[1040,128]{1,0:T(8,128)(2,1)S(1)}, bf16[1040,128]{1,0:T(8,128)(2,1)S(1)}, u32[]{:S(2)}, u32[]{:S(2)}) collective-permute-start(bf16[1040,128]{1,0:T(8,128)(2,1)S(1)} %get-tuple-element.57), channel_id=1, source_target_pairs={{0,2},{1,3},{2,0},{3,1},{4,6},{5,7},{6,4},{7,5},{8,10},{9,11},{10,... | collective-permute-start | bytes 798728 | tf_op jit(solution)/shard_map/ppermute | solution.py:440
  41.2 6.6 %copy-start.2 = (f32[32,128]{1,0:T(8,128)S(1)}, f32[32,128]{1,0:T(8,128)}, u32[]{:S(2)}) copy-start(f32[32,128]{1,0:T(8,128)} %refs_3_.5) | copy-start | bytes 49156
  50.2 2.8 %collective-permute-start.11 = (bf16[64,16,128]{2,1,0:T(8,128)(2,1)S(1)}, bf16[64,16,128]{2,1,0:T(8,128)(2,1)S(1)}, u32[]{:S(2)}, u32[]{:S(2)}) collective-permute-start(bf16[64,16,128]{2,1,0:T(8,128)(2,1)S(1)} %get-tuple-element.52), channel_id=1, source_target_pairs={{0,4},{1,5},{2,6},{3,7},{4,0},{5,1},{6,2},{7,3},{8,12},{9,13},{10,... | collective-permute-start | bytes 786440 | tf_op jit(solution)/shard_map/ppermute | solution.py:440
  50.3 2.8 %collective-permute-start.12 = (bf16[64,16,128]{2,1,0:T(8,128)(2,1)S(1)}, bf16[64,16,128]{2,1,0:T(8,128)(2,1)S(1)}, u32[]{:S(2)}, u32[]{:S(2)}) collective-permute-start(bf16[64,16,128]{2,1,0:T(8,128)(2,1)S(1)} %get-tuple-element.53), channel_id=1, source_target_pairs={{0,4},{1,5},{2,6},{3,7},{4,0},{5,1},{6,2},{7,3},{8,12},{9,13},{10,... | collective-permute-start | bytes 786440 | tf_op jit(solution)/shard_map/ppermute | solution.py:440

commit v6 on v5

--- a/solution.py
+++ b/solution.py
@@ -74,11 +74,6 @@
     for copy in copies:
         copy.start()
     return copies
-
-
-def split(value):
-    high = value.astype(BF16)
-    return high, (value - high.astype(F32)).astype(BF16)
 
 
 def source_kernel(places, at_ref, rate_hbm, sid_hbm, key_hbm, value_hbm, soft_key_hbm, soft_value_hbm, soft_query_hbm, *rest):
@@ -130,8 +125,7 @@
             head = share_of(places, place ^ k) * per + j
             values = values_by_head[head]
             weighted = jnp.transpose(keys_by_head[head].astype(F32)) * (open_row * jnp.exp(-rate_ref[head] * behind))
-            high, low = split(weighted)
-            state = dot(jnp.concatenate([high, low], 1), jnp.concatenate([values, values], 0), ((1,), (0,)))
+            state = dot(weighted.astype(BF16), values, ((1,), (0,)))
             outs[k][pl.ds(j * width, width), :] = state.astype(BF16)
         outs[k][pl.ds(per * width, TAIL), :] = tail
         outs[k][pl.ds(per * width + TAIL, TAIL), :] = tail

time: 55.8 us -> 55.6 us (level)
  no operation moved by 1% of the time
where the time goes in v6:
time: 55.6 us; the launch traced here: 55.4 us
  starting transfers between devices  24.4 us (44%)
  Pallas kernels  22.3 us (40%)
  waiting for transfers between devices  7.73 us (14%)
  between operations  0.93 us (2%)
    pallas_call x10, Pallas kernels, call(): return lambda *args: made(*args, *after)  22.3 us
    ppermute x12, starting transfers between devices, partner(): return lax.ppermute(value, AXES, pairs)  14.4 us
    ppermute x3, starting transfers between devices, onward(): lax.ppermute(value, AXES, [(i, i + step) for i in range(n_all - step)])  10 us
    ppermute x3, waiting for transfers between devices, onward(): lax.ppermute(value, AXES, [(i, i + step) for i in range(n_all - step)])  4.64 us
    ppermute x12, waiting for transfers between devices, partner(): return lax.ppermute(value, AXES, pairs)  3.09 us
  transfers between devices with their start and end apart: 15, of which 5 were waited for; matrix products, arithmetic and copies ran while one was open for 0% of the time, Pallas kernels for 30%

profile of v6, /device:TPU:0, one launch (start us, length us, event | category | flops | bytes accessed | tf_op | source)
XLA Modules:
  0.0 55.4 jit_solution(6428904434808947471)
XLA Ops:
  0.7 3.1 %source.1 = (bf16[1056,128]{1,0:T(8,128)(2,1)S(1)}, bf16[1056,128]{1,0:T(8,128)(2,1)S(1)}, bf16[1056,128]{1,0:T(8,128)(2,1)S(1)}, bf16[1056,128]{1,0:T(8,128)(2,...) custom-call(s32[3]{0:T(128)S(1)} %pad_add_fusion.refs_0_, ...), custom_call_target="tpu_custom_call" | custom-call | tf_op jit(solution)/shard_map/source/pallas_call | solution.py:43
  4.4 3.5 %collective-permute-start.2 = (bf16[1056,128]{1,0:T(8,128)(2,1)S(1)}, bf16[1056,128]{1,0:T(8,128)(2,1)S(1)}, u32[]{:S(2)}, u32[]{:S(2)}) collective-permute-start(bf16[1056,128]{1,0:T(8,128)(2,1)S(1)} %get-tuple-element.34), channel_id=1, source_target_pairs={{0,3},{1,2},{2,1},{3,0},{4,7},{5,6},{6,5},{7,4},{8,11},{9,10},{10,... | collective-permute-start | bytes 811016 | tf_op jit(solution)/shard_map/ppermute | solution.py:434
  8.5 3.5 %collective-permute-start.1 = (bf16[1040,128]{1,0:T(8,128)(2,1)S(1)}, bf16[1040,128]{1,0:T(8,128)(2,1)S(1)}, u32[]{:S(2)}, u32[]{:S(2)}) collective-permute-start(bf16[1040,128]{1,0:T(8,128)(2,1)S(1)} %pair.1.refs_1_), channel_id=1, source_target_pairs={{0,8},{1,9},{2,10},{3,11},{4,12},{5,13},{6,14},{7,15},{8,16},{9,17... | collective-permute-start | bytes 798728 | tf_op jit(solution)/shard_map/ppermute | solution.py:444
  12.0 1.1 %collective-permute-start.3 = (bf16[1056,128]{1,0:T(8,128)(2,1)S(1)}, bf16[1056,128]{1,0:T(8,128)(2,1)S(1)}, u32[]{:S(2)}, u32[]{:S(2)}) collective-permute-start(bf16[1056,128]{1,0:T(8,128)(2,1)S(1)} %get-tuple-element.37), channel_id=1, source_target_pairs={{0,1},{1,0},{2,3},{3,2},{4,5},{5,4},{6,7},{7,6},{8,9},{9,8},{10,11... | collective-permute-start | bytes 811016 | tf_op jit(solution)/shard_map/ppermute | solution.py:434
  13.1 1.5 %collective-permute-start.4 = (bf16[1056,128]{1,0:T(8,128)(2,1)S(1)}, bf16[1056,128]{1,0:T(8,128)(2,1)S(1)}, u32[]{:S(2)}, u32[]{:S(2)}) collective-permute-start(bf16[1056,128]{1,0:T(8,128)(2,1)S(1)} %get-tuple-element.38), channel_id=1, source_target_pairs={{0,2},{1,3},{2,0},{3,1},{4,6},{5,7},{6,4},{7,5},{8,10},{9,11},{10,... | collective-permute-start | bytes 811016 | tf_op jit(solution)/shard_map/ppermute | solution.py:434
  14.6 1.4 %prep.1.refs_3_.refs_4_ = bf16[32,128,256]{2,1,0:T(8,128)(2,1)S(1)} custom-call(f32[32]{0:T(128)S(1)} %copy-done.3, s32[1,128]{1,0:T(1,128)S(1)} %bitcast.5, bf16[128,32,128]{2,1,0:T(8,128)(2,1)S(1)} %copy-done.1, bf16[32,128,128]{2,1,0:T(8,128)(2,1)S(1)} %get-tuple-element.30.refs_3_), custom_call_target="tpu_custom_call" | custom-call | tf_op jit(solution)/shard_map/prep/pallas_call | solution.py:43
  16.1 1.8 %collective-permute-done.1.refs_2_ = bf16[1040,128]{1,0:T(8,128)(2,1)S(1)} collective-permute-done((bf16[1040,128]{1,0:T(8,128)(2,1)S(1)}, bf16[1040,128]{1,0:T(8,128)(2,1)S(1)}, u32[]{:S(2)}, u32[]{:S(2)}) %collective-permute-start.1) | collective-permute-done | bytes 266272 | tf_op jit(solution)/shard_map/ppermute | solution.py:444
  17.9 0.7 %mix.1 = (bf16[4,528,128]{2,1,0:T(8,128)(2,1)S(1)}, bf16[3,528,128]{2,1,0:T(8,128)(2,1)S(1)}, bf16[3,528,128]{2,1,0:T(8,128)(2,1)S(1)}, bf16[3,528,128]{2,1,0:T(8,128)(2,1)S(1)}) custom-call(s32[3]{0:T(128)S(1)} %pad_add_fusion.refs_0_, bf16[1040,128]{1,0:T(8,128)(2,1)S(1)} %pair.1.refs_1_, bf16[1040,128]{1,0:T(8,128)(2,1)S(1)} %collective-permute-done.1.refs_2_, ...), custom_call_target="tpu_custom_call" | custom-call | tf_op jit(solution)/shard_map/mix/pallas_call | solution.py:43
  18.6 1.1 %collective-permute-start.5 = (bf16[3,528,128]{2,1,0:T(8,128)(2,1)S(1)}, bf16[3,528,128]{2,1,0:T(8,128)(2,1)S(1)}, u32[]{:S(2)}, u32[]{:S(2)}) collective-permute-start(bf16[3,528,128]{2,1,0:T(8,128)(2,1)S(1)} %get-tuple-element.43), channel_id=1, source_target_pairs={{0,1},{1,0},{2,3},{3,2},{4,5},{5,4},{6,7},{7,6},{8,9},{9,8},{10,11... | collective-permute-start | bytes 1216520 | tf_op jit(solution)/shard_map/ppermute | solution.py:434
  19.7 1.5 %collective-permute-start.6 = (bf16[3,528,128]{2,1,0:T(8,128)(2,1)S(1)}, bf16[3,528,128]{2,1,0:T(8,128)(2,1)S(1)}, u32[]{:S(2)}, u32[]{:S(2)}) collective-permute-start(bf16[3,528,128]{2,1,0:T(8,128)(2,1)S(1)} %get-tuple-element.44), channel_id=1, source_target_pairs={{0,2},{1,3},{2,0},{3,1},{4,6},{5,7},{6,4},{7,5},{8,10},{9,11},{10,... | collective-permute-start | bytes 1216520 | tf_op jit(solution)/shard_map/ppermute | solution.py:434
  21.2 0.9 %collective-permute-start.7 = (bf16[3,528,128]{2,1,0:T(8,128)(2,1)S(1)}, bf16[3,528,128]{2,1,0:T(8,128)(2,1)S(1)}, u32[]{:S(2)}, u32[]{:S(2)}) collective-permute-start(bf16[3,528,128]{2,1,0:T(8,128)(2,1)S(1)} %get-tuple-element.45), channel_id=1, source_target_pairs={{0,3},{1,2},{2,1},{3,0},{4,7},{5,6},{6,5},{7,4},{8,11},{9,10},{10,... | collective-permute-start | bytes 1216520 | tf_op jit(solution)/shard_map/ppermute | solution.py:434
  22.2 1.0 %ending.1 = (bf16[1040,128]{1,0:T(8,128)(2,1)S(1)}, bf16[1040,128]{1,0:T(8,128)(2,1)S(1)}) custom-call(s32[3]{0:T(128)S(1)} %pad_add_fusion.refs_0_, f32[32]{0:T(128)S(1)} %copy-done.3, bf16[1056,128]{1,0:T(8,128)(2,1)S(1)} %get-tuple-element.36.refs_2_.refs_4_, bf16[1056,128]{1,0:T(8,128)(2,1)S(1)} %collective-permute-done.3.refs_3_.refs_5_, ...), custom_call_target="tpu_custom_call" | custom-call | tf_op jit(solution)/shard_map/ending/pallas_call | solution.py:43
  23.2 1.3 %collective-permute-start.8 = (bf16[1040,128]{1,0:T(8,128)(2,1)S(1)}, bf16[1040,128]{1,0:T(8,128)(2,1)S(1)}, u32[]{:S(2)}, u32[]{:S(2)}) collective-permute-start(bf16[1040,128]{1,0:T(8,128)(2,1)S(1)} %get-tuple-element.39.refs_4_), channel_id=1, source_target_pairs={{0,4},{1,5},{2,6},{3,7},{4,8},{5,9},{6,10},{7,11},{8,12},{9,13},{1... | collective-permute-start | bytes 798728 | tf_op jit(solution)/shard_map/ppermute | solution.py:444
  24.5 5.2 %collective-permute-start.9 = (bf16[1040,128]{1,0:T(8,128)(2,1)S(1)}, bf16[1040,128]{1,0:T(8,128)(2,1)S(1)}, u32[]{:S(2)}, u32[]{:S(2)}) collective-permute-start(bf16[1040,128]{1,0:T(8,128)(2,1)S(1)} %get-tuple-element.46), channel_id=1, source_target_pairs={{0,8},{1,9},{2,10},{3,11},{4,12},{5,13},{6,14},{7,15},{8,16},{9,17... | collective-permute-start | bytes 798728 | tf_op jit(solution)/shard_map/ppermute | solution.py:444
  29.7 3.8 %home.1 = (f32[4,1024,256]{2,1,0:T(8,128)S(1)}, f32[4,1024,128]{2,1,0:T(8,128)S(1)}, bf16[2,1024,128]{2,1,0:T(8,128)(2,1)S(1)}) custom-call(s32[3]{0:T(128)S(1)} %pad_add_fusion.refs_0_, bf16[161,16,128]{2,1,0:T(8,128)(2,1)S(1)} %collective-permute-done.refs_1_, bf16[128,32,128]{2,1,0:T(8,128)(2,1)S(1)} %copy-done, ...), custom_call_target="tpu_custom_call" | custom-call | tf_op jit(solution)/shard_map/home/pallas_call | solution.py:43
  33.5 2.8 %collective-permute-done.9.refs_3_ = bf16[1040,128]{1,0:T(8,128)(2,1)S(1)} collective-permute-done((bf16[1040,128]{1,0:T(8,128)(2,1)S(1)}, bf16[1040,128]{1,0:T(8,128)(2,1)S(1)}, u32[]{:S(2)}, u32[]{:S(2)}) %collective-permute-start.9) | collective-permute-done | bytes 266272 | tf_op jit(solution)/shard_map/ppermute | solution.py:444
  36.3 1.1 %prefix.1 = (bf16[1040,128]{1,0:T(8,128)(2,1)S(1)}, bf16[1040,128]{1,0:T(8,128)(2,1)S(1)}, bf16[1040,128]{1,0:T(8,128)(2,1)S(1)}, bf16[1040,128]{1,0:T(8,128)(2,1)S(1)}) custom-call(s32[3]{0:T(128)S(1)} %pad_add_fusion.refs_0_, f32[32]{0:T(128)S(1)} %copy-done.3, bf16[1040,128]{1,0:T(8,128)(2,1)S(1)} %collective-permute-done.8.refs_2_, ...), custom_call_target="tpu_custom_call" | custom-call | tf_op jit(solution)/shard_map/prefix/pallas_call | solution.py:43
  37.4 2.1 %collective-permute-start.10 = (bf16[1040,128]{1,0:T(8,128)(2,1)S(1)}, bf16[1040,128]{1,0:T(8,128)(2,1)S(1)}, u32[]{:S(2)}, u32[]{:S(2)}) collective-permute-start(bf16[1040,128]{1,0:T(8,128)(2,1)S(1)} %get-tuple-element.51), channel_id=1, source_target_pairs={{0,3},{1,2},{2,1},{3,0},{4,7},{5,6},{6,5},{7,4},{8,11},{9,10},{10,... | collective-permute-start | bytes 798728 | tf_op jit(solution)/shard_map/ppermute | solution.py:434
  40.0 1.0 %collective-permute-start.14 = (bf16[1040,128]{1,0:T(8,128)(2,1)S(1)}, bf16[1040,128]{1,0:T(8,128)(2,1)S(1)}, u32[]{:S(2)}, u32[]{:S(2)}) collective-permute-start(bf16[1040,128]{1,0:T(8,128)(2,1)S(1)} %get-tuple-element.57), channel_id=1, source_target_pairs={{0,2},{1,3},{2,0},{3,1},{4,6},{5,7},{6,4},{7,5},{8,10},{9,11},{10,... | collective-permute-start | bytes 798728 | tf_op jit(solution)/shard_map/ppermute | solution.py:434
  41.0 5.8 %away.1 = (bf16[64,16,128]{2,1,0:T(8,128)(2,1)S(1)}, bf16[64,16,128]{2,1,0:T(8,128)(2,1)S(1)}, bf16[128,16,128]{2,1,0:T(8,128)(2,1)S(1)}) custom-call(s32[3]{0:T(128)S(1)} %pad_add_fusion.refs_0_, bf16[161,16,128]{2,1,0:T(8,128)(2,1)S(1)} %collective-permute-done.refs_1_, bf16[128,32,128]{2,1,0:T(8,128)(2,1)S(1)} %copy-done, ...), custom_call_target="tpu_custom_call" | custom-call | flops 30000001024 | tf_op jit(solution)/shard_map/away/pallas_call | solution.py:43
  46.8 0.8 %collective-permute-done.10.refs_10_ = bf16[1040,128]{1,0:T(8,128)(2,1)S(1)} collective-permute-done((bf16[1040,128]{1,0:T(8,128)(2,1)S(1)}, bf16[1040,128]{1,0:T(8,128)(2,1)S(1)}, u32[]{:S(2)}, u32[]{:S(2)}) %collective-permute-start.10) | collective-permute-done | bytes 266272 | tf_op jit(solution)/shard_map/ppermute | solution.py:434
  47.6 2.4 %first.1 = (bf16[128,32,128]{2,1,0:T(8,128)(2,1)}, bf16[128,32,128]{2,1,0:T(8,128)(2,1)}, bf16[64,16,128]{2,1,0:T(8,128)(2,1)S(1)}, bf16[64,16,128]{2,1,0:T(8,128)(2,1)S(1)}) custom-call(s32[3]{0:T(128)S(1)} %pad_add_fusion.refs_0_, f32[32]{0:T(128)S(1)} %copy-done.3, s32[1,128]{1,0:T(1,128)S(1)} %bitcast.6, ...), custom_call_target="tpu_custom_call", output_to_operand_aliasing={{2}: (7, {}), {3}: (8, {})} | custom-call | tf_op jit(solution)/shard_map/first/pallas_call | solution.py:43
  50.6 1.9 %collective-permute-done.13.refs_10_ = bf16[1040,128]{1,0:T(8,128)(2,1)S(1)} collective-permute-done((bf16[1040,128]{1,0:T(8,128)(2,1)S(1)}, bf16[1040,128]{1,0:T(8,128)(2,1)S(1)}, u32[]{:S(2)}, u32[]{:S(2)}) %collective-permute-start.13) | collective-permute-done | bytes 266272 | tf_op jit(solution)/shard_map/ppermute | solution.py:434
  52.8 2.4 %second.1 = (bf16[128,32,128]{2,1,0:T(8,128)(2,1)}, bf16[128,32,128]{2,1,0:T(8,128)(2,1)}) custom-call(s32[3]{0:T(128)S(1)} %pad_add_fusion.refs_0_, f32[32]{0:T(128)S(1)} %copy-done.3, s32[1,128]{1,0:T(1,128)S(1)} %bitcast.7, f32[32,128]{1,0:T(8,128)S(1)} %copy-done.2, ...), custom_call_target="tpu_custom_call", output_to_operand_aliasing={{0}: (8, {}), {1}: (9, {})} | custom-call | flops 15000000512 | tf_op jit(solution)/shard_map/second/pallas_call | solution.py:43
  (27 shorter events, 2.7 us)
Async XLA Ops:
  0.7 13.9 %copy-start.1 = (bf16[128,32,128]{2,1,0:T(8,128)(2,1)S(1)}, bf16[128,32,128]{2,1,0:T(8,128)(2,1)}, u32[]{:S(2)}) copy-start(bf16[128,32,128]{2,1,0:T(8,128)(2,1)} %refs_2_.3) | copy-start | bytes 3145732
  0.7 13.9 %copy-start.3 = (f32[32]{0:T(128)S(1)}, f32[32]{0:T(128)}, u32[]{:S(2)}) copy-start(f32[32]{0:T(128)} %refs_1_.9) | copy-start | bytes 388
  0.7 13.9 %copy-start.4 = (s32[128]{0:T(128)S(1)}, s32[128]{0:T(128)}, u32[]{:S(2)}) copy-start(s32[128]{0:T(128)} %param.17) | copy-start | bytes 1540
  3.9 4.0 %collective-permute-start = (bf16[161,16,128]{2,1,0:T(8,128)(2,1)S(1)}, bf16[161,16,128]{2,1,0:T(8,128)(2,1)S(1)}, u32[]{:S(2)}, u32[]{:S(2)}) collective-permute-start(bf16[161,16,128]{2,1,0:T(8,128)(2,1)S(1)} %get-tuple-element.32), channel_id=1, source_target_pairs={{0,4},{1,5},{2,6},{3,7},{4,0},{5,1},{6,2},{7,3},{8,12},{9,13},{10,... | collective-permute-start | bytes 1978376 | tf_op jit(solution)/shard_map/ppermute | solution.py:434
  4.4 11.7 %collective-permute-start.2 = (bf16[1056,128]{1,0:T(8,128)(2,1)S(1)}, bf16[1056,128]{1,0:T(8,128)(2,1)S(1)}, u32[]{:S(2)}, u32[]{:S(2)}) collective-permute-start(bf16[1056,128]{1,0:T(8,128)(2,1)S(1)} %get-tuple-element.34), channel_id=1, source_target_pairs={{0,3},{1,2},{2,1},{3,0},{4,7},{5,6},{6,5},{7,4},{8,11},{9,10},{10,... | collective-permute-start | bytes 811016 | tf_op jit(solution)/shard_map/ppermute | solution.py:434
  8.5 9.5 %collective-permute-start.1 = (bf16[1040,128]{1,0:T(8,128)(2,1)S(1)}, bf16[1040,128]{1,0:T(8,128)(2,1)S(1)}, u32[]{:S(2)}, u32[]{:S(2)}) collective-permute-start(bf16[1040,128]{1,0:T(8,128)(2,1)S(1)} %pair.1.refs_1_), channel_id=1, source_target_pairs={{0,8},{1,9},{2,10},{3,11},{4,12},{5,13},{6,14},{7,15},{8,16},{9,17... | collective-permute-start | bytes 798728 | tf_op jit(solution)/shard_map/ppermute | solution.py:444
  12.0 10.2 %collective-permute-start.3 = (bf16[1056,128]{1,0:T(8,128)(2,1)S(1)}, bf16[1056,128]{1,0:T(8,128)(2,1)S(1)}, u32[]{:S(2)}, u32[]{:S(2)}) collective-permute-start(bf16[1056,128]{1,0:T(8,128)(2,1)S(1)} %get-tuple-element.37), channel_id=1, source_target_pairs={{0,1},{1,0},{2,3},{3,2},{4,5},{5,4},{6,7},{7,6},{8,9},{9,8},{10,11... | collective-permute-start | bytes 811016 | tf_op jit(solution)/shard_map/ppermute | solution.py:434
  13.1 9.1 %collective-permute-start.4 = (bf16[1056,128]{1,0:T(8,128)(2,1)S(1)}, bf16[1056,128]{1,0:T(8,128)(2,1)S(1)}, u32[]{:S(2)}, u32[]{:S(2)}) collective-permute-start(bf16[1056,128]{1,0:T(8,128)(2,1)S(1)} %get-tuple-element.38), channel_id=1, source_target_pairs={{0,2},{1,3},{2,0},{3,1},{4,6},{5,7},{6,4},{7,5},{8,10},{9,11},{10,... | collective-permute-start | bytes 811016 | tf_op jit(solution)/shard_map/ppermute | solution.py:434
  16.1 13.6 %copy-start = (bf16[128,32,128]{2,1,0:T(8,128)(2,1)S(1)}, bf16[128,32,128]{2,1,0:T(8,128)(2,1)}, u32[]{:S(2)}) copy-start(bf16[128,32,128]{2,1,0:T(8,128)(2,1)} %refs_2_.5) | copy-start | bytes 3145732
  18.6 21.4 %collective-permute-start.5 = (bf16[3,528,128]{2,1,0:T(8,128)(2,1)S(1)}, bf16[3,528,128]{2,1,0:T(8,128)(2,1)S(1)}, u32[]{:S(2)}, u32[]{:S(2)}) collective-permute-start(bf16[3,528,128]{2,1,0:T(8,128)(2,1)S(1)} %get-tuple-element.43), channel_id=1, source_target_pairs={{0,1},{1,0},{2,3},{3,2},{4,5},{5,4},{6,7},{7,6},{8,9},{9,8},{10,11... | collective-permute-start | bytes 1216520 | tf_op jit(solution)/shard_map/ppermute | solution.py:434
  19.7 21.2 %collective-permute-start.6 = (bf16[3,528,128]{2,1,0:T(8,128)(2,1)S(1)}, bf16[3,528,128]{2,1,0:T(8,128)(2,1)S(1)}, u32[]{:S(2)}, u32[]{:S(2)}) collective-permute-start(bf16[3,528,128]{2,1,0:T(8,128)(2,1)S(1)} %get-tuple-element.44), channel_id=1, source_target_pairs={{0,2},{1,3},{2,0},{3,1},{4,6},{5,7},{6,4},{7,5},{8,10},{9,11},{10,... | collective-permute-start | bytes 1216520 | tf_op jit(solution)/shard_map/ppermute | solution.py:434
  21.2 19.7 %collective-permute-start.7 = (bf16[3,528,128]{2,1,0:T(8,128)(2,1)S(1)}, bf16[3,528,128]{2,1,0:T(8,128)(2,1)S(1)}, u32[]{:S(2)}, u32[]{:S(2)}) collective-permute-start(bf16[3,528,128]{2,1,0:T(8,128)(2,1)S(1)} %get-tuple-element.45), channel_id=1, source_target_pairs={{0,3},{1,2},{2,1},{3,0},{4,7},{5,6},{6,5},{7,4},{8,11},{9,10},{10,... | collective-permute-start | bytes 1216520 | tf_op jit(solution)/shard_map/ppermute | solution.py:434
  23.2 10.3 %collective-permute-start.8 = (bf16[1040,128]{1,0:T(8,128)(2,1)S(1)}, bf16[1040,128]{1,0:T(8,128)(2,1)S(1)}, u32[]{:S(2)}, u32[]{:S(2)}) collective-permute-start(bf16[1040,128]{1,0:T(8,128)(2,1)S(1)} %get-tuple-element.39.refs_4_), channel_id=1, source_target_pairs={{0,4},{1,5},{2,6},{3,7},{4,8},{5,9},{6,10},{7,11},{8,12},{9,13},{1... | collective-permute-start | bytes 798728 | tf_op jit(solution)/shard_map/ppermute | solution.py:444
  24.5 11.8 %collective-permute-start.9 = (bf16[1040,128]{1,0:T(8,128)(2,1)S(1)}, bf16[1040,128]{1,0:T(8,128)(2,1)S(1)}, u32[]{:S(2)}, u32[]{:S(2)}) collective-permute-start(bf16[1040,128]{1,0:T(8,128)(2,1)S(1)} %get-tuple-element.46), channel_id=1, source_target_pairs={{0,8},{1,9},{2,10},{3,11},{4,12},{5,13},{6,14},{7,15},{8,16},{9,17... | collective-permute-start | bytes 798728 | tf_op jit(solution)/shard_map/ppermute | solution.py:444
  37.4 10.2 %collective-permute-start.10 = (bf16[1040,128]{1,0:T(8,128)(2,1)S(1)}, bf16[1040,128]{1,0:T(8,128)(2,1)S(1)}, u32[]{:S(2)}, u32[]{:S(2)}) collective-permute-start(bf16[1040,128]{1,0:T(8,128)(2,1)S(1)} %get-tuple-element.51), channel_id=1, source_target_pairs={{0,3},{1,2},{2,1},{3,0},{4,7},{5,6},{6,5},{7,4},{8,11},{9,10},{10,... | collective-permute-start | bytes 798728 | tf_op jit(solution)/shard_map/ppermute | solution.py:434
  39.5 13.0 %collective-permute-start.13 = (bf16[1040,128]{1,0:T(8,128)(2,1)S(1)}, bf16[1040,128]{1,0:T(8,128)(2,1)S(1)}, u32[]{:S(2)}, u32[]{:S(2)}) collective-permute-start(bf16[1040,128]{1,0:T(8,128)(2,1)S(1)} %get-tuple-element.56), channel_id=1, source_target_pairs={{0,1},{1,0},{2,3},{3,2},{4,5},{5,4},{6,7},{7,6},{8,9},{9,8},{10,11... | collective-permute-start | bytes 798728 | tf_op jit(solution)/shard_map/ppermute | solution.py:434
  40.0 12.8 %collective-permute-start.14 = (bf16[1040,128]{1,0:T(8,128)(2,1)S(1)}, bf16[1040,128]{1,0:T(8,128)(2,1)S(1)}, u32[]{:S(2)}, u32[]{:S(2)}) collective-permute-start(bf16[1040,128]{1,0:T(8,128)(2,1)S(1)} %get-tuple-element.57), channel_id=1, source_target_pairs={{0,2},{1,3},{2,0},{3,1},{4,6},{5,7},{6,4},{7,5},{8,10},{9,11},{10,... | collective-permute-start | bytes 798728 | tf_op jit(solution)/shard_map/ppermute | solution.py:434
  41.0 6.6 %copy-start.2 = (f32[32,128]{1,0:T(8,128)S(1)}, f32[32,128]{1,0:T(8,128)}, u32[]{:S(2)}) copy-start(f32[32,128]{1,0:T(8,128)} %refs_3_.5) | copy-start | bytes 49156
  50.0 2.8 %collective-permute-start.11 = (bf16[64,16,128]{2,1,0:T(8,128)(2,1)S(1)}, bf16[64,16,128]{2,1,0:T(8,128)(2,1)S(1)}, u32[]{:S(2)}, u32[]{:S(2)}) collective-permute-start(bf16[64,16,128]{2,1,0:T(8,128)(2,1)S(1)} %get-tuple-element.52), channel_id=1, source_target_pairs={{0,4},{1,5},{2,6},{3,7},{4,0},{5,1},{6,2},{7,3},{8,12},{9,13},{10,... | collective-permute-start | bytes 786440 | tf_op jit(solution)/shard_map/ppermute | solution.py:434
  50.1 2.8 %collective-permute-start.12 = (bf16[64,16,128]{2,1,0:T(8,128)(2,1)S(1)}, bf16[64,16,128]{2,1,0:T(8,128)(2,1)S(1)}, u32[]{:S(2)}, u32[]{:S(2)}) collective-permute-start(bf16[64,16,128]{2,1,0:T(8,128)(2,1)S(1)} %get-tuple-element.53), channel_id=1, source_target_pairs={{0,4},{1,5},{2,6},{3,7},{4,0},{5,1},{6,2},{7,3},{8,12},{9,13},{10,... | collective-permute-start | bytes 786440 | tf_op jit(solution)/shard_map/ppermute | solution.py:434

commit v7 on v5

--- a/solution.py
+++ b/solution.py
@@ -163,12 +163,15 @@
             home_ref[slot, pl.ds(0, span), :] = ref[pl.ds(block * span, span), :]
             row = block * (TAIL // LOOK)
             home_ref[slot, pl.ds(span, TAIL), :] = jnp.broadcast_to(tails[row : row + 1], (TAIL, width)).astype(BF16)
+    row_at = lax.broadcasted_iota(jnp.int32, (TAIL, width), 0)
     for k in range(1, places):
         out = outs[k - 1]
         later = ((place ^ k) > place).astype(jnp.int32)
-        out[0] = home_ref[0]
-        out[1] = home_ref[3]
-        out[2] = home_ref[1 + later]
+        tail = jnp.zeros((TAIL, width), F32)
+        for n, slot in enumerate((0, 3, 1 + later)):
+            out[pl.ds(n * span, span), :] = home_ref[slot, pl.ds(0, span), :]
+            tail = jnp.where(row_at == n, home_ref[slot, pl.ds(span, TAIL), :].astype(F32), tail)
+        out[pl.ds(3 * span, TAIL), :] = tail.astype(BF16)
 
 
 def gather_slots(places, at_ref, pays, slots):
@@ -318,8 +321,21 @@
 
     def marked(self, pick):
         ref, slot = pick
-        sids = ref[slot, pl.ds(2 * self.kv_heads * self.tokens, TAIL), :].astype(F32)[0:1, :]
+        span = 2 * self.kv_heads * self.tokens
+        if len(ref.shape) == 3:
+            sids = ref[slot, pl.ds(span, TAIL), :].astype(F32)[0:1, :]
+        else:
+            tail = ref[pl.ds(ref.shape[0] - TAIL, TAIL), :].astype(F32)
+            row_at = lax.broadcasted_iota(jnp.int32, tail.shape, 0)
+            sids = jnp.sum(jnp.where(row_at == slot, tail, 0.0), axis=0, keepdims=True)
         return column(sids) == self.lane.astype(F32)
+
+    def part(self, pick, n):
+        ref, slot = pick
+        if len(ref.shape) == 3:
+            return ref[slot, pl.ds(n * self.tokens, self.tokens), :]
+        start = slot * (2 * self.kv_heads * self.tokens) + n * self.tokens
+        return ref[pl.ds(pl.multiple_of(start, TAIL), self.tokens), :]
 
     def far(self, block, ks, pays):
         picks = []
@@ -346,7 +362,7 @@
     def scores(self, own, g, marks, picks):
         tokens = self.tokens
         query = jnp.concatenate([self.query(own, g), marks], 1)
-        keys = jnp.concatenate([ref[slot, pl.ds(g * tokens, tokens), :] for ref, slot in picks], 0)
+        keys = jnp.concatenate([self.part(pick, g) for pick in picks], 0)
         codes = self.codes[own, pl.ds(0, len(picks) * tokens), :]
         return dot(query, jnp.concatenate([keys, codes], 1), ((1,), (1,)))
 
@@ -355,9 +371,7 @@
         return jnp.exp2((scores - wide) * self.factor).astype(BF16)
 
     def mixed(self, g, probs, picks):
-        tokens = self.tokens
-        rows = pl.ds((self.kv_heads + g) * tokens, tokens)
-        values = jnp.concatenate([ref[slot, rows, :] for ref, slot in picks], 0)
+        values = jnp.concatenate([self.part(pick, self.kv_heads + g) for pick in picks], 0)
         return dot(probs, jnp.concatenate([values, jnp.ones_like(values)], 1), ((1,), (0,)))
 
     def top(self, scores):
@@ -487,7 +501,7 @@
     )(decay_rate, sid_row, light_query, keys_by_head)
     mixed = call(
         functools.partial(mix_kernel, places), "mix", 0, 8, [SMEM] + [VMEM] * 2,
-        [shape(4, *pay.shape)] + [shape(3, *pay.shape)] * (places - 1), [VMEM] * places, after=[left, *[states[k] for k in even[1:]]],
+        [shape(4, *pay.shape)] + [shape(3 * (pay.shape[0] - TAIL) + TAIL, width)] * (places - 1), [VMEM] * places, after=[left, *[states[k] for k in even[1:]]],
     )(at, own, before)
     home = mixed[0]
     parcels = to_places(mixed)

time: 55.8 us -> 55.8 us (level)
  no operation moved by 1% of the time
where the time goes in v7:
time: 55.8 us; the launch traced here: 55.6 us
  starting transfers between devices  24.4 us (44%)
  Pallas kernels  22.6 us (41%)
  waiting for transfers between devices  7.62 us (14%)
  between operations  0.93 us (2%)
    pallas_call x10, Pallas kernels, call(): return lambda *args: made(*args, *after)  22.6 us
    ppermute x12, starting transfers between devices, partner(): return lax.ppermute(value, AXES, pairs)  14.4 us
    ppermute x3, starting transfers between devices, onward(): lax.ppermute(value, AXES, [(i, i + step) for i in range(n_all - step)])  10 us
    ppermute x3, waiting for transfers between devices, onward(): lax.ppermute(value, AXES, [(i, i + step) for i in range(n_all - step)])  4.66 us
    ppermute x12, waiting for transfers between devices, partner(): return lax.ppermute(value, AXES, pairs)  2.96 us
  transfers between devices with their start and end apart: 15, of which 5 were waited for; matrix products, arithmetic and copies ran while one was open for 0% of the time, Pallas kernels for 30%

profile of v7, /device:TPU:0, one launch (start us, length us, event | category | flops | bytes accessed | tf_op | source)
XLA Modules:
  0.0 55.6 jit_solution(4781404202326743930)
XLA Ops:
  0.7 3.4 %source.1 = (bf16[1056,128]{1,0:T(8,128)(2,1)S(1)}, bf16[1056,128]{1,0:T(8,128)(2,1)S(1)}, bf16[1056,128]{1,0:T(8,128)(2,1)S(1)}, bf16[1056,128]{1,0:T(8,128)(2,...) custom-call(s32[3]{0:T(128)S(1)} %pad_add_fusion.refs_0_, ...), custom_call_target="tpu_custom_call" | custom-call | tf_op jit(solution)/shard_map/source/pallas_call | solution.py:43
  4.6 3.5 %collective-permute-start.2 = (bf16[1056,128]{1,0:T(8,128)(2,1)S(1)}, bf16[1056,128]{1,0:T(8,128)(2,1)S(1)}, u32[]{:S(2)}, u32[]{:S(2)}) collective-permute-start(bf16[1056,128]{1,0:T(8,128)(2,1)S(1)} %get-tuple-element.34), channel_id=1, source_target_pairs={{0,3},{1,2},{2,1},{3,0},{4,7},{5,6},{6,5},{7,4},{8,11},{9,10},{10,... | collective-permute-start | bytes 811016 | tf_op jit(solution)/shard_map/ppermute | solution.py:454
  8.7 3.5 %collective-permute-start.1 = (bf16[1040,128]{1,0:T(8,128)(2,1)S(1)}, bf16[1040,128]{1,0:T(8,128)(2,1)S(1)}, u32[]{:S(2)}, u32[]{:S(2)}) collective-permute-start(bf16[1040,128]{1,0:T(8,128)(2,1)S(1)} %pair.1.refs_1_), channel_id=1, source_target_pairs={{0,8},{1,9},{2,10},{3,11},{4,12},{5,13},{6,14},{7,15},{8,16},{9,17... | collective-permute-start | bytes 798728 | tf_op jit(solution)/shard_map/ppermute | solution.py:464
  12.2 1.1 %collective-permute-start.3 = (bf16[1056,128]{1,0:T(8,128)(2,1)S(1)}, bf16[1056,128]{1,0:T(8,128)(2,1)S(1)}, u32[]{:S(2)}, u32[]{:S(2)}) collective-permute-start(bf16[1056,128]{1,0:T(8,128)(2,1)S(1)} %get-tuple-element.37), channel_id=1, source_target_pairs={{0,1},{1,0},{2,3},{3,2},{4,5},{5,4},{6,7},{7,6},{8,9},{9,8},{10,11... | collective-permute-start | bytes 811016 | tf_op jit(solution)/shard_map/ppermute | solution.py:454
  13.3 1.5 %collective-permute-start.4 = (bf16[1056,128]{1,0:T(8,128)(2,1)S(1)}, bf16[1056,128]{1,0:T(8,128)(2,1)S(1)}, u32[]{:S(2)}, u32[]{:S(2)}) collective-permute-start(bf16[1056,128]{1,0:T(8,128)(2,1)S(1)} %get-tuple-element.38), channel_id=1, source_target_pairs={{0,2},{1,3},{2,0},{3,1},{4,6},{5,7},{6,4},{7,5},{8,10},{9,11},{10,... | collective-permute-start | bytes 811016 | tf_op jit(solution)/shard_map/ppermute | solution.py:454
  14.9 1.4 %prep.1.refs_3_.refs_4_ = bf16[32,128,256]{2,1,0:T(8,128)(2,1)S(1)} custom-call(f32[32]{0:T(128)S(1)} %copy-done.3, s32[1,128]{1,0:T(1,128)S(1)} %bitcast.5, bf16[128,32,128]{2,1,0:T(8,128)(2,1)S(1)} %copy-done.1, bf16[32,128,128]{2,1,0:T(8,128)(2,1)S(1)} %get-tuple-element.30.refs_3_), custom_call_target="tpu_custom_call" | custom-call | tf_op jit(solution)/shard_map/prep/pallas_call | solution.py:43
  16.3 1.9 %collective-permute-done.1.refs_2_ = bf16[1040,128]{1,0:T(8,128)(2,1)S(1)} collective-permute-done((bf16[1040,128]{1,0:T(8,128)(2,1)S(1)}, bf16[1040,128]{1,0:T(8,128)(2,1)S(1)}, u32[]{:S(2)}, u32[]{:S(2)}) %collective-permute-start.1) | collective-permute-done | bytes 266272 | tf_op jit(solution)/shard_map/ppermute | solution.py:464
  18.2 0.7 %mix.1 = (bf16[4,528,128]{2,1,0:T(8,128)(2,1)S(1)}, bf16[1552,128]{1,0:T(8,128)(2,1)S(1)}, bf16[1552,128]{1,0:T(8,128)(2,1)S(1)}, bf16[1552,128]{1,0:T(8,128)(2,1)S(1)}) custom-call(s32[3]{0:T(128)S(1)} %pad_add_fusion.refs_0_, bf16[1040,128]{1,0:T(8,128)(2,1)S(1)} %pair.1.refs_1_, bf16[1040,128]{1,0:T(8,128)(2,1)S(1)} %collective-permute-done.1.refs_2_, ...), custom_call_target="tpu_custom_call" | custom-call | tf_op jit(solution)/shard_map/mix/pallas_call | solution.py:43
  18.8 1.1 %collective-permute-start.5 = (bf16[1552,128]{1,0:T(8,128)(2,1)S(1)}, bf16[1552,128]{1,0:T(8,128)(2,1)S(1)}, u32[]{:S(2)}, u32[]{:S(2)}) collective-permute-start(bf16[1552,128]{1,0:T(8,128)(2,1)S(1)} %get-tuple-element.43), channel_id=1, source_target_pairs={{0,1},{1,0},{2,3},{3,2},{4,5},{5,4},{6,7},{7,6},{8,9},{9,8},{10,11... | collective-permute-start | bytes 1191944 | tf_op jit(solution)/shard_map/ppermute | solution.py:454
  20.0 1.5 %collective-permute-start.6 = (bf16[1552,128]{1,0:T(8,128)(2,1)S(1)}, bf16[1552,128]{1,0:T(8,128)(2,1)S(1)}, u32[]{:S(2)}, u32[]{:S(2)}) collective-permute-start(bf16[1552,128]{1,0:T(8,128)(2,1)S(1)} %get-tuple-element.44), channel_id=1, source_target_pairs={{0,2},{1,3},{2,0},{3,1},{4,6},{5,7},{6,4},{7,5},{8,10},{9,11},{10,... | collective-permute-start | bytes 1191944 | tf_op jit(solution)/shard_map/ppermute | solution.py:454
  21.5 0.9 %collective-permute-start.7 = (bf16[1552,128]{1,0:T(8,128)(2,1)S(1)}, bf16[1552,128]{1,0:T(8,128)(2,1)S(1)}, u32[]{:S(2)}, u32[]{:S(2)}) collective-permute-start(bf16[1552,128]{1,0:T(8,128)(2,1)S(1)} %get-tuple-element.45), channel_id=1, source_target_pairs={{0,3},{1,2},{2,1},{3,0},{4,7},{5,6},{6,5},{7,4},{8,11},{9,10},{10,... | collective-permute-start | bytes 1191944 | tf_op jit(solution)/shard_map/ppermute | solution.py:454
  22.4 1.0 %ending.1 = (bf16[1040,128]{1,0:T(8,128)(2,1)S(1)}, bf16[1040,128]{1,0:T(8,128)(2,1)S(1)}) custom-call(s32[3]{0:T(128)S(1)} %pad_add_fusion.refs_0_, f32[32]{0:T(128)S(1)} %copy-done.3, bf16[1056,128]{1,0:T(8,128)(2,1)S(1)} %get-tuple-element.36.refs_2_.refs_4_, bf16[1056,128]{1,0:T(8,128)(2,1)S(1)} %collective-permute-done.3.refs_3_.refs_5_, ...), custom_call_target="tpu_custom_call" | custom-call | tf_op jit(solution)/shard_map/ending/pallas_call | solution.py:43
  23.4 1.3 %collective-permute-start.8 = (bf16[1040,128]{1,0:T(8,128)(2,1)S(1)}, bf16[1040,128]{1,0:T(8,128)(2,1)S(1)}, u32[]{:S(2)}, u32[]{:S(2)}) collective-permute-start(bf16[1040,128]{1,0:T(8,128)(2,1)S(1)} %get-tuple-element.39.refs_4_), channel_id=1, source_target_pairs={{0,4},{1,5},{2,6},{3,7},{4,8},{5,9},{6,10},{7,11},{8,12},{9,13},{1... | collective-permute-start | bytes 798728 | tf_op jit(solution)/shard_map/ppermute | solution.py:464
  24.7 5.2 %collective-permute-start.9 = (bf16[1040,128]{1,0:T(8,128)(2,1)S(1)}, bf16[1040,128]{1,0:T(8,128)(2,1)S(1)}, u32[]{:S(2)}, u32[]{:S(2)}) collective-permute-start(bf16[1040,128]{1,0:T(8,128)(2,1)S(1)} %get-tuple-element.46), channel_id=1, source_target_pairs={{0,8},{1,9},{2,10},{3,11},{4,12},{5,13},{6,14},{7,15},{8,16},{9,17... | collective-permute-start | bytes 798728 | tf_op jit(solution)/shard_map/ppermute | solution.py:464
  29.9 3.8 %home.1 = (f32[4,1024,256]{2,1,0:T(8,128)S(1)}, f32[4,1024,128]{2,1,0:T(8,128)S(1)}, bf16[2,1024,128]{2,1,0:T(8,128)(2,1)S(1)}) custom-call(s32[3]{0:T(128)S(1)} %pad_add_fusion.refs_0_, bf16[161,16,128]{2,1,0:T(8,128)(2,1)S(1)} %collective-permute-done.refs_1_, bf16[128,32,128]{2,1,0:T(8,128)(2,1)S(1)} %copy-done, ...), custom_call_target="tpu_custom_call" | custom-call | tf_op jit(solution)/shard_map/home/pallas_call | solution.py:43
  33.7 2.8 %collective-permute-done.9.refs_3_ = bf16[1040,128]{1,0:T(8,128)(2,1)S(1)} collective-permute-done((bf16[1040,128]{1,0:T(8,128)(2,1)S(1)}, bf16[1040,128]{1,0:T(8,128)(2,1)S(1)}, u32[]{:S(2)}, u32[]{:S(2)}) %collective-permute-start.9) | collective-permute-done | bytes 266272 | tf_op jit(solution)/shard_map/ppermute | solution.py:464
  36.5 1.1 %prefix.1 = (bf16[1040,128]{1,0:T(8,128)(2,1)S(1)}, bf16[1040,128]{1,0:T(8,128)(2,1)S(1)}, bf16[1040,128]{1,0:T(8,128)(2,1)S(1)}, bf16[1040,128]{1,0:T(8,128)(2,1)S(1)}) custom-call(s32[3]{0:T(128)S(1)} %pad_add_fusion.refs_0_, f32[32]{0:T(128)S(1)} %copy-done.3, bf16[1040,128]{1,0:T(8,128)(2,1)S(1)} %collective-permute-done.8.refs_2_, ...), custom_call_target="tpu_custom_call" | custom-call | tf_op jit(solution)/shard_map/prefix/pallas_call | solution.py:43
  37.6 2.1 %collective-permute-start.10 = (bf16[1040,128]{1,0:T(8,128)(2,1)S(1)}, bf16[1040,128]{1,0:T(8,128)(2,1)S(1)}, u32[]{:S(2)}, u32[]{:S(2)}) collective-permute-start(bf16[1040,128]{1,0:T(8,128)(2,1)S(1)} %get-tuple-element.51), channel_id=1, source_target_pairs={{0,3},{1,2},{2,1},{3,0},{4,7},{5,6},{6,5},{7,4},{8,11},{9,10},{10,... | collective-permute-start | bytes 798728 | tf_op jit(solution)/shard_map/ppermute | solution.py:454
  40.2 1.0 %collective-permute-start.14 = (bf16[1040,128]{1,0:T(8,128)(2,1)S(1)}, bf16[1040,128]{1,0:T(8,128)(2,1)S(1)}, u32[]{:S(2)}, u32[]{:S(2)}) collective-permute-start(bf16[1040,128]{1,0:T(8,128)(2,1)S(1)} %get-tuple-element.57), channel_id=1, source_target_pairs={{0,2},{1,3},{2,0},{3,1},{4,6},{5,7},{6,4},{7,5},{8,10},{9,11},{10,... | collective-permute-start | bytes 798728 | tf_op jit(solution)/shard_map/ppermute | solution.py:454
  41.2 5.9 %away.1 = (bf16[64,16,128]{2,1,0:T(8,128)(2,1)S(1)}, bf16[64,16,128]{2,1,0:T(8,128)(2,1)S(1)}, bf16[128,16,128]{2,1,0:T(8,128)(2,1)S(1)}) custom-call(s32[3]{0:T(128)S(1)} %pad_add_fusion.refs_0_, bf16[161,16,128]{2,1,0:T(8,128)(2,1)S(1)} %collective-permute-done.refs_1_, bf16[128,32,128]{2,1,0:T(8,128)(2,1)S(1)} %copy-done, ...), custom_call_target="tpu_custom_call" | custom-call | flops 30000001024 | tf_op jit(solution)/shard_map/away/pallas_call | solution.py:43
  47.1 0.7 %collective-permute-done.10.refs_10_ = bf16[1040,128]{1,0:T(8,128)(2,1)S(1)} collective-permute-done((bf16[1040,128]{1,0:T(8,128)(2,1)S(1)}, bf16[1040,128]{1,0:T(8,128)(2,1)S(1)}, u32[]{:S(2)}, u32[]{:S(2)}) %collective-permute-start.10) | collective-permute-done | bytes 266272 | tf_op jit(solution)/shard_map/ppermute | solution.py:454
  47.8 2.4 %first.1 = (bf16[128,32,128]{2,1,0:T(8,128)(2,1)}, bf16[128,32,128]{2,1,0:T(8,128)(2,1)}, bf16[64,16,128]{2,1,0:T(8,128)(2,1)S(1)}, bf16[64,16,128]{2,1,0:T(8,128)(2,1)S(1)}) custom-call(s32[3]{0:T(128)S(1)} %pad_add_fusion.refs_0_, f32[32]{0:T(128)S(1)} %copy-done.3, s32[1,128]{1,0:T(1,128)S(1)} %bitcast.6, ...), custom_call_target="tpu_custom_call", output_to_operand_aliasing={{2}: (7, {}), {3}: (8, {})} | custom-call | tf_op jit(solution)/shard_map/first/pallas_call | solution.py:43
  50.8 1.9 %collective-permute-done.13.refs_10_ = bf16[1040,128]{1,0:T(8,128)(2,1)S(1)} collective-permute-done((bf16[1040,128]{1,0:T(8,128)(2,1)S(1)}, bf16[1040,128]{1,0:T(8,128)(2,1)S(1)}, u32[]{:S(2)}, u32[]{:S(2)}) %collective-permute-start.13) | collective-permute-done | bytes 266272 | tf_op jit(solution)/shard_map/ppermute | solution.py:454
  53.0 2.4 %second.1 = (bf16[128,32,128]{2,1,0:T(8,128)(2,1)}, bf16[128,32,128]{2,1,0:T(8,128)(2,1)}) custom-call(s32[3]{0:T(128)S(1)} %pad_add_fusion.refs_0_, f32[32]{0:T(128)S(1)} %copy-done.3, s32[1,128]{1,0:T(1,128)S(1)} %bitcast.7, f32[32,128]{1,0:T(8,128)S(1)} %copy-done.2, ...), custom_call_target="tpu_custom_call", output_to_operand_aliasing={{0}: (8, {}), {1}: (9, {})} | custom-call | flops 15000000512 | tf_op jit(solution)/shard_map/second/pallas_call | solution.py:43
  (27 shorter events, 2.6 us)
Async XLA Ops:
  0.7 14.1 %copy-start.1 = (bf16[128,32,128]{2,1,0:T(8,128)(2,1)S(1)}, bf16[128,32,128]{2,1,0:T(8,128)(2,1)}, u32[]{:S(2)}) copy-start(bf16[128,32,128]{2,1,0:T(8,128)(2,1)} %refs_2_.3) | copy-start | bytes 3145732
  0.7 14.1 %copy-start.3 = (f32[32]{0:T(128)S(1)}, f32[32]{0:T(128)}, u32[]{:S(2)}) copy-start(f32[32]{0:T(128)} %refs_1_.9) | copy-start | bytes 388
  0.7 14.1 %copy-start.4 = (s32[128]{0:T(128)S(1)}, s32[128]{0:T(128)}, u32[]{:S(2)}) copy-start(s32[128]{0:T(128)} %param.17) | copy-start | bytes 1540
  4.1 4.0 %collective-permute-start = (bf16[161,16,128]{2,1,0:T(8,128)(2,1)S(1)}, bf16[161,16,128]{2,1,0:T(8,128)(2,1)S(1)}, u32[]{:S(2)}, u32[]{:S(2)}) collective-permute-start(bf16[161,16,128]{2,1,0:T(8,128)(2,1)S(1)} %get-tuple-element.32), channel_id=1, source_target_pairs={{0,4},{1,5},{2,6},{3,7},{4,0},{5,1},{6,2},{7,3},{8,12},{9,13},{10,... | collective-permute-start | bytes 1978376 | tf_op jit(solution)/shard_map/ppermute | solution.py:454
  4.6 11.7 %collective-permute-start.2 = (bf16[1056,128]{1,0:T(8,128)(2,1)S(1)}, bf16[1056,128]{1,0:T(8,128)(2,1)S(1)}, u32[]{:S(2)}, u32[]{:S(2)}) collective-permute-start(bf16[1056,128]{1,0:T(8,128)(2,1)S(1)} %get-tuple-element.34), channel_id=1, source_target_pairs={{0,3},{1,2},{2,1},{3,0},{4,7},{5,6},{6,5},{7,4},{8,11},{9,10},{10,... | collective-permute-start | bytes 811016 | tf_op jit(solution)/shard_map/ppermute | solution.py:454
  8.7 9.5 %collective-permute-start.1 = (bf16[1040,128]{1,0:T(8,128)(2,1)S(1)}, bf16[1040,128]{1,0:T(8,128)(2,1)S(1)}, u32[]{:S(2)}, u32[]{:S(2)}) collective-permute-start(bf16[1040,128]{1,0:T(8,128)(2,1)S(1)} %pair.1.refs_1_), channel_id=1, source_target_pairs={{0,8},{1,9},{2,10},{3,11},{4,12},{5,13},{6,14},{7,15},{8,16},{9,17... | collective-permute-start | bytes 798728 | tf_op jit(solution)/shard_map/ppermute | solution.py:464
  12.2 10.2 %collective-permute-start.3 = (bf16[1056,128]{1,0:T(8,128)(2,1)S(1)}, bf16[1056,128]{1,0:T(8,128)(2,1)S(1)}, u32[]{:S(2)}, u32[]{:S(2)}) collective-permute-start(bf16[1056,128]{1,0:T(8,128)(2,1)S(1)} %get-tuple-element.37), channel_id=1, source_target_pairs={{0,1},{1,0},{2,3},{3,2},{4,5},{5,4},{6,7},{7,6},{8,9},{9,8},{10,11... | collective-permute-start | bytes 811016 | tf_op jit(solution)/shard_map/ppermute | solution.py:454
  13.3 9.1 %collective-permute-start.4 = (bf16[1056,128]{1,0:T(8,128)(2,1)S(1)}, bf16[1056,128]{1,0:T(8,128)(2,1)S(1)}, u32[]{:S(2)}, u32[]{:S(2)}) collective-permute-start(bf16[1056,128]{1,0:T(8,128)(2,1)S(1)} %get-tuple-element.38), channel_id=1, source_target_pairs={{0,2},{1,3},{2,0},{3,1},{4,6},{5,7},{6,4},{7,5},{8,10},{9,11},{10,... | collective-permute-start | bytes 811016 | tf_op jit(solution)/shard_map/ppermute | solution.py:454
  16.3 13.6 %copy-start = (bf16[128,32,128]{2,1,0:T(8,128)(2,1)S(1)}, bf16[128,32,128]{2,1,0:T(8,128)(2,1)}, u32[]{:S(2)}) copy-start(bf16[128,32,128]{2,1,0:T(8,128)(2,1)} %refs_2_.5) | copy-start | bytes 3145732
  18.8 21.4 %collective-permute-start.5 = (bf16[1552,128]{1,0:T(8,128)(2,1)S(1)}, bf16[1552,128]{1,0:T(8,128)(2,1)S(1)}, u32[]{:S(2)}, u32[]{:S(2)}) collective-permute-start(bf16[1552,128]{1,0:T(8,128)(2,1)S(1)} %get-tuple-element.43), channel_id=1, source_target_pairs={{0,1},{1,0},{2,3},{3,2},{4,5},{5,4},{6,7},{7,6},{8,9},{9,8},{10,11... | collective-permute-start | bytes 1191944 | tf_op jit(solution)/shard_map/ppermute | solution.py:454
  20.0 21.2 %collective-permute-start.6 = (bf16[1552,128]{1,0:T(8,128)(2,1)S(1)}, bf16[1552,128]{1,0:T(8,128)(2,1)S(1)}, u32[]{:S(2)}, u32[]{:S(2)}) collective-permute-start(bf16[1552,128]{1,0:T(8,128)(2,1)S(1)} %get-tuple-element.44), channel_id=1, source_target_pairs={{0,2},{1,3},{2,0},{3,1},{4,6},{5,7},{6,4},{7,5},{8,10},{9,11},{10,... | collective-permute-start | bytes 1191944 | tf_op jit(solution)/shard_map/ppermute | solution.py:454
  21.5 19.7 %collective-permute-start.7 = (bf16[1552,128]{1,0:T(8,128)(2,1)S(1)}, bf16[1552,128]{1,0:T(8,128)(2,1)S(1)}, u32[]{:S(2)}, u32[]{:S(2)}) collective-permute-start(bf16[1552,128]{1,0:T(8,128)(2,1)S(1)} %get-tuple-element.45), channel_id=1, source_target_pairs={{0,3},{1,2},{2,1},{3,0},{4,7},{5,6},{6,5},{7,4},{8,11},{9,10},{10,... | collective-permute-start | bytes 1191944 | tf_op jit(solution)/shard_map/ppermute | solution.py:454
  23.4 10.3 %collective-permute-start.8 = (bf16[1040,128]{1,0:T(8,128)(2,1)S(1)}, bf16[1040,128]{1,0:T(8,128)(2,1)S(1)}, u32[]{:S(2)}, u32[]{:S(2)}) collective-permute-start(bf16[1040,128]{1,0:T(8,128)(2,1)S(1)} %get-tuple-element.39.refs_4_), channel_id=1, source_target_pairs={{0,4},{1,5},{2,6},{3,7},{4,8},{5,9},{6,10},{7,11},{8,12},{9,13},{1... | collective-permute-start | bytes 798728 | tf_op jit(solution)/shard_map/ppermute | solution.py:464
  24.7 11.8 %collective-permute-start.9 = (bf16[1040,128]{1,0:T(8,128)(2,1)S(1)}, bf16[1040,128]{1,0:T(8,128)(2,1)S(1)}, u32[]{:S(2)}, u32[]{:S(2)}) collective-permute-start(bf16[1040,128]{1,0:T(8,128)(2,1)S(1)} %get-tuple-element.46), channel_id=1, source_target_pairs={{0,8},{1,9},{2,10},{3,11},{4,12},{5,13},{6,14},{7,15},{8,16},{9,17... | collective-permute-start | bytes 798728 | tf_op jit(solution)/shard_map/ppermute | solution.py:464
  37.6 10.2 %collective-permute-start.10 = (bf16[1040,128]{1,0:T(8,128)(2,1)S(1)}, bf16[1040,128]{1,0:T(8,128)(2,1)S(1)}, u32[]{:S(2)}, u32[]{:S(2)}) collective-permute-start(bf16[1040,128]{1,0:T(8,128)(2,1)S(1)} %get-tuple-element.51), channel_id=1, source_target_pairs={{0,3},{1,2},{2,1},{3,0},{4,7},{5,6},{6,5},{7,4},{8,11},{9,10},{10,... | collective-permute-start | bytes 798728 | tf_op jit(solution)/shard_map/ppermute | solution.py:454
  39.7 13.0 %collective-permute-start.13 = (bf16[1040,128]{1,0:T(8,128)(2,1)S(1)}, bf16[1040,128]{1,0:T(8,128)(2,1)S(1)}, u32[]{:S(2)}, u32[]{:S(2)}) collective-permute-start(bf16[1040,128]{1,0:T(8,128)(2,1)S(1)} %get-tuple-element.56), channel_id=1, source_target_pairs={{0,1},{1,0},{2,3},{3,2},{4,5},{5,4},{6,7},{7,6},{8,9},{9,8},{10,11... | collective-permute-start | bytes 798728 | tf_op jit(solution)/shard_map/ppermute | solution.py:454
  40.2 12.8 %collective-permute-start.14 = (bf16[1040,128]{1,0:T(8,128)(2,1)S(1)}, bf16[1040,128]{1,0:T(8,128)(2,1)S(1)}, u32[]{:S(2)}, u32[]{:S(2)}) collective-permute-start(bf16[1040,128]{1,0:T(8,128)(2,1)S(1)} %get-tuple-element.57), channel_id=1, source_target_pairs={{0,2},{1,3},{2,0},{3,1},{4,6},{5,7},{6,4},{7,5},{8,10},{9,11},{10,... | collective-permute-start | bytes 798728 | tf_op jit(solution)/shard_map/ppermute | solution.py:454
  41.2 6.6 %copy-start.2 = (f32[32,128]{1,0:T(8,128)S(1)}, f32[32,128]{1,0:T(8,128)}, u32[]{:S(2)}) copy-start(f32[32,128]{1,0:T(8,128)} %refs_3_.5) | copy-start | bytes 49156
  50.2 2.8 %collective-permute-start.11 = (bf16[64,16,128]{2,1,0:T(8,128)(2,1)S(1)}, bf16[64,16,128]{2,1,0:T(8,128)(2,1)S(1)}, u32[]{:S(2)}, u32[]{:S(2)}) collective-permute-start(bf16[64,16,128]{2,1,0:T(8,128)(2,1)S(1)} %get-tuple-element.52), channel_id=1, source_target_pairs={{0,4},{1,5},{2,6},{3,7},{4,0},{5,1},{6,2},{7,3},{8,12},{9,13},{10,... | collective-permute-start | bytes 786440 | tf_op jit(solution)/shard_map/ppermute | solution.py:454
  50.3 2.7 %collective-permute-start.12 = (bf16[64,16,128]{2,1,0:T(8,128)(2,1)S(1)}, bf16[64,16,128]{2,1,0:T(8,128)(2,1)S(1)}, u32[]{:S(2)}, u32[]{:S(2)}) collective-permute-start(bf16[64,16,128]{2,1,0:T(8,128)(2,1)S(1)} %get-tuple-element.53), channel_id=1, source_target_pairs={{0,4},{1,5},{2,6},{3,7},{4,0},{5,1},{6,2},{7,3},{8,12},{9,13},{10,... | collective-permute-start | bytes 786440 | tf_op jit(solution)/shard_map/ppermute | solution.py:454
